TPU v7x, 32 devices: a whole 2x2x4 slice. The times are simulated.
32 devices in a mesh: dp: 8 (over z, x), blk: 4 (over y, core).
Axes of the slice: x: 2, y: 2, z: 4, core: 2. Of those that a mesh axis runs over, the one named last changes fastest.
Arguments:
- entity_table: float32 [65536, 400], P(('dp', 'blk')), may hold values from -1.8 to 1.8
- adagrad_sum: float32 [65536], P(('dp', 'blk')), may hold values from 0.0001 to 0.001
- relations: float32 [7424, 400], replicated, may hold values from -1.8 to 1.8
- owner_map: int32 [65536], replicated, may hold values from 0 to 65535, as said below
- head_ids: int32 [4096], P(('dp', 'blk')), may hold values from 0 to 65535, as said below
- rel_ids: int32 [4096], P(('dp', 'blk')), may hold values from 0 to 7423
- tail_ids: int32 [4096], P(('dp', 'blk')), may hold values from 0 to 65535, as said below
- neg_ids: int32 [16384], P(('dp', 'blk')), may hold values from 0 to 65535, as said below
Outputs:
- new_table: float32 [65536, 400], P(('dp', 'blk'))
- new_sum: float32 [65536], P(('dp', 'blk'))
Inputs may be any that keep to these rules, and one draw needn't show every extreme that they name: `owner_map`: A permutation: every storage position appears once. The owner of position p is device p // 2048. `head_ids`: among the 128 heads, 128 tails and 512 negatives of one device taken together, at most 48 are stored on any one owner; in every draw 4 owners receive exactly 48 from every device. `tail_ids`: counted together with the heads and negatives of the same device, as stated for head_ids. `neg_ids`: counted together with the heads and tails of the same device, as stated for head_ids.
All inputs are finite; a program needn't handle non-finite values.
Results may differ from a plain program's by a relative error of at most 0.00005.
Values sent between devices are 32-bit elements; how exact they have to be, the bound alone decides.
No kernel may reach another device: no remote copies, remote signals or barrier semaphores. Data moves between devices by JAX's collectives and lax.ppermute only.
A program may use at most 128 MiB of HBM per device.

v0:
```python
import jax
import jax.numpy as jnp
from jax import lax
from jax.sharding import PartitionSpec as P

MARGIN = 10.0
EPSILON = 1e-05
LEARNING_RATE = 0.1


def negative_terms(queries, neg_block, weight):
    query_sq = jnp.sum(queries * queries, axis=1)
    block_sq = jnp.sum(neg_block * neg_block, axis=1)
    inner_prod = jnp.dot(
        queries, neg_block.T, precision=lax.Precision.HIGHEST, preferred_element_type=jnp.float32
    )
    distance = jnp.sqrt(query_sq[:, None] + block_sq[None, :] - 2.0 * inner_prod + EPSILON)
    coefficient = -jax.nn.sigmoid(MARGIN - distance) / (weight * distance)
    grad_query = queries * jnp.sum(coefficient, axis=1)[:, None] - jnp.dot(
        coefficient, neg_block, precision=lax.Precision.HIGHEST, preferred_element_type=jnp.float32
    )
    grad_block = neg_block * jnp.sum(coefficient, axis=0)[:, None] - jnp.dot(
        coefficient.T, queries, precision=lax.Precision.HIGHEST, preferred_element_type=jnp.float32
    )
    return (grad_query, grad_block)


def send_requests(requests):
    return lax.all_to_all(requests, ("dp", "blk"), split_axis=0, concat_axis=0, tiled=True)


def move_rows(payload):
    return lax.all_to_all(payload, ("dp", "blk"), split_axis=0, concat_axis=0, tiled=True)


def on_device(
    entity_table, adagrad_sum, relations, owner_map, head_ids, rel_ids, tail_ids, neg_ids
):
    dp_count = lax.axis_size("dp")
    blk_count = lax.axis_size("blk")
    owner_count = dp_count * blk_count
    rows_here, width = entity_table.shape
    edge_count = head_ids.shape[0]
    neg_count = neg_ids.shape[0]
    request_count = 2 * edge_count + neg_count
    capacity = max(2, 2 * request_count // owner_count)
    wanted = jnp.concatenate([head_ids, tail_ids, neg_ids])
    position = owner_map[wanted]
    owner_of = position // rows_here
    local_row = position % rows_here
    onehot = (owner_of[:, None] == jnp.arange(owner_count, dtype=jnp.int32)[None, :]).astype(
        jnp.int32
    )
    before = jnp.cumsum(onehot, axis=0) - onehot
    rank_in = jnp.sum(before * onehot, axis=1)
    slot_of = owner_of * capacity + rank_in
    requests = jnp.zeros((owner_count * capacity,), jnp.int32).at[slot_of].set(local_row)
    requests = requests.reshape(owner_count, capacity)
    asked_rows = send_requests(requests)
    served = entity_table[asked_rows]
    fetched = move_rows(served).reshape(owner_count * capacity, width)[slot_of]
    head_rows = fetched[:edge_count]
    tail_rows = fetched[edge_count : 2 * edge_count]
    neg_block = fetched[2 * edge_count :]
    queries = head_rows + relations[rel_ids]
    residue = queries - tail_rows
    pos_dist = jnp.sqrt(jnp.sum(residue * residue, axis=1) + EPSILON)
    grad_pos = (jax.nn.sigmoid(pos_dist - MARGIN) / pos_dist)[:, None] * residue
    weight = float(blk_count * neg_count)
    part_query, part_block = negative_terms(
        queries, lax.all_gather(neg_block, "blk", axis=0, tiled=True), weight
    )
    block_grad = lax.psum_scatter(part_block, "blk", scatter_dimension=0, tiled=True)
    gradients = jnp.concatenate([grad_pos + part_query, -grad_pos, block_grad])
    outgoing = jnp.zeros((owner_count * capacity, width), jnp.float32).at[slot_of].set(gradients)
    incoming = move_rows(outgoing.reshape(owner_count, capacity, width))
    summed = (
        jnp.zeros_like(entity_table).at[asked_rows.reshape(-1)].add(incoming.reshape(-1, width))
    )
    new_sum = adagrad_sum + jnp.mean(summed * summed, axis=1)
    new_table = entity_table - LEARNING_RATE * summed / jnp.sqrt(new_sum)[:, None]
    return (new_table, new_sum)


def solution(mesh):
    return jax.shard_map(
        on_device,
        mesh=mesh,
        in_specs=(
            P(("dp", "blk"), None),
            P(("dp", "blk")),
            P(),
            P(),
            P(("dp", "blk")),
            P(("dp", "blk")),
            P(("dp", "blk")),
            P(("dp", "blk")),
        ),
        out_specs=(P(("dp", "blk"), None), P(("dp", "blk"))),
        check_vma=False,
    )
```

profile of v0, /device:TPU:0, one launch (start us, length us, event | category | flops | bytes accessed | tf_op | source)
XLA Modules:
  0.0 319.5 jit_solution(5360426192991126961)
XLA Ops:
  8.1 4.5 %gather_fusion = s32[768]{0:T(1024)S(1)} fusion(s32[65536]{0:T(1024)S(1)} %copy-done, s32[1024]{0:T(1024)S(1)} %pad_clamp_fusion.3), kind=kCustom, calls=%fused_computation | custom fusion | bytes 9216 | tf_op jit(solution)/shard_map/gather | solution.py:48
  14.8 3.4 %scatter_custom_fusion = s32[1536]{0:T(1024)S(1)} fusion(s32[768]{0:T(1024)S(1)} %fusion.20, s32[768]{0:T(1024)S(1)} %get-tuple-element.13, s32[]{:T(128)} %constant.22.clone.1), kind=kCustom, calls=%fused_computation.63 | custom fusion | bytes 6148 | tf_op jit(solution)/shard_map/scatter | solution.py:57
  18.9 7.3 %all-to-all-start = ((s32[32,1,48]{2,1,0:T(1,128)}), s32[32,1,48]{2,1,0:T(1,128)S(1)}, u32[]{:S(2)}, u32[]{:S(2)}) async-start(s32[32,1,48]{2,1,0:T(1,128)} %all_to_all.14), calls=%async_computation | async-start | bytes 32768 | tf_op jit(solution)/shard_map/all_to_all | solution.py:29
  26.2 3.3 %copy.26 = f32[2048,400]{1,0:T(8,128)} copy(f32[2048,400]{0,1:T(8,128)S(1)} %copy-done.5) | data formatting | bytes 6553600 | tf_op args[0]
  29.6 3.7 %all-to-all-done = s32[32,1,48]{2,1,0:T(1,128)S(1)} async-done(((s32[32,1,48]{2,1,0:T(1,128)}), s32[32,1,48]{2,1,0:T(1,128)S(1)}, u32[]{:S(2)}, u32[]{:S(2)}) %all-to-all-start) | async-done | bytes 6176 | tf_op jit(solution)/shard_map/all_to_all | solution.py:29
  33.4 7.9 %gather_fusion.1 = f32[1536,400]{1,0:T(8,128)} fusion(f32[2048,400]{1,0:T(8,128)} %copy.26, s32[2048]{0:T(1024)S(1)} %pad_clamp_fusion), kind=kCustom, calls=%fused_computation.1 | custom fusion | bytes 4921344 | tf_op jit(solution)/shard_map/gather | solution.py:60
  41.3 2.8 all-to-all-start.1
  44.1 71.7 %all-to-all-done.1 = f32[32,48,400]{2,1,0:T(8,128)S(1)} async-done(((f32[32,48,400]{2,1,0:T(8,128)}), f32[32,48,400]{2,1,0:T(8,128)S(1)}, u32[]{:S(2)}, u32[]{:S(2)}) %all-to-all-start.1) | async-done | bytes 2457632 | tf_op jit(solution)/shard_map/all_to_all | solution.py:33
  115.9 3.1 gather_fusion.2
  121.7 14.3 %copy.21 = f32[7424,400]{1,0:T(8,128)} copy(f32[7424,400]{0,1:T(8,128)} %param.10) | data formatting | bytes 23756800 | tf_op args[2]
  136.0 6.3 %gather_fusion.3 = f32[128,400]{1,0:T(8,128)S(1)} fusion(f32[7424,400]{1,0:T(8,128)} %copy.21, s32[1024]{0:T(1024)S(1)} %pad_clamp_fusion.1), kind=kCustom, calls=%fused_computation.3 | custom fusion | bytes 410112 | tf_op jit(solution)/shard_map/gather | solution.py:65
  144.6 6.1 %all-gather.2.cloned.1.call-done = f32[2048,400]{0,1:T(8,128)} async-done(((f32[512,400]{0,1:T(8,128)}), f32[2048,400]{0,1:T(8,128)}) %all-gather.2.cloned.1.call-update) | async-done | bytes 3276816 | tf_op jit(solution)/shard_map/all_gather | solution.py:71
  150.7 2.4 multiply_reduce_fusion.1
  153.6 2.8 fusion.22
  157.5 4.5 %multiply_subtract_fusion = f32[2048,400]{0,1:T(8,128)} fusion(f32[2048,400]{0,1:T(8,128)S(1)} %copy-done.3, f32[128,2048]{1,0:T(8,128)S(1)} %get-tuple-element.15, f32[128,400]{0,1:T(8,128)S(1)} %get-tuple-element.10, f32[2048]{0:T(1024)S(1)} %get-tuple-element.5), kind=kOutput, calls=%fused_computation.9 | convolution fusion | flops 1259929600 | bytes 7815168 | tf_op jit(solution)/shard_map/dot_general | solution.py:22
  163.7 4.6 %fusion.7 = f32[128,400]{0,1:T(8,128)} fusion(f32[128,2048]{1,0:T(8,128)} %copy-done.4, f32[2048,400]{0,1:T(8,128)S(1)} %copy-done.3, f32[128,400]{0,1:T(8,128)S(1)} %get-tuple-element.10, f32[128,400]{0,1:T(8,128)} %get-tuple-element.9, f32[128]{0:T(128)S(1)} %get-tuple-element.4, f32[128]{0:T(128)S(1)} %multiply_divide_fusion.1), kind=kOutput, calls=%fused_computation.21 | convolution fusion | flops 1258496000 | bytes 4940800 | tf_op jit(solution)/shard_map/dot_general | solution.py:19
  168.3 32.6 %reduce-scatter.2.cloned.1.call-done = f32[512,400]{0,1:T(8,128)} async-done(((f32[2048,400]{0,1:T(8,128)}), f32[512,400]{0,1:T(8,128)}) %reduce-scatter.2.cloned.1.call-update) | async-done | bytes 819216 | tf_op jit(solution)/shard_map/reduce_scatter | solution.py:73
  202.7 7.7 %scatter_custom_fusion.1 = f32[1536,400]{1,0:T(8,128)} fusion(s32[768]{0:T(1024)} %copy-done.6, f32[768,400]{1,0:T(8,128)S(1)} %copy.25, f32[]{:T(128)} %constant.21.clone.1), kind=kCustom, calls=%fused_computation.17 | custom fusion | bytes 2458112 | tf_op jit(solution)/shard_map/scatter | solution.py:75
  210.4 4.6 %all-to-all-start.2 = ((f32[32,48,400]{2,1,0:T(8,128)}), f32[32,48,400]{2,1,0:T(8,128)S(1)}, u32[]{:S(2)}, u32[]{:S(2)}) async-start(f32[32,48,400]{2,1,0:T(8,128)} %bitcast.8), calls=%async_computation.3 | async-start | bytes 6291456 | tf_op jit(solution)/shard_map/all_to_all | solution.py:33
  216.4 70.4 %all-to-all-done.2 = f32[32,48,400]{2,1,0:T(8,128)S(1)} async-done(((f32[32,48,400]{2,1,0:T(8,128)}), f32[32,48,400]{2,1,0:T(8,128)S(1)}, u32[]{:S(2)}, u32[]{:S(2)}) %all-to-all-start.2) | async-done | bytes 2457632 | tf_op jit(solution)/shard_map/all_to_all | solution.py:33
  286.8 12.4 %scatter_custom_fusion.2 = f32[2048,400]{1,0:T(8,128)} fusion(s32[1536]{0:T(1024)S(1)} %fusion.12, f32[1536,400]{1,0:T(8,128)S(1)} %bitcast.54, f32[]{:T(128)} %constant.21.clone.1), kind=kCustom, calls=%fused_computation.15 | custom fusion | flops 614400 | bytes 3276804 | tf_op jit(solution)/shard_map/scatter-add | solution.py:78
  299.1 2.7 multiply_reduce_fusion
  302.6 4.9 %divide_subtract_fusion = f32[2048,400]{1,0:T(8,128)} fusion(f32[2048,400]{1,0:T(8,128)S(1)} %copy-done.2, f32[2048,400]{1,0:T(8,128)} %scatter_custom_fusion.2, f32[2048]{0:T(1024)S(1)} %get-tuple-element.6), kind=kLoop, calls=%fused_computation.7 | loop fusion | flops 2457600 | bytes 9838592 | tf_op jit(solution)/shard_map/sub | solution.py:81
  307.5 5.2 %copy.27 = f32[2048,400]{0,1:T(8,128)} copy(f32[2048,400]{1,0:T(8,128)} %divide_subtract_fusion) | data formatting | bytes 6553600
  (56 shorter events, 16.1 us)
Async XLA Ops:
  7.2 1.0 copy-start
  7.2 19.1 %copy-start.5 = (f32[2048,400]{0,1:T(8,128)S(1)}, f32[2048,400]{0,1:T(8,128)}, u32[]{:S(2)}) copy-start(f32[2048,400]{0,1:T(8,128)} %param.8) | copy-start | bytes 9830404
  14.8 29.3 %copy-start.6 = (s32[768]{0:T(1024)}, s32[768]{0:T(1024)S(1)}, u32[]{:S(2)}) copy-start(s32[768]{0:T(1024)S(1)} %fusion.20) | copy-start | bytes 9220
  18.9 14.4 %all-to-all-start = ((s32[32,1,48]{2,1,0:T(1,128)}), s32[32,1,48]{2,1,0:T(1,128)S(1)}, u32[]{:S(2)}, u32[]{:S(2)}) async-start(s32[32,1,48]{2,1,0:T(1,128)} %all_to_all.14), calls=%async_computation | async-start | bytes 32768 | tf_op jit(solution)/shard_map/all_to_all | solution.py:29
  41.3 74.6 %all-to-all-start.1 = ((f32[32,48,400]{2,1,0:T(8,128)}), f32[32,48,400]{2,1,0:T(8,128)S(1)}, u32[]{:S(2)}, u32[]{:S(2)}) async-start(f32[32,48,400]{2,1,0:T(8,128)} %bitcast.53), calls=%async_computation.1 | async-start | bytes 6291456 | tf_op jit(solution)/shard_map/all_to_all | solution.py:33
  44.1 106.6 %all-gather.2.cloned.1.call-start = ((), (), s32[]{:S(2)}) async-start(), calls=%async_computation.4 | async-start | bytes 4096000 | tf_op jit(solution)/shard_map/all_gather | solution.py:71
  121.5 14.5 %copy-start.8 = (s32[128]{0:T(128)S(1)}, s32[128]{0:T(128)}, u32[]{:S(2)}) copy-start(s32[128]{0:T(128)} %param.13) | copy-start | bytes 1540
  121.5 79.4 %reduce-scatter.2.cloned.1.call-start = ((), (), s32[]{:S(2)}) async-start(), calls=%async_computation.5 | async-start | bytes 4096000 | tf_op jit(solution)/shard_map/reduce_scatter | solution.py:73
  150.7 2.9 copy-start.3
  156.5 1.0 copy-start.4
  210.4 76.4 %all-to-all-start.2 = ((f32[32,48,400]{2,1,0:T(8,128)}), f32[32,48,400]{2,1,0:T(8,128)S(1)}, u32[]{:S(2)}, u32[]{:S(2)}) async-start(f32[32,48,400]{2,1,0:T(8,128)} %bitcast.8), calls=%async_computation.3 | async-start | bytes 6291456 | tf_op jit(solution)/shard_map/all_to_all | solution.py:33
  286.8 15.1 %copy-start.7 = (f32[2048]{0:T(1024)S(1)}, f32[2048]{0:T(1024)}, u32[]{:S(2)}) copy-start(f32[2048]{0:T(1024)} %param.9) | copy-start | bytes 24580
  299.1 3.4 %copy-start.2 = (f32[2048,400]{1,0:T(8,128)S(1)}, f32[2048,400]{1,0:T(8,128)}, u32[]{:S(2)}) copy-start(f32[2048,400]{1,0:T(8,128)} %copy.26) | copy-start | bytes 9830404
  302.6 10.0 %copy-start.1 = (s32[65536]{0:T(1024)S(1)}, s32[65536]{0:T(1024)}, u32[]{:S(2)}) copy-start(s32[65536]{0:T(1024)} %param.11) | copy-start | bytes 786436
Sparse Core Ops, SparseCore 0:
  121.6 29.0 all-gather.1
  162.1 38.7 reduce-scatter.1
where the time goes:
time: 320 us; the launch traced here: 319 us
  waiting for transfers between devices  185 us (58%)
  local copies, waits for them, and re-layouts  63.3 us (20%)
  other arithmetic  30.3 us (9%)
  starting transfers between devices  15 us (5%)
  between operations  14.3 us (4%)
  matrix products  12 us (4%)
    all_to_all x2, waiting for transfers between devices, move_rows(): lax.all_to_all(payload, ('dp', 'blk'), split_axis=0, concat_axis=0, tiled...  142 us
    reduce_scatter x1, waiting for transfers between devices, on_device(): lax.psum_scatter(part_block, 'blk', scatter_dimension=0, tiled=True)  32.6 us
    unnamed x24, local copies, waits for them, and re-layouts  26 us
    scatter-add x1, other arithmetic, on_device(): jnp.zeros_like(entity_table).at[asked_rows.reshape(-1)]  12.4 us
    gather x1, local copies, waits for them, and re-layouts, on_device(): served = entity_table[asked_rows]  7.87 us
    scatter x1, local copies, waits for them, and re-layouts, on_device(): jnp.zeros((owner_count * capacity, width), jnp.float32).at[slot_of]  7.68 us
    all_to_all x2, starting transfers between devices, move_rows(): lax.all_to_all(payload, ('dp', 'blk'), split_axis=0, concat_axis=0, tiled...  7.39 us
    all_to_all x1, starting transfers between devices, send_requests(): lax.all_to_all(requests, ('dp', 'blk'), split_axis=0, concat_axis=0, tile...  7.3 us
  transfers between devices with their start and end apart: 5, of which 5 were waited for; matrix products, arithmetic and copies ran while one was open for 11% of the time, Pallas kernels for 0%

commit v1 on v0

v1 whole, which is shorter than its diff:
```python
import functools

import jax
import jax.numpy as jnp
from jax import lax
from jax.experimental import pallas as pl
from jax.experimental.pallas import tpu as pltpu
from jax.sharding import PartitionSpec as P

MARGIN = 10.0
EPSILON = 1e-05
LEARNING_RATE = 0.1
LANES = 128
SUBLANES = 8
VMEM_BYTES = 40 * 1024 * 1024
HIGHEST = lax.Precision.HIGHEST


class Packing:
    def __init__(self, width, owners, capacity):
        self.width = width
        self.owners = owners
        self.capacity = capacity
        self.full = width // LANES
        self.rest = width - self.full * LANES
        assert 0 < self.rest <= LANES // SUBLANES and capacity % SUBLANES == 0
        self.shared = capacity // SUBLANES
        self.groups = self.full + 1
        self.wide = self.groups * LANES
        self.rests_at = self.full * capacity
        self.stride = -(-(self.rests_at + self.shared) // SUBLANES) * SUBLANES
        self.slots = owners * capacity
        self.rows = owners * self.stride


def compiler_params():
    return pltpu.CompilerParams(vmem_limit_bytes=VMEM_BYTES)


def vmem():
    return pl.BlockSpec(memory_space=pltpu.VMEM)


def smem():
    return pl.BlockSpec(memory_space=pltpu.SMEM)


def split(value):
    high = value.astype(jnp.bfloat16)
    low = (value - high.astype(jnp.float32)).astype(jnp.bfloat16)
    return high, low


def dot_halves(left, right, contract):
    numbers = (contract, ((), ()))

    def dot(a, b):
        return lax.dot_general(a, b, numbers, preferred_element_type=jnp.float32)

    return dot(left[0], right[0]) + (dot(left[0], right[1]) + dot(left[1], right[0]))


def loop(count, body):
    def step(index, carry):
        body(index)
        return carry

    lax.fori_loop(0, count, step, 0)


def expand_rests(pack, packed_ref, rests_ref):
    lane = lax.broadcasted_iota(jnp.int32, (pack.shared, LANES), 1)

    def body(owner):
        block = packed_ref[pl.ds(owner * pack.stride + pack.rests_at, pack.shared), :]
        for j in range(SUBLANES):
            moved = block if j == 0 else pltpu.roll(block, LANES - j * pack.rest, axis=1)
            rests_ref[pl.ds(owner * pack.capacity + j, pack.shared, stride=SUBLANES), :] = (
                jnp.where(lane < pack.rest, moved, 0.0)
            )

    loop(pack.owners, body)


def rows_kernel(pack, columns_ref, rows_ref):
    fill = jnp.zeros((pack.wide - pack.width, LANES), jnp.float32)
    for block in range(columns_ref.shape[1] // LANES):
        at = slice(block * LANES, (block + 1) * LANES)
        tile = jnp.concatenate([columns_ref[:, at], fill], axis=0)
        for c in range(pack.groups):
            rows_ref[at, c, :] = tile[c * LANES : (c + 1) * LANES].T


def to_rows(pack, columns):
    count = columns.shape[1]
    return pl.pallas_call(
        functools.partial(rows_kernel, pack),
        out_shape=jax.ShapeDtypeStruct((count, pack.groups, LANES), jnp.float32),
        in_specs=[vmem()],
        out_specs=vmem(),
        compiler_params=compiler_params(),
        name="table_rows",
    )(columns)


def serve_kernel(pack, asked_ref, table_ref, out_ref):
    lane = lax.broadcasted_iota(jnp.int32, (pack.groups, LANES), 1) // pack.rest

    def body(group):
        owner = group // pack.shared
        inner = group % pack.shared
        base = owner * pack.stride
        shared = None
        for j in range(SUBLANES):
            value = table_ref[jnp.maximum(asked_ref[group * SUBLANES + j], 0)]
            out_ref[pl.ds(base + (inner * SUBLANES + j) * pack.full, pack.full), :] = value[
                : pack.full
            ]
            if j == 0:
                shared = value
            else:
                shared = jnp.where(lane == j, pltpu.roll(value, j * pack.rest, axis=1), shared)
        out_ref[pl.ds(base + pack.rests_at + inner, 1), :] = shared[pack.full :]

    loop(pack.slots // SUBLANES, body)


def serve(pack, asked, table_rows):
    return pl.pallas_call(
        functools.partial(serve_kernel, pack),
        out_shape=jax.ShapeDtypeStruct((pack.rows, LANES), jnp.float32),
        in_specs=[smem(), vmem()],
        out_specs=vmem(),
        compiler_params=compiler_params(),
        name="serve_rows",
    )(asked, table_rows)


def unpack_kernel(
    pack, edges, address_ref, slot_ref, packed_ref, relation_ref,
    query_ref, positive_ref, negative_ref, rests_ref, rows_ref,
):
    expand_rests(pack, packed_ref, rests_ref)
    count = rows_ref.shape[0]

    def body(group):
        for j in range(SUBLANES):
            row = group * SUBLANES + j
            rows_ref[row, : pack.full, :] = packed_ref[pl.ds(address_ref[row], pack.full), :]
            rows_ref[row, pack.full :, :] = rests_ref[pl.ds(slot_ref[row], 1), :]

    loop(count // SUBLANES, body)
    for c in range(pack.groups):
        negative_ref[:, c * LANES : (c + 1) * LANES] = rows_ref[2 * edges :, c, :]

    def columns(first):
        parts = [rows_ref[first : first + edges, c, :].T for c in range(pack.groups)]
        return jnp.concatenate(parts, axis=0)[: pack.width]

    queries = columns(0) + relation_ref[...]
    residue = queries - columns(edges)
    distance = jnp.sqrt(jnp.sum(residue * residue, axis=0, keepdims=True) + EPSILON)
    query_ref[...] = queries
    positive_ref[...] = jax.nn.sigmoid(distance - MARGIN) / distance * residue


def unpack(pack, edges, negatives, address, slot, packed, relation_rows):
    shape = jax.ShapeDtypeStruct
    return pl.pallas_call(
        functools.partial(unpack_kernel, pack, edges),
        out_shape=(
            shape((pack.width, edges), jnp.float32),
            shape((pack.width, edges), jnp.float32),
            shape((negatives, pack.wide), jnp.float32),
        ),
        in_specs=[smem(), smem(), vmem(), vmem()],
        out_specs=(vmem(), vmem(), vmem()),
        scratch_shapes=[
            pltpu.VMEM((pack.slots, LANES), jnp.float32),
            pltpu.VMEM((2 * edges + negatives, pack.groups, LANES), jnp.float32),
        ],
        compiler_params=compiler_params(),
        name="unpack_rows",
    )(address, slot, packed, relation_rows)


def negatives_kernel(pack, blocks, weight, *refs):
    negative_ref = refs[0]
    query_refs = refs[1 : 1 + blocks]
    block_ref, *part_refs = refs[1 + blocks :]
    negatives = negative_ref[...]
    queries = jnp.concatenate([ref[...] for ref in query_refs], axis=1)
    queries = jnp.concatenate(
        [queries, jnp.zeros((pack.wide - pack.width, queries.shape[1]), jnp.float32)], axis=0
    )
    query_sq = jnp.sum(queries * queries, axis=0, keepdims=True)
    block_sq = jnp.sum(negatives * negatives, axis=1, keepdims=True)
    inner = jnp.dot(negatives, queries, precision=HIGHEST, preferred_element_type=jnp.float32)
    distance = jnp.sqrt(query_sq + block_sq - 2.0 * inner + EPSILON)
    coefficient = -1.0 / ((1.0 + jnp.exp(distance - MARGIN)) * (weight * distance))
    query_halves = split(queries)
    coefficient_halves = split(coefficient)
    negative_halves = split(negatives.T)
    block_ref[...] = negatives * jnp.sum(coefficient, axis=1, keepdims=True) - dot_halves(
        coefficient_halves, query_halves, ((1,), (1,))
    )
    part = queries * jnp.sum(coefficient, axis=0, keepdims=True) - dot_halves(
        negative_halves, coefficient_halves, ((1,), (0,))
    )
    width = query_refs[0].shape[1]
    for index, ref in enumerate(part_refs):
        ref[...] = part[: pack.width, index * width : (index + 1) * width]


def negative_terms(pack, weight, negatives, queries):
    shape = jax.ShapeDtypeStruct
    return pl.pallas_call(
        functools.partial(negatives_kernel, pack, len(queries), weight),
        out_shape=(shape(negatives.shape, jnp.float32),)
        + tuple(shape(q.shape, jnp.float32) for q in queries),
        in_specs=[vmem()] * (1 + len(queries)),
        out_specs=(vmem(),) * (1 + len(queries)),
        compiler_params=compiler_params(),
        name="negative_terms",
    )(negatives, *queries)


def pack_kernel(
    pack, edges, address_ref, slot_ref, query_grad_ref, positive_ref, block_ref,
    out_ref, rests_ref, rows_ref,
):
    out_ref[...] = jnp.zeros_like(out_ref)
    rests_ref[...] = jnp.zeros_like(rests_ref)
    positive = positive_ref[...]
    fill = jnp.zeros((pack.wide - pack.width, edges), jnp.float32)
    heads = jnp.concatenate([query_grad_ref[...] + positive, fill], axis=0)
    tails = jnp.concatenate([-positive, fill], axis=0)
    for c in range(pack.groups):
        at = slice(c * LANES, (c + 1) * LANES)
        rows_ref[:edges, c, :] = heads[at].T
        rows_ref[edges : 2 * edges, c, :] = tails[at].T
        rows_ref[2 * edges :, c, :] = block_ref[:, at]

    def body(group):
        for j in range(SUBLANES):
            row = group * SUBLANES + j
            value = rows_ref[row]
            out_ref[pl.ds(address_ref[row], pack.full), :] = value[: pack.full]
            rests_ref[pl.ds(slot_ref[row], 1), :] = value[pack.full :]

    loop(rows_ref.shape[0] // SUBLANES, body)

    def share(owner):
        total = None
        for j in range(SUBLANES):
            block = rests_ref[pl.ds(owner * pack.capacity + j, pack.shared, stride=SUBLANES), :]
            moved = block if j == 0 else pltpu.roll(block, j * pack.rest, axis=1)
            total = moved if total is None else total + moved
        out_ref[pl.ds(owner * pack.stride + pack.rests_at, pack.shared), :] = total

    loop(pack.owners, share)


def pack_gradients(pack, address, slot, query_grad, positive, block_grad):
    edges = positive.shape[1]
    return pl.pallas_call(
        functools.partial(pack_kernel, pack, edges),
        out_shape=jax.ShapeDtypeStruct((pack.rows, LANES), jnp.float32),
        in_specs=[smem(), smem(), vmem(), vmem(), vmem()],
        out_specs=vmem(),
        scratch_shapes=[
            pltpu.VMEM((pack.slots, LANES), jnp.float32),
            pltpu.VMEM((2 * edges + block_grad.shape[0], pack.groups, LANES), jnp.float32),
        ],
        compiler_params=compiler_params(),
        name="pack_gradients",
    )(address, slot, query_grad, positive, block_grad)


def update_kernel(
    pack, columns, asked_ref, packed_ref, sum_ref, table_ref,
    new_table_ref, new_sum_ref, rests_ref, rows_ref, high_ref, low_ref,
):
    @pl.when(pl.program_id(0) == 0)
    def _():
        expand_rests(pack, packed_ref, rests_ref)

        def body(owner):
            rows = pl.ds(owner * pack.capacity, pack.capacity)
            for c in range(pack.full):
                rows_ref[rows, c * LANES : (c + 1) * LANES] = packed_ref[
                    pl.ds(owner * pack.stride + c, pack.capacity, stride=pack.full), :
                ]
            rows_ref[rows, pack.full * LANES :] = rests_ref[rows, :]

        loop(pack.owners, body)
        high, low = split(rows_ref[...].T)
        high_ref[...] = high[: pack.width]
        low_ref[...] = low[: pack.width]

    row = lax.broadcasted_iota(jnp.int32, (columns, pack.slots), 0) + pl.program_id(0) * columns
    chosen = (row == asked_ref[...]).astype(jnp.float32).astype(jnp.bfloat16)

    def pick(half_ref):
        return lax.dot_general(
            half_ref[...], chosen, (((1,), (1,)), ((), ())), preferred_element_type=jnp.float32
        )

    summed = pick(high_ref) + pick(low_ref)
    new_sum = sum_ref[...] + jnp.sum(summed * summed, axis=0, keepdims=True) / pack.width
    new_sum_ref[...] = new_sum
    new_table_ref[...] = table_ref[...] - summed * (LEARNING_RATE / jnp.sqrt(new_sum))


def update(pack, asked, packed, adagrad_sum, table_columns):
    width, rows = table_columns.shape
    columns = 256
    shape = jax.ShapeDtypeStruct
    return pl.pallas_call(
        functools.partial(update_kernel, pack, columns),
        grid=(rows // columns,),
        out_shape=(shape((width, rows), jnp.float32), shape((1, rows), jnp.float32)),
        in_specs=[
            pl.BlockSpec((1, pack.slots), lambda i: (0, 0)),
            pl.BlockSpec((pack.rows, LANES), lambda i: (0, 0)),
            pl.BlockSpec((1, columns), lambda i: (0, i)),
            pl.BlockSpec((width, columns), lambda i: (0, i)),
        ],
        out_specs=(
            pl.BlockSpec((width, columns), lambda i: (0, i)),
            pl.BlockSpec((1, columns), lambda i: (0, i)),
        ),
        scratch_shapes=[
            pltpu.VMEM((pack.slots, LANES), jnp.float32),
            pltpu.VMEM((pack.slots, pack.wide), jnp.float32),
            pltpu.VMEM((width, pack.slots), jnp.bfloat16),
            pltpu.VMEM((width, pack.slots), jnp.bfloat16),
        ],
        compiler_params=compiler_params(),
        name="update_table",
    )(asked, packed, adagrad_sum, table_columns)


def exchange(payload):
    return lax.all_to_all(payload, ("dp", "blk"), split_axis=0, concat_axis=0, tiled=True)


def to_sibling(value, blk_count):
    return lax.ppermute(value, "blk", [(i, i ^ 1) for i in range(blk_count)])


def to_chip(value, blk_count, hops):
    return lax.ppermute(
        value, "blk", [(i, (i + 2 * hops) % blk_count) for i in range(blk_count)]
    )


def on_device(
    entity_table, adagrad_sum, relations, owner_map, head_ids, rel_ids, tail_ids, neg_ids
):
    dp_count = lax.axis_size("dp")
    blk_count = lax.axis_size("blk")
    owner_count = dp_count * blk_count
    chip_count = blk_count // 2
    rows_here, width = entity_table.shape
    edge_count = head_ids.shape[0]
    neg_count = neg_ids.shape[0]
    request_count = 2 * edge_count + neg_count
    capacity = -(-2 * request_count // owner_count // SUBLANES) * SUBLANES
    pack = Packing(width, owner_count, capacity)
    wanted = jnp.concatenate([head_ids, tail_ids, neg_ids])
    position = owner_map[wanted]
    owner_of = position // rows_here
    local_row = position % rows_here
    onehot = (owner_of[:, None] == jnp.arange(owner_count, dtype=jnp.int32)[None, :]).astype(
        jnp.int32
    )
    before = jnp.cumsum(onehot, axis=0) - onehot
    rank_in = jnp.sum(before * onehot, axis=1)
    slot_of = owner_of * capacity + rank_in
    address = owner_of * pack.stride + rank_in * pack.full
    requests = jnp.full((pack.slots,), -1, jnp.int32).at[slot_of].set(local_row)
    asked = exchange(requests.reshape(owner_count, capacity)).reshape(-1)
    served = serve(pack, asked, to_rows(pack, entity_table.T))
    fetched = exchange(served.reshape(owner_count, pack.stride, LANES))
    queries, positive, negatives = unpack(
        pack, edge_count, neg_count, address, slot_of,
        fetched.reshape(pack.rows, LANES), relations[rel_ids].T,
    )
    group = []
    for hops in range(chip_count):
        same = queries if hops == 0 else to_chip(queries, blk_count, hops)
        group += [same, to_sibling(same, blk_count)]
    weight = float(blk_count * neg_count)
    block_grad, *parts = negative_terms(pack, weight, negatives, group)
    query_grad = None
    for hops in range(chip_count):
        total = parts[2 * hops] + to_sibling(parts[2 * hops + 1], blk_count)
        if hops:
            total = to_chip(total, blk_count, chip_count - hops)
        query_grad = total if query_grad is None else query_grad + total
    outgoing = pack_gradients(pack, address, slot_of, query_grad, positive, block_grad)
    incoming = exchange(outgoing.reshape(owner_count, pack.stride, LANES))
    new_columns, new_sum = update(
        pack, asked.reshape(1, -1), incoming.reshape(pack.rows, LANES),
        adagrad_sum.reshape(1, -1), entity_table.T,
    )
    return (new_columns.T, new_sum.reshape(-1))


def solution(mesh):
    return jax.shard_map(
        on_device,
        mesh=mesh,
        in_specs=(
            P(("dp", "blk"), None),
            P(("dp", "blk")),
            P(),
            P(),
            P(("dp", "blk")),
            P(("dp", "blk")),
            P(("dp", "blk")),
            P(("dp", "blk")),
        ),
        out_specs=(P(("dp", "blk"), None), P(("dp", "blk"))),
        check_vma=False,
    )
```

time: 320 us -> 227 us (0.71)
  waiting for transfers between devices: 185 us -> 105 us
  Pallas kernels: 0 us -> 48.6 us
  local copies, waits for them, and re-layouts: 63.3 us -> 42.7 us
  other arithmetic: 30.3 us -> 10.1 us
  between operations: 14.3 us -> 0.8 us
  matrix products: 12 us -> 0 us
  starting transfers between devices: 15 us -> 19 us
    all_to_all x3, waiting for transfers between devices: 146 us -> 90.9 us  [exchange(): lax.all_to_all(payload, ('dp', 'blk'), split_axis=0, concat_axis=0, tiled...]
    pallas_call x0 -> x6, Pallas kernels: none -> 48.6 us  [the longest x1 15.7 us: serve(): pl.pallas_call(functools.partial(serve_kernel, pack), out_shape=jax.Shape...]
    reduce_scatter x1 -> x0, waiting for transfers between devices: 32.6 us -> none  [on_device(): lax.psum_scatter(part_block, 'blk', scatter_dimension=0, tiled=True)]
    ppermute x0 -> x6, waiting for transfers between devices: none -> 13.6 us  [the longest x2 11.2 us: to_chip(): lax.ppermute(value, 'blk', [(i, (i + 2 * hops) % blk_count) for i in rang...]
    scatter-add x1 -> x0, other arithmetic: 12.4 us -> none  [on_device(): jnp.zeros_like(entity_table).at[asked_rows.reshape(-1)]]
    dot_general x3 -> x0, matrix products: 12 us -> none  [the longest x1 4.64 us: negative_terms(): jnp.dot(coefficient, neg_block, precision=lax.Precision.HIGHEST, preferre...]
    gather x4 -> x2, local copies, waits for them, and re-layouts: 17.3 us -> 8.63 us  [on_device(): relations[rel_ids]]
    scatter x2 -> x1, local copies, waits for them, and re-layouts: 11.1 us -> 3.52 us  [on_device(): requests = jnp.full((pack.slots,), -1, jnp.int32).at[slot_of].set(local_row)]
  transfers between devices with their start and end apart: 5 -> 9, of which waited for: 5 -> 7; matrix products, arithmetic and copies ran while one was open for 11% -> 12% of each run, Pallas kernels for 0% -> 1%
where the time goes in v1:
time: 227 us; the launch traced here: 226 us
  waiting for transfers between devices  105 us (46%)
  Pallas kernels  48.6 us (21%)
  local copies, waits for them, and re-layouts  42.7 us (19%)
  starting transfers between devices  19 us (8%)
  other arithmetic  10.1 us (4%)
    all_to_all x3, waiting for transfers between devices, exchange(): lax.all_to_all(payload, ('dp', 'blk'), split_axis=0, concat_axis=0, tiled...  90.9 us
    unnamed x19, local copies, waits for them, and re-layouts  22.1 us
    all_to_all x3, starting transfers between devices, exchange(): lax.all_to_all(payload, ('dp', 'blk'), split_axis=0, concat_axis=0, tiled...  15.8 us
    pallas_call x1, Pallas kernels, serve(): pl.pallas_call(functools.partial(serve_kernel, pack), out_shape=jax.Shape...  15.7 us
    pallas_call x1, Pallas kernels, update(): pl.pallas_call(functools.partial(update_kernel, pack, columns), grid=(row...  13.9 us
    ppermute x2, waiting for transfers between devices, to_chip(): lax.ppermute(value, 'blk', [(i, (i + 2 * hops) % blk_count) for i in rang...  11.2 us
    gather x2, local copies, waits for them, and re-layouts, on_device(): relations[rel_ids]  8.63 us
    pallas_call x1, Pallas kernels, unpack(): pl.pallas_call(functools.partial(unpack_kernel, pack, edges), out_shape=(...  6.5 us
  transfers between devices with their start and end apart: 9, of which 7 were waited for; matrix products, arithmetic and copies ran while one was open for 12% of the time, Pallas kernels for 1%

profile of v1, /device:TPU:0, one launch (start us, length us, event | category | flops | bytes accessed | tf_op | source)
XLA Modules:
  0.0 225.7 jit_solution(18092855608782167661)
XLA Ops:
  1.6 4.5 %gather_fusion = s32[768]{0:T(1024)S(1)} fusion(s32[65536]{0:T(1024)S(1)} %copy-done, s32[1024]{0:T(1024)S(1)} %pad_clamp_fusion.1), kind=kCustom, calls=%fused_computation | custom fusion | bytes 9216 | tf_op jit(solution)/shard_map/gather | solution.py:372
  6.7 4.2 %reduce-window.6 = s32[32,6,128]{2,0,1:T(8,128)} reduce-window(s32[32,6,128]{2,0,1:T(8,128)} %fusion.3, s32[]{:T(128)} %constant.37.clone.1), window={size=1x1x128 pad=0_0x0_0x127_0}, to_apply=%region_0.1 | reduce-window | flops 3121152 | bytes 196612 | tf_op jit(solution)/shard_map/reduce-window
  14.3 3.5 %scatter_custom_fusion = s32[1536]{0:T(1024)S(1)} fusion(s32[768]{0:T(1024)} %fusion.11, s32[768]{0:T(1024)} %get-tuple-element.24, s32[]{:T(128)} %constant.36.clone.1), kind=kCustom, calls=%fused_computation.37 | custom fusion | bytes 6656 | tf_op jit(solution)/shard_map/scatter | solution.py:382
  18.6 7.4 %all-to-all-start = ((s32[32,1,48]{2,1,0:T(1,128)}), s32[32,1,48]{2,1,0:T(1,128)}, u32[]{:S(2)}, u32[]{:S(2)}) async-start(s32[32,1,48]{2,1,0:T(1,128)} %all_to_all.12), calls=%async_computation | async-start | bytes 32768 | tf_op jit(solution)/shard_map/all_to_all | solution.py:345
  26.0 2.4 %table_rows.1.table_ref = f32[2048,4,128]{2,1,0:T(4,128)S(1)} custom-call(f32[400,2048]{1,0:T(8,128)S(1)} %bitcast.50), custom_call_target="tpu_custom_call" | custom-call | tf_op jit(solution)/shard_map/table_rows/pallas_call | solution.py:96
  28.4 1.9 copy-done.1
  30.3 2.6 %all-to-all-done = s32[32,1,48]{2,1,0:T(1,128)} async-done(((s32[32,1,48]{2,1,0:T(1,128)}), s32[32,1,48]{2,1,0:T(1,128)}, u32[]{:S(2)}, u32[]{:S(2)}) %all-to-all-start) | async-done | bytes 6176 | tf_op jit(solution)/shard_map/all_to_all | solution.py:345
  33.7 2.2 copy-done.2
  35.9 15.7 %serve_rows.1 = f32[4864,128]{1,0:T(8,128)S(1)} custom-call(s32[1536]{0:T(1024)S(1)} %reshape.239.asked_ref, f32[2048,4,128]{2,1,0:T(4,128)S(1)} %copy-done.2), custom_call_target="tpu_custom_call" | custom-call | tf_op jit(solution)/shard_map/serve_rows/pallas_call | solution.py:129
  53.0 3.7 %all-to-all-start.1 = ((f32[32,152,128]{2,1,0:T(8,128)}), f32[32,152,128]{2,1,0:T(8,128)}, u32[]{:S(2)}, u32[]{:S(2)}) async-start(f32[32,152,128]{2,1,0:T(8,128)} %bitcast.52), calls=%async_computation.1 | async-start | bytes 4980736 | tf_op jit(solution)/shard_map/all_to_all | solution.py:345
  56.7 14.1 %copy.18 = f32[7424,400]{1,0:T(8,128)} copy(f32[7424,400]{0,1:T(8,128)} %param.10) | data formatting | bytes 23756800 | tf_op args[2]
  70.9 6.9 %gather_fusion.1 = f32[128,400]{1,0:T(8,128)} fusion(f32[7424,400]{1,0:T(8,128)} %copy.18, s32[1024]{0:T(1024)S(1)} %pad_clamp_fusion), kind=kCustom, calls=%fused_computation.1 | custom fusion | bytes 410112 | tf_op jit(solution)/shard_map/gather | solution.py:388
  77.7 1.7 copy.19
  79.5 34.4 %all-to-all-done.1 = f32[32,152,128]{2,1,0:T(8,128)} async-done(((f32[32,152,128]{2,1,0:T(8,128)}), f32[32,152,128]{2,1,0:T(8,128)}, u32[]{:S(2)}, u32[]{:S(2)}) %all-to-all-start.1) | async-done | bytes 2490400 | tf_op jit(solution)/shard_map/all_to_all | solution.py:345
  114.8 6.5 %unpack_rows.1 = (f32[400,128]{1,0:T(8,128)S(1)}, f32[400,128]{1,0:T(8,128)S(1)}, f32[512,512]{1,0:T(8,128)S(1)}) custom-call(s32[768]{0:T(1024)S(1)} %get-tuple-element.23.address_ref, s32[768]{0:T(1024)S(1)} %get-tuple-element.22.slot_ref, f32[4864,128]{1,0:T(8,128)} %bitcast.7.packed_ref, f32[400,128]{1,0:T(8,128)S(1)} %bitcast.54), custom_call_target="tpu_custom_call" | custom-call | tf_op jit(solution)/shard_map/unpack_rows/pallas_call | solution.py:169
  122.6 5.4 %collective-permute-done.1.refs_3_ = f32[400,128]{1,0:T(8,128)S(1)} collective-permute-done((f32[400,128]{1,0:T(8,128)S(1)}, f32[400,128]{1,0:T(8,128)S(1)}, u32[]{:S(2)}, u32[]{:S(2)}) %collective-permute-start.1) | collective-permute-done | bytes 204832 | tf_op jit(solution)/shard_map/ppermute | solution.py:353
  129.5 4.4 %negative_terms.1 = (f32[512,512]{1,0:T(8,128)S(1)}, f32[400,128]{1,0:T(8,128)S(1)}, f32[400,128]{1,0:T(8,128)S(1)}, f32[400,128]{1,0:T(8,128)S(1)}, f32[400,128]{1,0:T(8,128)S(1)}) custom-call(f32[512,512]{1,0:T(8,128)S(1)} %get-tuple-element.12.refs_0_, f32[400,128]{1,0:T(8,128)S(1)} %get-tuple-element.13.refs_1_, ...), custom_call_target="tpu_custom_call" | custom-call | tf_op jit(solution)/shard_map/negative_terms/pallas_call | solution.py:217
  136.7 5.9 %collective-permute-done.5 = f32[400,128]{1,0:T(8,128)S(1)} collective-permute-done((f32[400,128]{1,0:T(8,128)S(1)}, f32[400,128]{1,0:T(8,128)S(1)}, u32[]{:S(2)}, u32[]{:S(2)}) %collective-permute-start.5) | collective-permute-done | bytes 204832 | tf_op jit(solution)/shard_map/ppermute | solution.py:353
  142.6 5.8 %pack_gradients.1 = f32[4864,128]{1,0:T(8,128)S(1)} custom-call(s32[768]{0:T(1024)S(1)} %get-tuple-element.23.address_ref, s32[768]{0:T(1024)S(1)} %get-tuple-element.22.slot_ref, f32[400,128]{1,0:T(8,128)S(1)} %add_add_fusion.query_grad_ref, f32[400,128]{1,0:T(8,128)S(1)} %get-tuple-element.18.positive_ref, f32[512,512]{1,0:T(8,128)S(1)} %get-tuple-element.19.block_ref), custom_call_target="tpu_custom_call" | custom-call | tf_op jit(solution)/shard_map/pack_gradients/pallas_call | solution.py:266
  148.4 1.5 copy-done.5
  149.9 4.7 %all-to-all-start.2 = ((f32[32,152,128]{2,1,0:T(8,128)}), f32[32,152,128]{2,1,0:T(8,128)}, u32[]{:S(2)}, u32[]{:S(2)}) async-start(f32[32,152,128]{2,1,0:T(8,128)} %bitcast.53), calls=%async_computation.2 | async-start | bytes 4980736 | tf_op jit(solution)/shard_map/all_to_all | solution.py:345
  155.1 2.0 reduce.11
  157.9 53.9 %all-to-all-done.2 = f32[32,152,128]{2,1,0:T(8,128)} async-done(((f32[32,152,128]{2,1,0:T(8,128)}), f32[32,152,128]{2,1,0:T(8,128)}, u32[]{:S(2)}, u32[]{:S(2)}) %all-to-all-start.2) | async-done | bytes 2490400 | tf_op jit(solution)/shard_map/all_to_all | solution.py:345
  211.9 13.9 %update_table.1 = (f32[400,2048]{1,0:T(8,128)}, f32[1,2048]{1,0:T(1,128)}) custom-call(s32[1,1536]{1,0:T(1,128)S(1)} %reshape_reshape.3.asked_ref, f32[4864,128]{1,0:T(8,128)} %bitcast.10.packed_ref, f32[1,2048]{1,0:T(1,128)S(1)} %bitcast.55, f32[400,2048]{1,0:T(8,128)S(1)} %bitcast.51), custom_call_target="tpu_custom_call" | custom-call | tf_op jit(solution)/shard_map/update_table/pallas_call | solution.py:319
  (43 shorter events, 15.9 us)
Async XLA Ops:
  0.6 1.0 copy-start
  0.6 25.4 %copy-start.3 = (f32[2048,400]{0,1:T(8,128)S(1)}, f32[2048,400]{0,1:T(8,128)}, u32[]{:S(2)}) copy-start(f32[2048,400]{0,1:T(8,128)} %param.8) | copy-start | bytes 9830404
  18.6 14.3 %all-to-all-start = ((s32[32,1,48]{2,1,0:T(1,128)}), s32[32,1,48]{2,1,0:T(1,128)}, u32[]{:S(2)}, u32[]{:S(2)}) async-start(s32[32,1,48]{2,1,0:T(1,128)} %all_to_all.12), calls=%async_computation | async-start | bytes 32768 | tf_op jit(solution)/shard_map/all_to_all | solution.py:345
  28.4 1.9 copy-start.1
  33.7 2.2 copy-start.2
  51.5 1.4 copy-start.4
  53.0 60.9 %all-to-all-start.1 = ((f32[32,152,128]{2,1,0:T(8,128)}), f32[32,152,128]{2,1,0:T(8,128)}, u32[]{:S(2)}, u32[]{:S(2)}) async-start(f32[32,152,128]{2,1,0:T(8,128)} %bitcast.52), calls=%async_computation.1 | async-start | bytes 4980736 | tf_op jit(solution)/shard_map/all_to_all | solution.py:345
  56.7 14.1 %copy-start.8 = (s32[128]{0:T(128)S(1)}, s32[128]{0:T(128)}, u32[]{:S(2)}) copy-start(s32[128]{0:T(128)} %param.13) | copy-start | bytes 1540
  113.9 0.9 copy-start.6
  121.3 6.7 %collective-permute-start.1 = (f32[400,128]{1,0:T(8,128)S(1)}, f32[400,128]{1,0:T(8,128)S(1)}, u32[]{:S(2)}, u32[]{:S(2)}) collective-permute-start(f32[400,128]{1,0:T(8,128)S(1)} %get-tuple-element.13.refs_1_), channel_id=1, source_target_pairs={{0,2},{1,3},{2,0},{3,1},{4,6},{5,7},{6,4},{7,5},{8,10},{9,11},{10,... | collective-permute-start | bytes 614408 | tf_op jit(solution)/shard_map/ppermute | solution.py:353
  122.6 5.4 %collective-permute-start = (f32[400,128]{1,0:T(8,128)S(1)}, f32[400,128]{1,0:T(8,128)S(1)}, u32[]{:S(2)}, u32[]{:S(2)}) collective-permute-start(f32[400,128]{1,0:T(8,128)S(1)} %get-tuple-element.13.refs_1_), channel_id=1, source_target_pairs={{0,1},{1,0},{2,3},{3,2},{4,5},{5,4},{6,7},{7,6},{8,9},{9,8},{10,11... | collective-permute-start | bytes 614408 | tf_op jit(solution)/shard_map/ppermute | solution.py:349
  128.0 1.5 collective-permute-start.2
  133.9 1.5 collective-permute-start.4
  134.1 2.7 %collective-permute-start.3 = (f32[400,128]{1,0:T(8,128)S(1)}, f32[400,128]{1,0:T(8,128)S(1)}, u32[]{:S(2)}, u32[]{:S(2)}) collective-permute-start(f32[400,128]{1,0:T(8,128)S(1)} %get-tuple-element.15), channel_id=1, source_target_pairs={{0,1},{1,0},{2,3},{3,2},{4,5},{5,4},{6,7},{7,6},{8,9},{9,8},{10,11... | collective-permute-start | bytes 614408 | tf_op jit(solution)/shard_map/ppermute | solution.py:349
  135.4 7.2 %collective-permute-start.5 = (f32[400,128]{1,0:T(8,128)S(1)}, f32[400,128]{1,0:T(8,128)S(1)}, u32[]{:S(2)}, u32[]{:S(2)}) collective-permute-start(f32[400,128]{1,0:T(8,128)S(1)} %add.78), channel_id=1, source_target_pairs={{0,2},{1,3},{2,0},{3,1},{4,6},{5,7},{6,4},{7,5},{8,10},{9,11},{10,... | collective-permute-start | bytes 614408 | tf_op jit(solution)/shard_map/ppermute | solution.py:353
  148.4 1.5 copy-start.5
  149.9 62.0 %copy-start.7 = (f32[2048]{0:T(1024)S(1)}, f32[2048]{0:T(1024)}, u32[]{:S(2)}) copy-start(f32[2048]{0:T(1024)} %param.9) | copy-start | bytes 24580
  149.9 62.0 %all-to-all-start.2 = ((f32[32,152,128]{2,1,0:T(8,128)}), f32[32,152,128]{2,1,0:T(8,128)}, u32[]{:S(2)}, u32[]{:S(2)}) async-start(f32[32,152,128]{2,1,0:T(8,128)} %bitcast.53), calls=%async_computation.2 | async-start | bytes 4980736 | tf_op jit(solution)/shard_map/all_to_all | solution.py:345

commit v2 on v1

--- a/solution.py
+++ b/solution.py
@@ -82,20 +82,87 @@
     loop(pack.owners, body)
 
 
+def one_hot(mask):
+    return mask.astype(jnp.float32).astype(jnp.bfloat16)
+
+
+def request_kernel(
+    pack, rows_here, map_ref, head_ref, tail_ref, negative_ref,
+    request_ref, address_ref, slot_ref,
+):
+    ids = jnp.concatenate([head_ref[...], tail_ref[...], negative_ref[...]], axis=1)
+    count = ids.shape[1]
+    lines = map_ref.shape[0]
+
+    def iota(rows, axis):
+        return lax.broadcasted_iota(jnp.int32, (rows, count), axis)
+
+    line_chosen = one_hot(iota(lines, 0) == ids // LANES)
+    table = map_ref[...].T
+    digits = [(table >> shift) & 255 for shift in range(0, 24, 8)]
+    stacked = jnp.concatenate(digits, axis=0).astype(jnp.float32).astype(jnp.bfloat16)
+    found = jnp.dot(stacked, line_chosen, preferred_element_type=jnp.float32)
+    found = found[:LANES] + 256.0 * found[LANES : 2 * LANES] + 65536.0 * found[2 * LANES :]
+    found = jnp.where(iota(LANES, 0) == ids % LANES, found, 0.0)
+    position = jnp.sum(found, axis=0, keepdims=True).astype(jnp.int32)
+    owner = position // rows_here
+    row = position % rows_here
+    to_owner = iota(pack.owners, 0) == owner
+    earlier = one_hot(iota(count, 0) < iota(count, 1))
+    before = jnp.dot(one_hot(to_owner), earlier, preferred_element_type=jnp.float32)
+    rank = jnp.sum(jnp.where(to_owner, before, 0.0), axis=0, keepdims=True).astype(jnp.int32)
+    slot_ref[...] = owner * pack.capacity + rank
+    address_ref[...] = owner * pack.stride + rank * pack.full
+    at_rank = one_hot(iota(pack.capacity, 0) == rank)
+    absent = row - rows_here
+
+    def place(values):
+        chosen = jnp.where(to_owner, values.astype(jnp.float32), 0.0).astype(jnp.bfloat16)
+        return lax.dot_general(
+            chosen, at_rank, (((1,), (1,)), ((), ())), preferred_element_type=jnp.float32
+        )
+
+    high = -((-absent) // 256)
+    low = absent - high * 256
+    request_ref[:, 0, :] = (place(high) * 256.0 + place(low)).astype(jnp.int32) + rows_here
+
+
+def build_requests(pack, rows_here, owner_map, head_ids, tail_ids, neg_ids):
+    count = head_ids.shape[0] + tail_ids.shape[0] + neg_ids.shape[0]
+    shape = jax.ShapeDtypeStruct
+    return pl.pallas_call(
+        functools.partial(request_kernel, pack, rows_here),
+        out_shape=(
+            shape((pack.owners, 1, pack.capacity), jnp.int32),
+            shape((1, count), jnp.int32),
+            shape((1, count), jnp.int32),
+        ),
+        in_specs=[vmem()] * 4,
+        out_specs=(vmem(),) * 3,
+        compiler_params=compiler_params(),
+        name="build_requests",
+    )(
+        owner_map.reshape(-1, LANES), head_ids.reshape(1, -1), tail_ids.reshape(1, -1),
+        neg_ids.reshape(1, -1),
+    )
+
+
 def rows_kernel(pack, columns_ref, rows_ref):
+    count = columns_ref.shape[1]
     fill = jnp.zeros((pack.wide - pack.width, LANES), jnp.float32)
-    for block in range(columns_ref.shape[1] // LANES):
+    for block in range(count // LANES):
         at = slice(block * LANES, (block + 1) * LANES)
         tile = jnp.concatenate([columns_ref[:, at], fill], axis=0)
         for c in range(pack.groups):
             rows_ref[at, c, :] = tile[c * LANES : (c + 1) * LANES].T
+    rows_ref[count:] = jnp.zeros((SUBLANES, pack.groups, LANES), jnp.float32)
 
 
 def to_rows(pack, columns):
     count = columns.shape[1]
     return pl.pallas_call(
         functools.partial(rows_kernel, pack),
-        out_shape=jax.ShapeDtypeStruct((count, pack.groups, LANES), jnp.float32),
+        out_shape=jax.ShapeDtypeStruct((count + SUBLANES, pack.groups, LANES), jnp.float32),
         in_specs=[vmem()],
         out_specs=vmem(),
         compiler_params=compiler_params(),
@@ -106,23 +173,22 @@
 def serve_kernel(pack, asked_ref, table_ref, out_ref):
     lane = lax.broadcasted_iota(jnp.int32, (pack.groups, LANES), 1) // pack.rest
 
-    def body(group):
-        owner = group // pack.shared
-        inner = group % pack.shared
-        base = owner * pack.stride
-        shared = None
-        for j in range(SUBLANES):
-            value = table_ref[jnp.maximum(asked_ref[group * SUBLANES + j], 0)]
-            out_ref[pl.ds(base + (inner * SUBLANES + j) * pack.full, pack.full), :] = value[
-                : pack.full
-            ]
-            if j == 0:
-                shared = value
-            else:
-                shared = jnp.where(lane == j, pltpu.roll(value, j * pack.rest, axis=1), shared)
-        out_ref[pl.ds(base + pack.rests_at + inner, 1), :] = shared[pack.full :]
-
-    loop(pack.slots // SUBLANES, body)
+    def body(owner):
+        base = pl.multiple_of(owner * pack.stride, SUBLANES)
+        for group in range(pack.shared):
+            first = group * SUBLANES
+            values = [table_ref[asked_ref[owner, 0, first + j]] for j in range(SUBLANES)]
+            shared = values[0]
+            for j in range(1, SUBLANES):
+                moved = pltpu.roll(values[j], j * pack.rest, axis=1)
+                shared = jnp.where(lane == j, moved, shared)
+            for j in range(SUBLANES):
+                out_ref[pl.ds(base + (first + j) * pack.full, pack.full), :] = values[j][
+                    : pack.full
+                ]
+            out_ref[pl.ds(base + pack.rests_at + group, 1), :] = shared[pack.full :]
+
+    loop(pack.owners, body)
 
 
 def serve(pack, asked, table_rows):
@@ -144,10 +210,18 @@
     count = rows_ref.shape[0]
 
     def body(group):
+        first = group * SUBLANES
+        values = []
         for j in range(SUBLANES):
-            row = group * SUBLANES + j
-            rows_ref[row, : pack.full, :] = packed_ref[pl.ds(address_ref[row], pack.full), :]
-            rows_ref[row, pack.full :, :] = rests_ref[pl.ds(slot_ref[row], 1), :]
+            values.append(
+                (
+                    packed_ref[pl.ds(address_ref[0, first + j], pack.full), :],
+                    rests_ref[pl.ds(slot_ref[0, first + j], 1), :],
+                )
+            )
+        for j, (groups, rest) in enumerate(values):
+            rows_ref[first + j, : pack.full, :] = groups
+            rows_ref[first + j, pack.full :, :] = rest
 
     loop(count // SUBLANES, body)
     for c in range(pack.groups):
@@ -242,11 +316,11 @@
         rows_ref[2 * edges :, c, :] = block_ref[:, at]
 
     def body(group):
-        for j in range(SUBLANES):
-            row = group * SUBLANES + j
-            value = rows_ref[row]
-            out_ref[pl.ds(address_ref[row], pack.full), :] = value[: pack.full]
-            rests_ref[pl.ds(slot_ref[row], 1), :] = value[pack.full :]
+        first = group * SUBLANES
+        values = [rows_ref[first + j] for j in range(SUBLANES)]
+        for j, value in enumerate(values):
+            out_ref[pl.ds(address_ref[0, first + j], pack.full), :] = value[: pack.full]
+            rests_ref[pl.ds(slot_ref[0, first + j], 1), :] = value[pack.full :]
 
     loop(rows_ref.shape[0] // SUBLANES, body)
 
@@ -368,19 +442,10 @@
     request_count = 2 * edge_count + neg_count
     capacity = -(-2 * request_count // owner_count // SUBLANES) * SUBLANES
     pack = Packing(width, owner_count, capacity)
-    wanted = jnp.concatenate([head_ids, tail_ids, neg_ids])
-    position = owner_map[wanted]
-    owner_of = position // rows_here
-    local_row = position % rows_here
-    onehot = (owner_of[:, None] == jnp.arange(owner_count, dtype=jnp.int32)[None, :]).astype(
-        jnp.int32
-    )
-    before = jnp.cumsum(onehot, axis=0) - onehot
-    rank_in = jnp.sum(before * onehot, axis=1)
-    slot_of = owner_of * capacity + rank_in
-    address = owner_of * pack.stride + rank_in * pack.full
-    requests = jnp.full((pack.slots,), -1, jnp.int32).at[slot_of].set(local_row)
-    asked = exchange(requests.reshape(owner_count, capacity)).reshape(-1)
+    requests, address, slot_of = build_requests(
+        pack, rows_here, owner_map, head_ids, tail_ids, neg_ids
+    )
+    asked = exchange(requests)
     served = serve(pack, asked, to_rows(pack, entity_table.T))
     fetched = exchange(served.reshape(owner_count, pack.stride, LANES))
     queries, positive, negatives = unpack(

time: 227 us -> 201 us (0.89)
  Pallas kernels: 48.6 us -> 38 us
  local copies, waits for them, and re-layouts: 42.7 us -> 32.9 us
  other arithmetic: 10.1 us -> 0.77 us
    pallas_call x1, Pallas kernels: 15.7 us -> 4.46 us  [serve(): pl.pallas_call(functools.partial(serve_kernel, pack), out_shape=jax.Shape...]
    gather x1 -> x0, local copies, waits for them, and re-layouts: 4.45 us -> none  [on_device(): position = owner_map[wanted]]
    another operation x2 -> x0, other arithmetic: 4.23 us -> none
    unnamed x19 -> x25, local copies, waits for them, and re-layouts: 22.1 us -> 26 us
    scatter x1 -> x0, local copies, waits for them, and re-layouts: 3.52 us -> none  [on_device(): requests = jnp.full((pack.slots,), -1, jnp.int32).at[slot_of].set(local_row)]
    all_to_all x3, waiting for transfers between devices: 90.9 us -> 93.6 us  [exchange(): lax.all_to_all(payload, ('dp', 'blk'), split_axis=0, concat_axis=0, tiled...]
    gather x2, local copies, waits for them, and re-layouts: 8.63 us -> 6.32 us  [on_device(): relations[rel_ids]]
  transfers between devices with their start and end apart: 9 -> 9, of which waited for: 7 -> 7; matrix products, arithmetic and copies ran while one was open for 12% -> 11% of each run, Pallas kernels for 1% -> 1%
where the time goes in v2:
time: 201 us; the launch traced here: 200 us
  waiting for transfers between devices  107 us (53%)
  Pallas kernels  38 us (19%)
  local copies, waits for them, and re-layouts  32.9 us (16%)
  starting transfers between devices  20.6 us (10%)
    all_to_all x3, waiting for transfers between devices, exchange(): lax.all_to_all(payload, ('dp', 'blk'), split_axis=0, concat_axis=0, tiled...  93.6 us
    unnamed x25, local copies, waits for them, and re-layouts  26 us
    all_to_all x3, starting transfers between devices, exchange(): lax.all_to_all(payload, ('dp', 'blk'), split_axis=0, concat_axis=0, tiled...  17.2 us
    pallas_call x1, Pallas kernels, update(): pl.pallas_call(functools.partial(update_kernel, pack, columns), grid=(row...  13.9 us
    ppermute x2, waiting for transfers between devices, to_chip(): lax.ppermute(value, 'blk', [(i, (i + 2 * hops) % blk_count) for i in rang...  11.1 us
    gather x2, local copies, waits for them, and re-layouts, on_device(): relations[rel_ids]  6.32 us
    pallas_call x1, Pallas kernels, pack_gradients(): pl.pallas_call(functools.partial(pack_kernel, pack, edges), out_shape=jax...  5.79 us
    pallas_call x1, Pallas kernels, unpack(): pl.pallas_call(functools.partial(unpack_kernel, pack, edges), out_shape=(...  5.43 us
  transfers between devices with their start and end apart: 9, of which 7 were waited for; matrix products, arithmetic and copies ran while one was open for 11% of the time, Pallas kernels for 1%

profile of v2, /device:TPU:0, one launch (start us, length us, event | category | flops | bytes accessed | tf_op | source)
XLA Modules:
  0.0 200.1 jit_solution(1361742438975333437)
XLA Ops:
  3.6 1.7 build_requests.1
  5.3 7.3 %all-to-all-start = ((s32[32,1,48]{2,1,0:T(1,128)}), s32[32,1,48]{2,1,0:T(1,128)S(1)}, u32[]{:S(2)}, u32[]{:S(2)}) async-start(s32[32,1,48]{2,1,0:T(1,128)} %get-tuple-element.15), calls=%async_computation | async-start | bytes 32768 | tf_op jit(solution)/shard_map/all_to_all | solution.py:419
  12.6 1.9 copy-done.2
  14.5 2.4 %table_rows.1.table_ref = f32[2056,4,128]{2,1,0:T(4,128)S(1)} custom-call(f32[400,2048]{1,0:T(8,128)S(1)} %bitcast.13), custom_call_target="tpu_custom_call" | custom-call | tf_op jit(solution)/shard_map/table_rows/pallas_call | solution.py:163
  16.9 1.9 copy-done
  19.7 2.2 %copy-done.1 = f32[2056,4,128]{2,1,0:T(4,128)S(1)} copy-done((f32[2056,4,128]{2,1,0:T(4,128)S(1)}, f32[2056,4,128]{2,1,0:T(4,128)}, u32[]{:S(2)}) %copy-start.1) | copy-done | bytes 4210712
  21.9 4.5 %serve_rows.1 = f32[4864,128]{1,0:T(8,128)S(1)} custom-call(s32[32,1,48]{2,1,0:T(1,128)S(1)} %all-to-all-done.asked_ref, f32[2056,4,128]{2,1,0:T(4,128)S(1)} %copy-done.1), custom_call_target="tpu_custom_call" | custom-call | tf_op jit(solution)/shard_map/serve_rows/pallas_call | solution.py:195
  26.4 1.4 copy-done.5
  27.8 5.0 %all-to-all-start.1 = ((f32[32,152,128]{2,1,0:T(8,128)}), f32[32,152,128]{2,1,0:T(8,128)S(1)}, u32[]{:S(2)}, u32[]{:S(2)}) async-start(f32[32,152,128]{2,1,0:T(8,128)} %bitcast.17), calls=%async_computation.1 | async-start | bytes 4980736 | tf_op jit(solution)/shard_map/all_to_all | solution.py:419
  32.8 14.1 %copy.10 = f32[7424,400]{1,0:T(8,128)} copy(f32[7424,400]{0,1:T(8,128)} %param.10) | data formatting | bytes 23756800 | tf_op args[2]
  47.0 6.2 %gather_fusion = f32[128,400]{1,0:T(8,128)S(1)} fusion(f32[7424,400]{1,0:T(8,128)} %copy.10, s32[1024]{0:T(1024)S(1)} %pad_clamp_fusion), kind=kCustom, calls=%fused_computation | custom fusion | bytes 410112 | tf_op jit(solution)/shard_map/gather | solution.py:453
  53.3 36.8 %all-to-all-done.1 = f32[32,152,128]{2,1,0:T(8,128)S(1)} async-done(((f32[32,152,128]{2,1,0:T(8,128)}), f32[32,152,128]{2,1,0:T(8,128)S(1)}, u32[]{:S(2)}, u32[]{:S(2)}) %all-to-all-start.1) | async-done | bytes 2490400 | tf_op jit(solution)/shard_map/all_to_all | solution.py:419
  90.1 5.4 %unpack_rows.1 = (f32[400,128]{1,0:T(8,128)S(1)}, f32[400,128]{1,0:T(8,128)S(1)}, f32[512,512]{1,0:T(8,128)S(1)}) custom-call(s32[1,768]{1,0:T(1,128)S(1)} %get-tuple-element.16.address_ref, s32[1,768]{1,0:T(1,128)S(1)} %get-tuple-element.17.slot_ref, f32[4864,128]{1,0:T(8,128)S(1)} %bitcast.15, f32[400,128]{1,0:T(8,128)S(1)} %bitcast.18), custom_call_target="tpu_custom_call" | custom-call | tf_op jit(solution)/shard_map/unpack_rows/pallas_call | solution.py:243
  95.5 1.4 collective-permute-start.1
  96.9 5.3 %collective-permute-done.1.refs_3_ = f32[400,128]{1,0:T(8,128)S(1)} collective-permute-done((f32[400,128]{1,0:T(8,128)S(1)}, f32[400,128]{1,0:T(8,128)S(1)}, u32[]{:S(2)}, u32[]{:S(2)}) %collective-permute-start.1) | collective-permute-done | bytes 204832 | tf_op jit(solution)/shard_map/ppermute | solution.py:427
  102.2 1.4 collective-permute-done.2.refs_4_
  103.7 4.4 %negative_terms.1 = (f32[512,512]{1,0:T(8,128)S(1)}, f32[400,128]{1,0:T(8,128)S(1)}, f32[400,128]{1,0:T(8,128)S(1)}, f32[400,128]{1,0:T(8,128)S(1)}, f32[400,128]{1,0:T(8,128)S(1)}) custom-call(f32[512,512]{1,0:T(8,128)S(1)} %get-tuple-element.18.refs_0_, f32[400,128]{1,0:T(8,128)S(1)} %get-tuple-element.19.refs_1_, ...), custom_call_target="tpu_custom_call" | custom-call | tf_op jit(solution)/shard_map/negative_terms/pallas_call | solution.py:291
  109.6 1.4 collective-permute-start.5
  111.0 5.8 %collective-permute-done.5 = f32[400,128]{1,0:T(8,128)S(1)} collective-permute-done((f32[400,128]{1,0:T(8,128)S(1)}, f32[400,128]{1,0:T(8,128)S(1)}, u32[]{:S(2)}, u32[]{:S(2)}) %collective-permute-start.5) | collective-permute-done | bytes 204832 | tf_op jit(solution)/shard_map/ppermute | solution.py:427
  116.8 5.8 %pack_gradients.1 = f32[4864,128]{1,0:T(8,128)S(1)} custom-call(s32[1,768]{1,0:T(1,128)S(1)} %get-tuple-element.16.address_ref, s32[1,768]{1,0:T(1,128)S(1)} %get-tuple-element.17.slot_ref, f32[400,128]{1,0:T(8,128)S(1)} %add_add_fusion.query_grad_ref, f32[400,128]{1,0:T(8,128)S(1)} %get-tuple-element.24.positive_ref, f32[512,512]{1,0:T(8,128)S(1)} %get-tuple-element.25.block_ref), custom_call_target="tpu_custom_call" | custom-call | tf_op jit(solution)/shard_map/pack_gradients/pallas_call | solution.py:340
  122.6 1.5 copy-done.4
  124.1 4.9 %all-to-all-start.2 = ((f32[32,152,128]{2,1,0:T(8,128)}), f32[32,152,128]{2,1,0:T(8,128)}, u32[]{:S(2)}, u32[]{:S(2)}) async-start(f32[32,152,128]{2,1,0:T(8,128)} %bitcast.16), calls=%async_computation.2 | async-start | bytes 4980736 | tf_op jit(solution)/shard_map/all_to_all | solution.py:419
  130.3 56.0 %all-to-all-done.2 = f32[32,152,128]{2,1,0:T(8,128)} async-done(((f32[32,152,128]{2,1,0:T(8,128)}), f32[32,152,128]{2,1,0:T(8,128)}, u32[]{:S(2)}, u32[]{:S(2)}) %all-to-all-start.2) | async-done | bytes 2490400 | tf_op jit(solution)/shard_map/all_to_all | solution.py:419
  186.2 13.9 %update_table.1 = (f32[400,2048]{1,0:T(8,128)}, f32[1,2048]{1,0:T(1,128)}) custom-call(s32[1,1536]{1,0:T(1,128)S(1)} %reshape.41.asked_ref, f32[4864,128]{1,0:T(8,128)} %bitcast.9.packed_ref, f32[1,2048]{1,0:T(1,128)S(1)} %bitcast.20, f32[400,2048]{1,0:T(8,128)S(1)} %bitcast.14), custom_call_target="tpu_custom_call" | custom-call | tf_op jit(solution)/shard_map/update_table/pallas_call | solution.py:393
  (35 shorter events, 6.8 us)
Async XLA Ops:
  0.6 1.0 copy-start.6
  1.6 0.7 copy-start.8
  2.3 0.7 copy-start.9
  2.9 0.7 copy-start.10
  5.3 14.4 %all-to-all-start = ((s32[32,1,48]{2,1,0:T(1,128)}), s32[32,1,48]{2,1,0:T(1,128)S(1)}, u32[]{:S(2)}, u32[]{:S(2)}) async-start(s32[32,1,48]{2,1,0:T(1,128)} %get-tuple-element.15), calls=%async_computation | async-start | bytes 32768 | tf_op jit(solution)/shard_map/all_to_all | solution.py:419
  12.6 1.9 copy-start.2
  16.9 1.9 copy-start
  19.7 2.2 %copy-start.1 = (f32[2056,4,128]{2,1,0:T(4,128)S(1)}, f32[2056,4,128]{2,1,0:T(4,128)}, u32[]{:S(2)}) copy-start(f32[2056,4,128]{2,1,0:T(4,128)} %copy-done) | copy-start | bytes 12632068
  26.3 1.5 copy-start.5
  27.8 62.3 %all-to-all-start.1 = ((f32[32,152,128]{2,1,0:T(8,128)}), f32[32,152,128]{2,1,0:T(8,128)S(1)}, u32[]{:S(2)}, u32[]{:S(2)}) async-start(f32[32,152,128]{2,1,0:T(8,128)} %bitcast.17), calls=%async_computation.1 | async-start | bytes 4980736 | tf_op jit(solution)/shard_map/all_to_all | solution.py:419
  32.8 14.1 %copy-start.11 = (s32[128]{0:T(128)S(1)}, s32[128]{0:T(128)}, u32[]{:S(2)}) copy-start(s32[128]{0:T(128)} %param.13) | copy-start | bytes 1540
  95.5 6.7 %collective-permute-start.1 = (f32[400,128]{1,0:T(8,128)S(1)}, f32[400,128]{1,0:T(8,128)S(1)}, u32[]{:S(2)}, u32[]{:S(2)}) collective-permute-start(f32[400,128]{1,0:T(8,128)S(1)} %get-tuple-element.19.refs_1_), channel_id=1, source_target_pairs={{0,2},{1,3},{2,0},{3,1},{4,6},{5,7},{6,4},{7,5},{8,10},{9,11},{10,... | collective-permute-start | bytes 614408 | tf_op jit(solution)/shard_map/ppermute | solution.py:427
  96.9 5.3 %collective-permute-start = (f32[400,128]{1,0:T(8,128)S(1)}, f32[400,128]{1,0:T(8,128)S(1)}, u32[]{:S(2)}, u32[]{:S(2)}) collective-permute-start(f32[400,128]{1,0:T(8,128)S(1)} %get-tuple-element.19.refs_1_), channel_id=1, source_target_pairs={{0,1},{1,0},{2,3},{3,2},{4,5},{5,4},{6,7},{7,6},{8,9},{9,8},{10,11... | collective-permute-start | bytes 614408 | tf_op jit(solution)/shard_map/ppermute | solution.py:423
  102.2 1.5 collective-permute-start.2
  108.0 1.5 collective-permute-start.4
  108.2 2.8 %collective-permute-start.3 = (f32[400,128]{1,0:T(8,128)S(1)}, f32[400,128]{1,0:T(8,128)S(1)}, u32[]{:S(2)}, u32[]{:S(2)}) collective-permute-start(f32[400,128]{1,0:T(8,128)S(1)} %get-tuple-element.21), channel_id=1, source_target_pairs={{0,1},{1,0},{2,3},{3,2},{4,5},{5,4},{6,7},{7,6},{8,9},{9,8},{10,11... | collective-permute-start | bytes 614408 | tf_op jit(solution)/shard_map/ppermute | solution.py:423
  109.6 7.2 %collective-permute-start.5 = (f32[400,128]{1,0:T(8,128)S(1)}, f32[400,128]{1,0:T(8,128)S(1)}, u32[]{:S(2)}, u32[]{:S(2)}) collective-permute-start(f32[400,128]{1,0:T(8,128)S(1)} %add.18), channel_id=1, source_target_pairs={{0,2},{1,3},{2,0},{3,1},{4,6},{5,7},{6,4},{7,5},{8,10},{9,11},{10,... | collective-permute-start | bytes 614408 | tf_op jit(solution)/shard_map/ppermute | solution.py:427
  122.6 1.5 copy-start.4
  124.1 62.2 %copy-start.3 = (f32[2048,400]{0,1:T(8,128)S(1)}, f32[2048,400]{0,1:T(8,128)}, u32[]{:S(2)}) copy-start(f32[2048,400]{0,1:T(8,128)} %param.8) | copy-start | bytes 9830404
  124.1 62.2 %copy-start.7 = (f32[2048]{0:T(1024)S(1)}, f32[2048]{0:T(1024)}, u32[]{:S(2)}) copy-start(f32[2048]{0:T(1024)} %param.9) | copy-start | bytes 24580
  124.1 62.2 %all-to-all-start.2 = ((f32[32,152,128]{2,1,0:T(8,128)}), f32[32,152,128]{2,1,0:T(8,128)}, u32[]{:S(2)}, u32[]{:S(2)}) async-start(f32[32,152,128]{2,1,0:T(8,128)} %bitcast.16), calls=%async_computation.2 | async-start | bytes 4980736 | tf_op jit(solution)/shard_map/all_to_all | solution.py:419

commit v3 on v2

v3 whole, which is shorter than its diff:
```python
import functools

import jax
import jax.numpy as jnp
from jax import lax
from jax.experimental import pallas as pl
from jax.experimental.pallas import tpu as pltpu
from jax.sharding import PartitionSpec as P

MARGIN = 10.0
EPSILON = 1e-05
LEARNING_RATE = 0.1
LANES = 128
SUBLANES = 8
VMEM_BYTES = 24 * 1024 * 1024
HIGHEST = lax.Precision.HIGHEST


class Packing:
    def __init__(self, width, owners, capacity):
        self.width = width
        self.owners = owners
        self.capacity = capacity
        self.full = width // LANES
        self.rest = width - self.full * LANES
        assert 0 < self.rest <= LANES // SUBLANES and capacity % SUBLANES == 0
        self.shared = capacity // SUBLANES
        self.groups = self.full + 1
        self.wide = self.groups * LANES
        self.rests_at = self.full * capacity
        self.stride = -(-(self.rests_at + self.shared) // SUBLANES) * SUBLANES
        self.slots = owners * capacity
        self.rows = owners * self.stride


def compiler_params():
    return pltpu.CompilerParams(vmem_limit_bytes=VMEM_BYTES)


def vmem():
    return pl.BlockSpec(memory_space=pltpu.VMEM)


def smem():
    return pl.BlockSpec(memory_space=pltpu.SMEM)


def hbm():
    return pl.BlockSpec(memory_space=pltpu.HBM)


def in_hbm(value):
    return pltpu.with_memory_space_constraint(value, pltpu.HBM)


def split(value):
    high = value.astype(jnp.bfloat16)
    low = (value - high.astype(jnp.float32)).astype(jnp.bfloat16)
    return high, low


def dot_halves(left, right, contract):
    numbers = (contract, ((), ()))

    def dot(a, b):
        return lax.dot_general(a, b, numbers, preferred_element_type=jnp.float32)

    return dot(left[0], right[0]) + (dot(left[0], right[1]) + dot(left[1], right[0]))


def loop(count, body):
    def step(index, carry):
        body(index)
        return carry

    lax.fori_loop(0, count, step, 0)


def expand_rests(pack, packed_ref, shared_ref, rests_ref):
    for owner in range(pack.owners):
        shared_ref[owner * pack.shared : (owner + 1) * pack.shared, :] = packed_ref[
            pl.ds(owner * pack.stride + pack.rests_at, pack.shared), :
        ]
    shared = shared_ref[...]
    lane = lax.broadcasted_iota(jnp.int32, shared.shape, 1)
    for j in range(SUBLANES):
        moved = shared if j == 0 else pltpu.roll(shared, LANES - j * pack.rest, axis=1)
        rests_ref[pl.ds(j, shared.shape[0], stride=SUBLANES), :] = jnp.where(
            lane < pack.rest, moved, 0.0
        )


def rests_scratch(pack):
    return [
        pltpu.VMEM((pack.owners * pack.shared, LANES), jnp.float32),
        pltpu.VMEM((pack.slots, LANES), jnp.float32),
    ]


def row_columns(pack, rows):
    parts = [rows[:, c, :].T for c in range(pack.groups)]
    return jnp.concatenate(parts, axis=0)[: pack.width]


def one_hot(mask):
    return mask.astype(jnp.float32).astype(jnp.bfloat16)


def request_kernel(
    pack, rows_here, map_hbm, head_hbm, tail_hbm, negative_hbm,
    request_ref, address_ref, slot_ref, map_ref, ids_ref, sems,
):
    copies = [pltpu.make_async_copy(map_hbm, map_ref, sems.at[0])]
    first = 0
    for index, source in enumerate((head_hbm, tail_hbm, negative_hbm)):
        target = ids_ref.at[:, pl.ds(first, source.shape[1])]
        copies.append(pltpu.make_async_copy(source, target, sems.at[index + 1]))
        first += source.shape[1]
    for copy in copies:
        copy.start()
    for copy in copies:
        copy.wait()
    ids = ids_ref[...]
    count = ids.shape[1]
    lines = map_ref.shape[0]

    def iota(rows, axis):
        return lax.broadcasted_iota(jnp.int32, (rows, count), axis)

    line_chosen = one_hot(iota(lines, 0) == ids // LANES)
    table = map_ref[...].T
    digits = [(table >> shift) & 255 for shift in range(0, 24, 8)]
    stacked = jnp.concatenate(digits, axis=0).astype(jnp.float32).astype(jnp.bfloat16)
    found = jnp.dot(stacked, line_chosen, preferred_element_type=jnp.float32)
    found = found[:LANES] + 256.0 * found[LANES : 2 * LANES] + 65536.0 * found[2 * LANES :]
    found = jnp.where(iota(LANES, 0) == ids % LANES, found, 0.0)
    position = jnp.sum(found, axis=0, keepdims=True).astype(jnp.int32)
    owner = position // rows_here
    row = position % rows_here
    to_owner = iota(pack.owners, 0) == owner
    earlier = one_hot(iota(count, 0) < iota(count, 1))
    before = jnp.dot(one_hot(to_owner), earlier, preferred_element_type=jnp.float32)
    rank = jnp.sum(jnp.where(to_owner, before, 0.0), axis=0, keepdims=True).astype(jnp.int32)
    slot_ref[...] = owner * pack.capacity + rank
    address_ref[...] = owner * pack.stride + rank * pack.full
    at_rank = one_hot(iota(pack.capacity, 0) == rank)
    absent = row - rows_here

    def place(values):
        chosen = jnp.where(to_owner, values.astype(jnp.float32), 0.0).astype(jnp.bfloat16)
        return lax.dot_general(
            chosen, at_rank, (((1,), (1,)), ((), ())), preferred_element_type=jnp.float32
        )

    high = -((-absent) // 256)
    low = absent - high * 256
    request_ref[:, 0, :] = (place(high) * 256.0 + place(low)).astype(jnp.int32) + rows_here


def build_requests(pack, rows_here, owner_map, head_ids, tail_ids, neg_ids):
    count = head_ids.shape[0] + tail_ids.shape[0] + neg_ids.shape[0]
    shape = jax.ShapeDtypeStruct
    return pl.pallas_call(
        functools.partial(request_kernel, pack, rows_here),
        out_shape=(
            shape((pack.owners, 1, pack.capacity), jnp.int32),
            shape((1, count), jnp.int32),
            shape((1, count), jnp.int32),
        ),
        in_specs=[hbm()] * 4,
        out_specs=(vmem(),) * 3,
        scratch_shapes=[
            pltpu.VMEM((owner_map.shape[0] // LANES, LANES), jnp.int32),
            pltpu.VMEM((1, count), jnp.int32),
            pltpu.SemaphoreType.DMA((4,)),
        ],
        compiler_params=compiler_params(),
        name="build_requests",
    )(
        in_hbm(owner_map.reshape(-1, LANES)), in_hbm(head_ids.reshape(1, -1)),
        in_hbm(tail_ids.reshape(1, -1)), in_hbm(neg_ids.reshape(1, -1)),
    )


def rows_kernel(pack, columns_ref, rows_hbm, rows_ref, sem):
    count = columns_ref.shape[1]
    fill = jnp.zeros((pack.wide - pack.width, LANES), jnp.float32)
    for block in range(count // LANES):
        at = slice(block * LANES, (block + 1) * LANES)
        tile = jnp.concatenate([columns_ref[:, at], fill], axis=0)
        for c in range(pack.groups):
            rows_ref[at, c, :] = tile[c * LANES : (c + 1) * LANES].T
    rows_ref[count:] = jnp.zeros((SUBLANES, pack.groups, LANES), jnp.float32)
    copy = pltpu.make_async_copy(rows_ref, rows_hbm, sem)
    copy.start()
    copy.wait()


def to_rows(pack, columns):
    count = columns.shape[1]
    return pl.pallas_call(
        functools.partial(rows_kernel, pack),
        out_shape=pltpu.HBM((count + SUBLANES, pack.groups, LANES), jnp.float32),
        in_specs=[vmem()],
        out_specs=hbm(),
        scratch_shapes=[
            pltpu.VMEM((count + SUBLANES, pack.groups, LANES), jnp.float32),
            pltpu.SemaphoreType.DMA(()),
        ],
        compiler_params=compiler_params(),
        name="table_rows",
    )(columns)


def sends(pack, out_ref, out_hbm, sems):
    count = sems.shape[0]
    each = pack.owners // count
    copies = []
    for index in range(count):
        rows = pl.ds(index * each * pack.stride, each * pack.stride)
        copies.append(pltpu.make_async_copy(out_ref.at[rows, :], out_hbm.at[rows, :], sems.at[index]))
    return copies, each


def serve_kernel(pack, asked_ref, table_hbm, out_hbm, table_ref, out_ref, sems, table_sem):
    load = pltpu.make_async_copy(table_hbm, table_ref, table_sem)
    load.start()
    load.wait()
    lane = lax.broadcasted_iota(jnp.int32, (pack.groups, LANES), 1) // pack.rest
    copies, each = sends(pack, out_ref, out_hbm, sems)

    def body(owner):
        base = pl.multiple_of(owner * pack.stride, SUBLANES)
        for group in range(pack.shared):
            first = group * SUBLANES
            values = [table_ref[asked_ref[owner, 0, first + j]] for j in range(SUBLANES)]
            shared = values[0]
            for j in range(1, SUBLANES):
                moved = pltpu.roll(values[j], j * pack.rest, axis=1)
                shared = jnp.where(lane == j, moved, shared)
            for j in range(SUBLANES):
                out_ref[pl.ds(base + (first + j) * pack.full, pack.full), :] = values[j][
                    : pack.full
                ]
            out_ref[pl.ds(base + pack.rests_at + group, 1), :] = shared[pack.full :]

    for index, copy in enumerate(copies):
        loop(each, lambda owner: body(index * each + owner))
        copy.start()
    for copy in copies:
        copy.wait()


def serve(pack, asked, table_rows):
    return pl.pallas_call(
        functools.partial(serve_kernel, pack),
        out_shape=pltpu.HBM((pack.rows, LANES), jnp.float32),
        in_specs=[smem(), hbm()],
        out_specs=hbm(),
        scratch_shapes=[
            pltpu.VMEM(table_rows.shape, jnp.float32),
            pltpu.VMEM((pack.rows, LANES), jnp.float32),
            pltpu.SemaphoreType.DMA((8,)),
            pltpu.SemaphoreType.DMA(()),
        ],
        compiler_params=compiler_params(),
        name="serve_rows",
    )(asked, in_hbm(table_rows))


def copy_rows(pack, first_request, address_ref, slot_ref, packed_ref, rests_ref, rows_ref):
    def body(group):
        first = group * SUBLANES
        values = []
        for j in range(SUBLANES):
            request = first_request + first + j
            values.append(
                (
                    packed_ref[pl.ds(address_ref[0, request], pack.full), :],
                    rests_ref[pl.ds(slot_ref[0, request], 1), :],
                )
            )
        for j, (groups, rest) in enumerate(values):
            rows_ref[first + j, : pack.full, :] = groups
            rows_ref[first + j, pack.full :, :] = rest

    loop(rows_ref.shape[0] // SUBLANES, body)


def heads_kernel(
    pack, address_ref, slot_ref, packed_ref, relation_ref,
    query_ref, shared_ref, rests_ref, rows_ref,
):
    expand_rests(pack, packed_ref, shared_ref, rests_ref)
    copy_rows(pack, 0, address_ref, slot_ref, packed_ref, rests_ref, rows_ref)
    query_ref[...] = row_columns(pack, rows_ref[...]) + relation_ref[...]


def unpack_heads(pack, edges, address, slot, packed, relation_rows):
    return pl.pallas_call(
        functools.partial(heads_kernel, pack),
        out_shape=jax.ShapeDtypeStruct((pack.width, edges), jnp.float32),
        in_specs=[smem(), smem(), vmem(), vmem()],
        out_specs=vmem(),
        scratch_shapes=rests_scratch(pack)
        + [pltpu.VMEM((edges, pack.groups, LANES), jnp.float32)],
        compiler_params=compiler_params(),
        cost_estimate=pl.CostEstimate(flops=10**7, bytes_accessed=3 * 10**6, transcendentals=0),
        name="unpack_heads",
    )(address, slot, packed, relation_rows)


def rest_kernel(
    pack, edges, address_ref, slot_ref, packed_ref, query_ref,
    positive_ref, negative_ref, shared_ref, rests_ref, rows_ref,
):
    expand_rests(pack, packed_ref, shared_ref, rests_ref)
    copy_rows(pack, edges, address_ref, slot_ref, packed_ref, rests_ref, rows_ref)
    for c in range(pack.groups):
        negative_ref[:, c * LANES : (c + 1) * LANES] = rows_ref[edges:, c, :]
    residue = query_ref[...] - row_columns(pack, rows_ref[:edges])
    distance = jnp.sqrt(jnp.sum(residue * residue, axis=0, keepdims=True) + EPSILON)
    positive_ref[...] = jax.nn.sigmoid(distance - MARGIN) / distance * residue


def unpack_rest(pack, negatives, address, slot, packed, queries):
    edges = queries.shape[1]
    shape = jax.ShapeDtypeStruct
    return pl.pallas_call(
        functools.partial(rest_kernel, pack, edges),
        out_shape=(
            shape((pack.width, edges), jnp.float32),
            shape((negatives, pack.wide), jnp.float32),
        ),
        in_specs=[smem(), smem(), vmem(), vmem()],
        out_specs=(vmem(), vmem()),
        scratch_shapes=rests_scratch(pack)
        + [pltpu.VMEM((edges + negatives, pack.groups, LANES), jnp.float32)],
        compiler_params=compiler_params(),
        cost_estimate=pl.CostEstimate(flops=10**7, bytes_accessed=9 * 10**6, transcendentals=0),
        name="unpack_rest",
    )(address, slot, packed, queries)


def gather_queries(pack, query_refs):
    queries = jnp.concatenate([ref[...] for ref in query_refs], axis=1)
    fill = jnp.zeros((pack.wide - pack.width, queries.shape[1]), jnp.float32)
    return jnp.concatenate([queries, fill], axis=0)


def negatives_kernel(pack, blocks, weight, *refs):
    negative_ref = refs[0]
    query_refs = refs[1 : 1 + blocks]
    coefficient_ref, *part_refs = refs[1 + blocks :]
    negatives = negative_ref[...]
    queries = gather_queries(pack, query_refs)
    query_sq = jnp.sum(queries * queries, axis=0, keepdims=True)
    block_sq = jnp.sum(negatives * negatives, axis=1, keepdims=True)
    inner = jnp.dot(negatives, queries, precision=HIGHEST, preferred_element_type=jnp.float32)
    distance = jnp.sqrt(query_sq + block_sq - 2.0 * inner + EPSILON)
    coefficient = -1.0 / ((1.0 + jnp.exp(distance - MARGIN)) * (weight * distance))
    coefficient_ref[...] = coefficient
    part = queries * jnp.sum(coefficient, axis=0, keepdims=True) - dot_halves(
        split(negatives.T), split(coefficient), ((1,), (0,))
    )
    width = query_refs[0].shape[1]
    for index, ref in enumerate(part_refs):
        ref[...] = part[: pack.width, index * width : (index + 1) * width]


def negative_terms(pack, weight, negatives, queries):
    shape = jax.ShapeDtypeStruct
    count = sum(q.shape[1] for q in queries)
    rows = negatives.shape[0]
    return pl.pallas_call(
        functools.partial(negatives_kernel, pack, len(queries), weight),
        out_shape=(shape((rows, count), jnp.float32),)
        + tuple(shape(q.shape, jnp.float32) for q in queries),
        in_specs=[vmem()] * (1 + len(queries)),
        out_specs=(vmem(),) * (1 + len(queries)),
        compiler_params=compiler_params(),
        cost_estimate=pl.CostEstimate(
            flops=18 * rows * count * pack.wide, bytes_accessed=4 * 10**6, transcendentals=0
        ),
        name="negative_terms",
    )(negatives, *queries)


def store_rows(pack, first_request, address_ref, slot_ref, rows_ref, out_ref, rests_ref):
    def body(group):
        first = group * SUBLANES
        values = [rows_ref[first + j] for j in range(SUBLANES)]
        for j, value in enumerate(values):
            request = first_request + first + j
            out_ref[pl.ds(address_ref[0, request], pack.full), :] = value[: pack.full]
            rests_ref[pl.ds(slot_ref[0, request], 1), :] = value[pack.full :]

    loop(rows_ref.shape[0] // SUBLANES, body)


def store_columns(pack, columns, rows_ref):
    fill = jnp.zeros((pack.wide - pack.width, columns.shape[1]), jnp.float32)
    columns = jnp.concatenate([columns, fill], axis=0)
    for c in range(pack.groups):
        rows_ref[:, c, :] = columns[c * LANES : (c + 1) * LANES].T


def block_kernel(pack, blocks, coefficients, address_ref, slot_ref, *refs):
    positive_ref, negative_ref = refs[:2]
    query_refs = refs[2 : 2 + blocks]
    coefficient_refs = refs[2 + blocks : 2 + blocks + coefficients]
    out_ref, rests_ref, rows_ref = refs[2 + blocks + coefficients :]
    edges = positive_ref.shape[1]
    out_ref[...] = jnp.zeros_like(out_ref)
    rests_ref[...] = jnp.zeros_like(rests_ref)
    store_columns(pack, -positive_ref[...], rows_ref.at[:edges])
    coefficient = jnp.concatenate([ref[...] for ref in coefficient_refs], axis=1)
    block_grad = negative_ref[...] * jnp.sum(coefficient, axis=1, keepdims=True) - dot_halves(
        split(coefficient), split(gather_queries(pack, query_refs)), ((1,), (1,))
    )
    for c in range(pack.groups):
        rows_ref[edges:, c, :] = block_grad[:, c * LANES : (c + 1) * LANES]
    store_rows(pack, edges, address_ref, slot_ref, rows_ref, out_ref, rests_ref)


def block_gradients(pack, address, slot, positive, negatives, queries, coefficients):
    shape = jax.ShapeDtypeStruct
    rows = positive.shape[1] + negatives.shape[0]
    flops = 6 * sum(c.size for c in coefficients) * pack.wide
    return pl.pallas_call(
        functools.partial(block_kernel, pack, len(queries), len(coefficients)),
        out_shape=(
            shape((pack.rows, LANES), jnp.float32),
            shape((pack.slots, LANES), jnp.float32),
        ),
        in_specs=[smem()] * 2 + [vmem()] * (2 + len(queries) + len(coefficients)),
        out_specs=(vmem(), vmem()),
        scratch_shapes=[pltpu.VMEM((rows, pack.groups, LANES), jnp.float32)],
        compiler_params=compiler_params(),
        cost_estimate=pl.CostEstimate(
            flops=flops, bytes_accessed=10**7, transcendentals=0
        ),
        name="block_gradients",
    )(address, slot, positive, negatives, *queries, *coefficients)


def finish_kernel(pack, parts, address_ref, slot_ref, *refs):
    partial_ref, partial_rests_ref, positive_ref = refs[:3]
    part_refs = refs[3 : 3 + parts]
    out_hbm, out_ref, rests_ref, rows_ref, sems = refs[3 + parts :]
    copies, each = sends(pack, out_ref, out_hbm, sems)
    out_ref[...] = partial_ref[...]
    rests_ref[...] = partial_rests_ref[...]
    total = positive_ref[...]
    for ref in part_refs:
        total = total + ref[...]
    store_columns(pack, total, rows_ref)
    store_rows(pack, 0, address_ref, slot_ref, rows_ref, out_ref, rests_ref)
    count = each * pack.shared
    for index, copy in enumerate(copies):
        first = index * each * pack.capacity
        shared = rests_ref[pl.ds(first, count, stride=SUBLANES), :]
        for j in range(1, SUBLANES):
            block = rests_ref[pl.ds(first + j, count, stride=SUBLANES), :]
            shared = shared + pltpu.roll(block, j * pack.rest, axis=1)
        for owner in range(each):
            start = (index * each + owner) * pack.stride + pack.rests_at
            out_ref[pl.ds(start, pack.shared), :] = shared[
                owner * pack.shared : (owner + 1) * pack.shared
            ]
        copy.start()
    for copy in copies:
        copy.wait()


def finish_gradients(pack, address, slot, partial, partial_rests, positive, parts):
    edges = positive.shape[1]
    return pl.pallas_call(
        functools.partial(finish_kernel, pack, len(parts)),
        out_shape=pltpu.HBM((pack.rows, LANES), jnp.float32),
        in_specs=[smem()] * 2 + [vmem()] * (3 + len(parts)),
        out_specs=hbm(),
        scratch_shapes=[
            pltpu.VMEM((pack.rows, LANES), jnp.float32),
            pltpu.VMEM((pack.slots, LANES), jnp.float32),
            pltpu.VMEM((edges, pack.groups, LANES), jnp.float32),
            pltpu.SemaphoreType.DMA((8,)),
        ],
        compiler_params=compiler_params(),
        name="finish_gradients",
    )(address, slot, partial, partial_rests, positive, *parts)


def update_kernel(
    pack, columns, asked_ref, packed_ref, sum_ref, table_ref,
    new_table_hbm, new_sum_ref, shared_ref, rests_ref, rows_ref, halves_ref, out_ref, sems,
):
    expand_rests(pack, packed_ref, shared_ref, rests_ref)

    def body(owner):
        rows = pl.ds(pl.multiple_of(owner * pack.capacity, SUBLANES), pack.capacity)
        for c in range(pack.full):
            rows_ref[rows, c * LANES : (c + 1) * LANES] = packed_ref[
                pl.ds(owner * pack.stride + c, pack.capacity, stride=pack.full), :
            ]
        rows_ref[rows, pack.full * LANES :] = rests_ref[rows, :]

    loop(pack.owners, body)
    width = pack.width
    high, low = split(rows_ref[...].T)
    halves_ref[:width] = high[:width]
    halves_ref[width:] = low[:width]
    asked = asked_ref[...]
    row = lax.broadcasted_iota(jnp.int32, (columns, pack.slots), 0)
    copies = []
    for index in range(table_ref.shape[1] // columns):
        at = slice(index * columns, (index + 1) * columns)
        chosen = one_hot(row == asked - index * columns)
        both = lax.dot_general(
            halves_ref[...], chosen, (((1,), (1,)), ((), ())), preferred_element_type=jnp.float32
        )
        summed = both[:width] + both[width:]
        new_sum = sum_ref[:, at] + jnp.sum(summed * summed, axis=0, keepdims=True) / width
        new_sum_ref[:, at] = new_sum
        out_ref[:, at] = table_ref[:, at] - summed * (LEARNING_RATE / jnp.sqrt(new_sum))
        copies.append(
            pltpu.make_async_copy(out_ref.at[:, at], new_table_hbm.at[:, at], sems.at[index])
        )
        copies[-1].start()
    for copy in copies:
        copy.wait()


def update(pack, asked, packed, adagrad_sum, table_columns):
    width, rows = table_columns.shape
    columns = 256
    shape = jax.ShapeDtypeStruct
    return pl.pallas_call(
        functools.partial(update_kernel, pack, columns),
        out_shape=(pltpu.HBM((width, rows), jnp.float32), shape((1, rows), jnp.float32)),
        in_specs=[vmem()] * 4,
        out_specs=(hbm(), vmem()),
        scratch_shapes=rests_scratch(pack)
        + [
            pltpu.VMEM((pack.slots, pack.wide), jnp.float32),
            pltpu.VMEM((2 * width, pack.slots), jnp.bfloat16),
            pltpu.VMEM((width, rows), jnp.float32),
            pltpu.SemaphoreType.DMA((rows // columns,)),
        ],
        compiler_params=compiler_params(),
        name="update_table",
    )(asked, packed, adagrad_sum, table_columns)


def exchange(payload):
    return lax.all_to_all(payload, ("dp", "blk"), split_axis=0, concat_axis=0, tiled=True)


def to_sibling(value, blk_count):
    return lax.ppermute(value, "blk", [(i, i ^ 1) for i in range(blk_count)])


def to_chip(value, blk_count, hops):
    return lax.ppermute(
        value, "blk", [(i, (i + 2 * hops) % blk_count) for i in range(blk_count)]
    )


def on_device(
    entity_table, adagrad_sum, relations, owner_map, head_ids, rel_ids, tail_ids, neg_ids
):
    dp_count = lax.axis_size("dp")
    blk_count = lax.axis_size("blk")
    owner_count = dp_count * blk_count
    chip_count = blk_count // 2
    rows_here, width = entity_table.shape
    edge_count = head_ids.shape[0]
    neg_count = neg_ids.shape[0]
    request_count = 2 * edge_count + neg_count
    capacity = -(-2 * request_count // owner_count // SUBLANES) * SUBLANES
    pack = Packing(width, owner_count, capacity)
    requests, address, slot_of = build_requests(
        pack, rows_here, owner_map, head_ids, tail_ids, neg_ids
    )
    asked = exchange(requests)
    served = serve(pack, asked, to_rows(pack, entity_table.T))
    fetched = exchange(served.reshape(owner_count, pack.stride, LANES))
    fetched = fetched.reshape(pack.rows, LANES)
    queries = unpack_heads(pack, edge_count, address, slot_of, fetched, relations[rel_ids].T)
    weight = float(blk_count * neg_count)
    arriving = [to_chip(queries, blk_count, hops) for hops in range(1, chip_count)]
    nearby = [queries, to_sibling(queries, blk_count)]
    positive, negatives = unpack_rest(pack, neg_count, address, slot_of, fetched, queries)
    near, *near_parts = negative_terms(pack, weight, negatives, nearby)
    arriving, near, near_parts = lax.optimization_barrier((arriving, near, near_parts))
    distant = []
    for same in arriving:
        distant += [same, to_sibling(same, blk_count)]
    far, *far_parts = negative_terms(pack, weight, negatives, distant)
    group = nearby + distant
    totals = [near_parts[0], to_sibling(near_parts[1], blk_count)]
    for hops in range(1, chip_count):
        total = far_parts[2 * hops - 2] + to_sibling(far_parts[2 * hops - 1], blk_count)
        totals.append(to_chip(total, blk_count, chip_count - hops))
    partial, partial_rests = block_gradients(
        pack, address, slot_of, positive, negatives, group, (near, far)
    )
    outgoing = finish_gradients(
        pack, address, slot_of, partial, partial_rests, positive, totals
    )
    incoming = exchange(outgoing.reshape(owner_count, pack.stride, LANES))
    new_columns, new_sum = update(
        pack, asked.reshape(1, -1), incoming.reshape(pack.rows, LANES),
        adagrad_sum.reshape(1, -1), entity_table.T,
    )
    return (new_columns.T, new_sum.reshape(-1))


def solution(mesh):
    return jax.shard_map(
        on_device,
        mesh=mesh,
        in_specs=(
            P(("dp", "blk"), None),
            P(("dp", "blk")),
            P(),
            P(),
            P(("dp", "blk")),
            P(("dp", "blk")),
            P(("dp", "blk")),
            P(("dp", "blk")),
        ),
        out_specs=(P(("dp", "blk"), None), P(("dp", "blk"))),
        check_vma=False,
    )
```

time: 201 us -> 185 us (0.920)
  local copies, waits for them, and re-layouts: 32.9 us -> 23 us
  waiting for transfers between devices: 107 us -> 98.6 us
  Pallas kernels: 38 us -> 40.1 us
    unnamed x25 -> x9, local copies, waits for them, and re-layouts: 26 us -> 16.1 us
    ppermute x2, waiting for transfers between devices: 11.1 us -> 2.91 us  [to_chip(): lax.ppermute(value, 'blk', [(i, (i + 2 * hops) % blk_count) for i in rang...]
    pallas_call x1 -> x2, Pallas kernels: 4.37 us -> 5.24 us  [negative_terms(): pl.pallas_call(functools.partial(negatives_kernel, pack, len(queries), we...]
    pallas_call x5 -> x7, Pallas kernels: 31.9 us -> 32.1 us  [the longest x1 9.72 us: update(): pl.pallas_call(functools.partial(update_kernel, pack, columns), out_shape...]
  transfers between devices with their start and end apart: 9 -> 9, of which waited for: 7 -> 7; matrix products, arithmetic and copies ran while one was open for 11% -> 12% of each run, Pallas kernels for 1% -> 7%
where the time goes in v3:
time: 185 us; the launch traced here: 184 us
  waiting for transfers between devices  98.6 us (53%)
  Pallas kernels  40.1 us (22%)
  local copies, waits for them, and re-layouts  23 us (12%)
  starting transfers between devices  20.5 us (11%)
    all_to_all x3, waiting for transfers between devices, exchange(): lax.all_to_all(payload, ('dp', 'blk'), split_axis=0, concat_axis=0, tiled...  93.3 us
    all_to_all x3, starting transfers between devices, exchange(): lax.all_to_all(payload, ('dp', 'blk'), split_axis=0, concat_axis=0, tiled...  17.2 us
    unnamed x9, local copies, waits for them, and re-layouts  16.1 us
    pallas_call x1, Pallas kernels, update(): pl.pallas_call(functools.partial(update_kernel, pack, columns), out_shape...  9.72 us
    pallas_call x1, Pallas kernels, serve(): pl.pallas_call(functools.partial(serve_kernel, pack), out_shape=pltpu.HBM...  7.45 us
    gather x2, local copies, waits for them, and re-layouts, on_device(): relations[rel_ids]  6.32 us
    pallas_call x2, Pallas kernels, negative_terms(): pl.pallas_call(functools.partial(negatives_kernel, pack, len(queries), we...  5.24 us
    pallas_call x1, Pallas kernels, to_rows(): pl.pallas_call(functools.partial(rows_kernel, pack), out_shape=pltpu.HBM(...  4.33 us
  transfers between devices with their start and end apart: 9, of which 7 were waited for; matrix products, arithmetic and copies ran while one was open for 12% of the time, Pallas kernels for 7%

profile of v3, /device:TPU:0, one launch (start us, length us, event | category | flops | bytes accessed | tf_op | source)
XLA Modules:
  0.0 183.9 jit_solution(12997357007306905222)
XLA Ops:
  0.6 2.7 %build_requests.1 = (s32[32,1,48]{2,1,0:T(1,128)}, s32[1,768]{1,0:T(1,128)S(1)}, s32[1,768]{1,0:T(1,128)S(1)}) custom-call(s32[512,128]{1,0:T(8,128)} %bitcast.21, s32[1,128]{1,0:T(1,128)} %bitcast.23, s32[1,128]{1,0:T(1,128)} %bitcast.24, s32[1,512]{1,0:T(1,128)} %bitcast.22), custom_call_target="tpu_custom_call" | custom-call | tf_op jit(solution)/shard_map/build_requests/pallas_call | solution.py:163
  3.4 7.3 %all-to-all-start = ((s32[32,1,48]{2,1,0:T(1,128)}), s32[32,1,48]{2,1,0:T(1,128)S(1)}, u32[]{:S(2)}, u32[]{:S(2)}) async-start(s32[32,1,48]{2,1,0:T(1,128)} %get-tuple-element.21), calls=%async_computation | async-start | bytes 32768 | tf_op jit(solution)/shard_map/all_to_all | solution.py:556
  10.7 1.9 %copy-done = f32[2048,400]{0,1:T(8,128)S(1)} copy-done((f32[2048,400]{0,1:T(8,128)S(1)}, f32[2048,400]{0,1:T(8,128)}, u32[]{:S(2)}) %copy-start) | copy-done | bytes 3276824
  12.6 4.3 %table_rows.1.table_hbm = f32[2056,4,128]{2,1,0:T(4,128)} custom-call(f32[400,2048]{1,0:T(8,128)S(1)} %bitcast.15), custom_call_target="tpu_custom_call" | custom-call | tf_op jit(solution)/shard_map/table_rows/pallas_call | solution.py:201
  16.9 0.8 all-to-all-done.asked_ref
  17.7 7.5 %serve_rows.1 = f32[4864,128]{1,0:T(8,128)} custom-call(s32[32,1,48]{2,1,0:T(1,128)S(1)} %all-to-all-done.asked_ref, f32[2056,4,128]{2,1,0:T(4,128)} %table_rows.1.table_hbm), custom_call_target="tpu_custom_call" | custom-call | tf_op jit(solution)/shard_map/serve_rows/pallas_call | solution.py:255
  25.2 5.2 %all-to-all-start.1 = ((f32[32,152,128]{2,1,0:T(8,128)}), f32[32,152,128]{2,1,0:T(8,128)S(1)}, u32[]{:S(2)}, u32[]{:S(2)}) async-start(f32[32,152,128]{2,1,0:T(8,128)} %bitcast.19), calls=%async_computation.1 | async-start | bytes 4980736 | tf_op jit(solution)/shard_map/all_to_all | solution.py:556
  30.4 14.1 %copy.10 = f32[7424,400]{1,0:T(8,128)} copy(f32[7424,400]{0,1:T(8,128)} %param.10) | data formatting | bytes 23756800 | tf_op args[2]
  44.6 6.2 %gather_fusion = f32[128,400]{1,0:T(8,128)S(1)} fusion(f32[7424,400]{1,0:T(8,128)} %copy.10, s32[1024]{0:T(1024)S(1)} %pad_clamp_fusion), kind=kCustom, calls=%fused_computation | custom fusion | bytes 410112 | tf_op jit(solution)/shard_map/gather | solution.py:589
  50.9 36.7 %all-to-all-done.1 = f32[32,152,128]{2,1,0:T(8,128)S(1)} async-done(((f32[32,152,128]{2,1,0:T(8,128)}), f32[32,152,128]{2,1,0:T(8,128)S(1)}, u32[]{:S(2)}, u32[]{:S(2)}) %all-to-all-start.1) | async-done | bytes 2490400 | tf_op jit(solution)/shard_map/all_to_all | solution.py:556
  87.6 1.3 unpack_heads.1.query_ref.refs_1_.refs_2_
  89.0 1.4 collective-permute-start.1
  90.3 2.9 %unpack_rest.1 = (f32[400,128]{1,0:T(8,128)S(1)}, f32[512,512]{1,0:T(8,128)S(1)}) custom-call(s32[1,768]{1,0:T(1,128)S(1)} %get-tuple-element.22.address_ref, s32[1,768]{1,0:T(1,128)S(1)} %get-tuple-element.23.slot_ref, f32[4864,128]{1,0:T(8,128)S(1)} %bitcast.14, f32[400,128]{1,0:T(8,128)S(1)} %unpack_heads.1.query_ref.refs_1_.refs_2_), custom_call_target="tpu_custom_call" | custom-call | flops 10000000 | bytes 9000000 | tf_op jit(solution)/shard_map/unpack_rest/pallas_call | solution.py:329
  93.2 2.6 %negative_terms.2 = (f32[512,256]{1,0:T(8,128)S(1)}, f32[400,128]{1,0:T(8,128)S(1)}, f32[400,128]{1,0:T(8,128)S(1)}) custom-call(f32[512,512]{1,0:T(8,128)S(1)} %get-tuple-element.25.refs_0_.refs_1_, f32[400,128]{1,0:T(8,128)S(1)} %unpack_heads.1.query_ref.refs_1_.refs_2_, f32[400,128]{1,0:T(8,128)S(1)} %collective-permute-done.refs_2_.refs_3_), custom_call_target="tpu_custom_call" | custom-call | flops 1207959552 | bytes 4000000 | tf_op jit(solution)/shard_map/negative_terms/pallas_call | solution.py:375
  96.5 1.5 collective-permute-done.2.refs_2_.refs_5_
  97.9 2.6 %negative_terms.3 = (f32[512,256]{1,0:T(8,128)S(1)}, f32[400,128]{1,0:T(8,128)S(1)}, f32[400,128]{1,0:T(8,128)S(1)}) custom-call(f32[512,512]{1,0:T(8,128)S(1)} %get-tuple-element.25.refs_0_.refs_1_, f32[400,128]{1,0:T(8,128)S(1)} %collective-permute-done.1.refs_1_.refs_4_, f32[400,128]{1,0:T(8,128)S(1)} %collective-permute-done.2.refs_2_.refs_5_), custom_call_target="tpu_custom_call" | custom-call | flops 1207959552 | bytes 4000000 | tf_op jit(solution)/shard_map/negative_terms/pallas_call | solution.py:375
  101.1 0.9 collective-permute-done.4
  102.1 1.4 collective-permute-start.5
  103.4 3.5 %block_gradients.1 = (f32[4864,128]{1,0:T(8,128)S(1)}, f32[1536,128]{1,0:T(8,128)S(1)}) custom-call(s32[1,768]{1,0:T(1,128)S(1)} %get-tuple-element.22.address_ref, s32[1,768]{1,0:T(1,128)S(1)} %get-tuple-element.23.slot_ref, f32[400,128]{1,0:T(8,128)S(1)} %get-tuple-element.24.refs_0_.refs_2_, f32[512,512]{1,0:T(8,128)S(1)} %get-tuple-element.25.refs_0_.refs_1_, ...), custom_call_target="tpu_custom_call" | custom-call | flops 805306368 | bytes 10000000 | tf_op jit(solution)/shard_map/block_gradients/pallas_call | solution.py:430
  107.0 2.3 %collective-permute-done.5.refs_5_ = f32[400,128]{1,0:T(8,128)S(1)} collective-permute-done((f32[400,128]{1,0:T(8,128)S(1)}, f32[400,128]{1,0:T(8,128)S(1)}, u32[]{:S(2)}, u32[]{:S(2)}) %collective-permute-start.5) | collective-permute-done | bytes 204832 | tf_op jit(solution)/shard_map/ppermute | solution.py:564
  109.3 2.9 %finish_gradients.1 = f32[4864,128]{1,0:T(8,128)} custom-call(s32[1,768]{1,0:T(1,128)S(1)} %get-tuple-element.22.address_ref, s32[1,768]{1,0:T(1,128)S(1)} %get-tuple-element.23.slot_ref, f32[4864,128]{1,0:T(8,128)S(1)} %get-tuple-element.32.refs_0_, f32[1536,128]{1,0:T(8,128)S(1)} %get-tuple-element.33.refs_1_, ...), custom_call_target="tpu_custom_call" | custom-call | tf_op jit(solution)/shard_map/finish_gradients/pallas_call | solution.py:478
  112.2 4.6 %all-to-all-start.2 = ((f32[32,152,128]{2,1,0:T(8,128)}), f32[32,152,128]{2,1,0:T(8,128)}, u32[]{:S(2)}, u32[]{:S(2)}) async-start(f32[32,152,128]{2,1,0:T(8,128)} %bitcast.20), calls=%async_computation.2 | async-start | bytes 4980736 | tf_op jit(solution)/shard_map/all_to_all | solution.py:556
  118.2 55.8 %all-to-all-done.2 = f32[32,152,128]{2,1,0:T(8,128)} async-done(((f32[32,152,128]{2,1,0:T(8,128)}), f32[32,152,128]{2,1,0:T(8,128)}, u32[]{:S(2)}, u32[]{:S(2)}) %all-to-all-start.2) | async-done | bytes 2490400 | tf_op jit(solution)/shard_map/all_to_all | solution.py:556
  174.0 9.7 %update_table.1 = (f32[400,2048]{1,0:T(8,128)}, f32[1,2048]{1,0:T(1,128)}) custom-call(s32[1,1536]{1,0:T(1,128)S(1)} %reshape.41.asked_ref, f32[4864,128]{1,0:T(8,128)} %bitcast.9.packed_ref, f32[1,2048]{1,0:T(1,128)S(1)} %bitcast.18, f32[400,2048]{1,0:T(8,128)S(1)} %bitcast.16), custom_call_target="tpu_custom_call" | custom-call | tf_op jit(solution)/shard_map/update_table/pallas_call | solution.py:538
  (21 shorter events, 2.7 us)
Async XLA Ops:
  3.4 14.4 %all-to-all-start = ((s32[32,1,48]{2,1,0:T(1,128)}), s32[32,1,48]{2,1,0:T(1,128)S(1)}, u32[]{:S(2)}, u32[]{:S(2)}) async-start(s32[32,1,48]{2,1,0:T(1,128)} %get-tuple-element.21), calls=%async_computation | async-start | bytes 32768 | tf_op jit(solution)/shard_map/all_to_all | solution.py:556
  10.7 1.9 %copy-start = (f32[2048,400]{0,1:T(8,128)S(1)}, f32[2048,400]{0,1:T(8,128)}, u32[]{:S(2)}) copy-start(f32[2048,400]{0,1:T(8,128)} %param.8) | copy-start | bytes 9830404
  25.2 62.4 %all-to-all-start.1 = ((f32[32,152,128]{2,1,0:T(8,128)}), f32[32,152,128]{2,1,0:T(8,128)S(1)}, u32[]{:S(2)}, u32[]{:S(2)}) async-start(f32[32,152,128]{2,1,0:T(8,128)} %bitcast.19), calls=%async_computation.1 | async-start | bytes 4980736 | tf_op jit(solution)/shard_map/all_to_all | solution.py:556
  30.4 14.1 %copy-start.3 = (s32[128]{0:T(128)S(1)}, s32[128]{0:T(128)}, u32[]{:S(2)}) copy-start(s32[128]{0:T(128)} %param.13) | copy-start | bytes 1540
  88.9 4.3 %collective-permute-start = (f32[400,128]{1,0:T(8,128)S(1)}, f32[400,128]{1,0:T(8,128)S(1)}, u32[]{:S(2)}, u32[]{:S(2)}) collective-permute-start(f32[400,128]{1,0:T(8,128)S(1)} %unpack_heads.1.query_ref.refs_1_.refs_2_), channel_id=1, source_target_pairs={{0,1},{1,0},{2,3},{3,2},{4,5},{5,4},{6,7},{7,6},{8,9},{9,8},{10,11... | collective-permute-start | bytes 614408 | tf_op jit(solution)/shard_map/ppermute | solution.py:560
  89.0 7.5 %collective-permute-start.1 = (f32[400,128]{1,0:T(8,128)S(1)}, f32[400,128]{1,0:T(8,128)S(1)}, u32[]{:S(2)}, u32[]{:S(2)}) collective-permute-start(f32[400,128]{1,0:T(8,128)S(1)} %unpack_heads.1.query_ref.refs_1_.refs_2_), channel_id=1, source_target_pairs={{0,2},{1,3},{2,0},{3,1},{4,6},{5,7},{6,4},{7,5},{8,10},{9,11},{10,... | collective-permute-start | bytes 614408 | tf_op jit(solution)/shard_map/ppermute | solution.py:564
  96.5 1.5 collective-permute-start.2
  100.5 1.5 collective-permute-start.4
  100.7 6.2 %collective-permute-start.3 = (f32[400,128]{1,0:T(8,128)S(1)}, f32[400,128]{1,0:T(8,128)S(1)}, u32[]{:S(2)}, u32[]{:S(2)}) collective-permute-start(f32[400,128]{1,0:T(8,128)S(1)} %get-tuple-element.35), channel_id=1, source_target_pairs={{0,1},{1,0},{2,3},{3,2},{4,5},{5,4},{6,7},{7,6},{8,9},{9,8},{10,11... | collective-permute-start | bytes 614408 | tf_op jit(solution)/shard_map/ppermute | solution.py:560
  102.1 7.2 %collective-permute-start.5 = (f32[400,128]{1,0:T(8,128)S(1)}, f32[400,128]{1,0:T(8,128)S(1)}, u32[]{:S(2)}, u32[]{:S(2)}) collective-permute-start(f32[400,128]{1,0:T(8,128)S(1)} %add.11), channel_id=1, source_target_pairs={{0,2},{1,3},{2,0},{3,1},{4,6},{5,7},{6,4},{7,5},{8,10},{9,11},{10,... | collective-permute-start | bytes 614408 | tf_op jit(solution)/shard_map/ppermute | solution.py:564
  112.2 61.8 %copy-start.1 = (f32[2048,400]{0,1:T(8,128)S(1)}, f32[2048,400]{0,1:T(8,128)}, u32[]{:S(2)}) copy-start(f32[2048,400]{0,1:T(8,128)} %param.8) | copy-start | bytes 9830404
  112.2 61.8 %copy-start.2 = (f32[2048]{0:T(1024)S(1)}, f32[2048]{0:T(1024)}, u32[]{:S(2)}) copy-start(f32[2048]{0:T(1024)} %param.9) | copy-start | bytes 24580
  112.2 61.8 %all-to-all-start.2 = ((f32[32,152,128]{2,1,0:T(8,128)}), f32[32,152,128]{2,1,0:T(8,128)}, u32[]{:S(2)}, u32[]{:S(2)}) async-start(f32[32,152,128]{2,1,0:T(8,128)} %bitcast.20), calls=%async_computation.2 | async-start | bytes 4980736 | tf_op jit(solution)/shard_map/all_to_all | solution.py:556

commit v4 on v3

--- a/solution.py
+++ b/solution.py
@@ -13,7 +13,6 @@
 LANES = 128
 SUBLANES = 8
 VMEM_BYTES = 24 * 1024 * 1024
-HIGHEST = lax.Precision.HIGHEST
 
 
 class Packing:
@@ -76,18 +75,19 @@
     lax.fori_loop(0, count, step, 0)
 
 
-def expand_rests(pack, packed_ref, shared_ref, rests_ref):
-    for owner in range(pack.owners):
+def expand_rests(pack, packed_ref, shared_ref, rests_ref, first_owner=0, owners=None):
+    owners = pack.owners if owners is None else owners
+    for owner in range(first_owner, first_owner + owners):
         shared_ref[owner * pack.shared : (owner + 1) * pack.shared, :] = packed_ref[
             pl.ds(owner * pack.stride + pack.rests_at, pack.shared), :
         ]
-    shared = shared_ref[...]
+    first = first_owner * pack.shared
+    shared = shared_ref[first : first + owners * pack.shared, :]
     lane = lax.broadcasted_iota(jnp.int32, shared.shape, 1)
     for j in range(SUBLANES):
         moved = shared if j == 0 else pltpu.roll(shared, LANES - j * pack.rest, axis=1)
-        rests_ref[pl.ds(j, shared.shape[0], stride=SUBLANES), :] = jnp.where(
-            lane < pack.rest, moved, 0.0
-        )
+        rows = pl.ds(first * SUBLANES + j, shared.shape[0], stride=SUBLANES)
+        rests_ref[rows, :] = jnp.where(lane < pack.rest, moved, 0.0)
 
 
 def rests_scratch(pack):
@@ -222,30 +222,53 @@
     return copies, each
 
 
-def serve_kernel(pack, asked_ref, table_hbm, out_hbm, table_ref, out_ref, sems, table_sem):
-    load = pltpu.make_async_copy(table_hbm, table_ref, table_sem)
-    load.start()
-    load.wait()
-    lane = lax.broadcasted_iota(jnp.int32, (pack.groups, LANES), 1) // pack.rest
+def share_rests(pack, rests_ref, out_ref, first_owner, owners):
+    count = owners * pack.shared
+    first = first_owner * pack.capacity
+    shared = rests_ref[pl.ds(first, count, stride=SUBLANES), :]
+    place = lax.broadcasted_iota(jnp.int32, shared.shape, 1) // pack.rest
+    for j in range(1, SUBLANES):
+        block = rests_ref[pl.ds(first + j, count, stride=SUBLANES), :]
+        shared = jnp.where(place == j, pltpu.roll(block, j * pack.rest, axis=1), shared)
+    for owner in range(owners):
+        start = (first_owner + owner) * pack.stride + pack.rests_at
+        out_ref[pl.ds(start, pack.shared), :] = shared[
+            owner * pack.shared : (owner + 1) * pack.shared
+        ]
+
+
+def serve_kernel(
+    pack, asked_ref, table_hbm, out_hbm, table_ref, out_ref, rests_ref, sems, table_sems
+):
+    pieces = table_sems.shape[0]
+    rows = table_ref.shape[0] // pieces
+    loads = []
+    for index in range(pieces):
+        at = pl.ds(index * rows, rows)
+        loads.append(
+            pltpu.make_async_copy(table_hbm.at[at], table_ref.at[at], table_sems.at[index])
+        )
+        loads[-1].start()
+    for load in loads:
+        load.wait()
     copies, each = sends(pack, out_ref, out_hbm, sems)
 
     def body(owner):
         base = pl.multiple_of(owner * pack.stride, SUBLANES)
-        for group in range(pack.shared):
-            first = group * SUBLANES
+        slots = pl.multiple_of(owner * pack.capacity, SUBLANES)
+        for first in range(0, pack.capacity, SUBLANES):
             values = [table_ref[asked_ref[owner, 0, first + j]] for j in range(SUBLANES)]
-            shared = values[0]
-            for j in range(1, SUBLANES):
-                moved = pltpu.roll(values[j], j * pack.rest, axis=1)
-                shared = jnp.where(lane == j, moved, shared)
+            rests_ref[pl.ds(slots + first, SUBLANES), :] = jnp.concatenate(
+                [value[pack.full :] for value in values], axis=0
+            )
             for j in range(SUBLANES):
                 out_ref[pl.ds(base + (first + j) * pack.full, pack.full), :] = values[j][
                     : pack.full
                 ]
-            out_ref[pl.ds(base + pack.rests_at + group, 1), :] = shared[pack.full :]
 
     for index, copy in enumerate(copies):
         loop(each, lambda owner: body(index * each + owner))
+        share_rests(pack, rests_ref, out_ref, index * each, each)
         copy.start()
     for copy in copies:
         copy.wait()
@@ -260,8 +283,9 @@
         scratch_shapes=[
             pltpu.VMEM(table_rows.shape, jnp.float32),
             pltpu.VMEM((pack.rows, LANES), jnp.float32),
+            pltpu.VMEM((pack.slots, LANES), jnp.float32),
             pltpu.SemaphoreType.DMA((8,)),
-            pltpu.SemaphoreType.DMA(()),
+            pltpu.SemaphoreType.DMA((8,)),
         ],
         compiler_params=compiler_params(),
         name="serve_rows",
@@ -312,12 +336,17 @@
 
 def rest_kernel(
     pack, edges, address_ref, slot_ref, packed_ref, query_ref,
-    positive_ref, negative_ref, shared_ref, rests_ref, rows_ref,
+    positive_ref, negative_ref, high_ref, low_ref, high_columns_ref, low_columns_ref, square_ref,
+    shared_ref, rests_ref, rows_ref,
 ):
     expand_rests(pack, packed_ref, shared_ref, rests_ref)
     copy_rows(pack, edges, address_ref, slot_ref, packed_ref, rests_ref, rows_ref)
     for c in range(pack.groups):
         negative_ref[:, c * LANES : (c + 1) * LANES] = rows_ref[edges:, c, :]
+    negatives = negative_ref[...]
+    high_ref[...], low_ref[...] = split(negatives)
+    high_columns_ref[...], low_columns_ref[...] = split(negatives.T[: pack.width])
+    square_ref[...] = jnp.sum(negatives * negatives, axis=1, keepdims=True)
     residue = query_ref[...] - row_columns(pack, rows_ref[:edges])
     distance = jnp.sqrt(jnp.sum(residue * residue, axis=0, keepdims=True) + EPSILON)
     positive_ref[...] = jax.nn.sigmoid(distance - MARGIN) / distance * residue
@@ -331,9 +360,14 @@
         out_shape=(
             shape((pack.width, edges), jnp.float32),
             shape((negatives, pack.wide), jnp.float32),
+            shape((negatives, pack.wide), jnp.bfloat16),
+            shape((negatives, pack.wide), jnp.bfloat16),
+            shape((pack.width, negatives), jnp.bfloat16),
+            shape((pack.width, negatives), jnp.bfloat16),
+            shape((negatives, 1), jnp.float32),
         ),
         in_specs=[smem(), smem(), vmem(), vmem()],
-        out_specs=(vmem(), vmem()),
+        out_specs=(vmem(),) * 7,
         scratch_shapes=rests_scratch(pack)
         + [pltpu.VMEM((edges + negatives, pack.groups, LANES), jnp.float32)],
         compiler_params=compiler_params(),
@@ -349,41 +383,42 @@
 
 
 def negatives_kernel(pack, blocks, weight, *refs):
-    negative_ref = refs[0]
-    query_refs = refs[1 : 1 + blocks]
-    coefficient_ref, *part_refs = refs[1 + blocks :]
-    negatives = negative_ref[...]
+    half_refs = refs[:2]
+    column_refs = refs[2:4]
+    square_ref = refs[4]
+    query_refs = refs[5 : 5 + blocks]
+    coefficient_ref, *part_refs = refs[5 + blocks :]
     queries = gather_queries(pack, query_refs)
     query_sq = jnp.sum(queries * queries, axis=0, keepdims=True)
-    block_sq = jnp.sum(negatives * negatives, axis=1, keepdims=True)
-    inner = jnp.dot(negatives, queries, precision=HIGHEST, preferred_element_type=jnp.float32)
-    distance = jnp.sqrt(query_sq + block_sq - 2.0 * inner + EPSILON)
+    inner = dot_halves([ref[...] for ref in half_refs], split(queries), ((1,), (0,)))
+    squared = jnp.maximum(query_sq + square_ref[...] - 2.0 * inner + EPSILON, EPSILON)
+    distance = jnp.sqrt(squared)
     coefficient = -1.0 / ((1.0 + jnp.exp(distance - MARGIN)) * (weight * distance))
     coefficient_ref[...] = coefficient
-    part = queries * jnp.sum(coefficient, axis=0, keepdims=True) - dot_halves(
-        split(negatives.T), split(coefficient), ((1,), (0,))
+    part = queries[: pack.width] * jnp.sum(coefficient, axis=0, keepdims=True) - dot_halves(
+        [ref[...] for ref in column_refs], split(coefficient), ((1,), (0,))
     )
     width = query_refs[0].shape[1]
     for index, ref in enumerate(part_refs):
-        ref[...] = part[: pack.width, index * width : (index + 1) * width]
-
-
-def negative_terms(pack, weight, negatives, queries):
+        ref[...] = part[:, index * width : (index + 1) * width]
+
+
+def negative_terms(pack, weight, negative_parts, queries):
     shape = jax.ShapeDtypeStruct
     count = sum(q.shape[1] for q in queries)
-    rows = negatives.shape[0]
+    rows = negative_parts[0].shape[0]
     return pl.pallas_call(
         functools.partial(negatives_kernel, pack, len(queries), weight),
         out_shape=(shape((rows, count), jnp.float32),)
         + tuple(shape(q.shape, jnp.float32) for q in queries),
-        in_specs=[vmem()] * (1 + len(queries)),
+        in_specs=[vmem()] * (len(negative_parts) + len(queries)),
         out_specs=(vmem(),) * (1 + len(queries)),
         compiler_params=compiler_params(),
         cost_estimate=pl.CostEstimate(
-            flops=18 * rows * count * pack.wide, bytes_accessed=4 * 10**6, transcendentals=0
+            flops=12 * rows * count * pack.wide, bytes_accessed=4 * 10**6, transcendentals=0
         ),
         name="negative_terms",
-    )(negatives, *queries)
+    )(*negative_parts, *queries)
 
 
 def store_rows(pack, first_request, address_ref, slot_ref, rows_ref, out_ref, rests_ref):
@@ -445,29 +480,17 @@
 
 
 def finish_kernel(pack, parts, address_ref, slot_ref, *refs):
-    partial_ref, partial_rests_ref, positive_ref = refs[:3]
+    positive_ref = refs[2]
     part_refs = refs[3 : 3 + parts]
     out_hbm, out_ref, rests_ref, rows_ref, sems = refs[3 + parts :]
     copies, each = sends(pack, out_ref, out_hbm, sems)
-    out_ref[...] = partial_ref[...]
-    rests_ref[...] = partial_rests_ref[...]
     total = positive_ref[...]
     for ref in part_refs:
         total = total + ref[...]
     store_columns(pack, total, rows_ref)
     store_rows(pack, 0, address_ref, slot_ref, rows_ref, out_ref, rests_ref)
-    count = each * pack.shared
     for index, copy in enumerate(copies):
-        first = index * each * pack.capacity
-        shared = rests_ref[pl.ds(first, count, stride=SUBLANES), :]
-        for j in range(1, SUBLANES):
-            block = rests_ref[pl.ds(first + j, count, stride=SUBLANES), :]
-            shared = shared + pltpu.roll(block, j * pack.rest, axis=1)
-        for owner in range(each):
-            start = (index * each + owner) * pack.stride + pack.rests_at
-            out_ref[pl.ds(start, pack.shared), :] = shared[
-                owner * pack.shared : (owner + 1) * pack.shared
-            ]
+        share_rests(pack, rests_ref, out_ref, index * each, each)
         copy.start()
     for copy in copies:
         copy.wait()
@@ -475,41 +498,54 @@
 
 def finish_gradients(pack, address, slot, partial, partial_rests, positive, parts):
     edges = positive.shape[1]
+    shape = jax.ShapeDtypeStruct
     return pl.pallas_call(
         functools.partial(finish_kernel, pack, len(parts)),
-        out_shape=pltpu.HBM((pack.rows, LANES), jnp.float32),
+        out_shape=(
+            pltpu.HBM((pack.rows, LANES), jnp.float32),
+            shape(partial.shape, jnp.float32),
+            shape(partial_rests.shape, jnp.float32),
+        ),
         in_specs=[smem()] * 2 + [vmem()] * (3 + len(parts)),
-        out_specs=hbm(),
+        out_specs=(hbm(), vmem(), vmem()),
+        input_output_aliases={2: 1, 3: 2},
         scratch_shapes=[
-            pltpu.VMEM((pack.rows, LANES), jnp.float32),
-            pltpu.VMEM((pack.slots, LANES), jnp.float32),
             pltpu.VMEM((edges, pack.groups, LANES), jnp.float32),
             pltpu.SemaphoreType.DMA((8,)),
         ],
         compiler_params=compiler_params(),
         name="finish_gradients",
-    )(address, slot, partial, partial_rests, positive, *parts)
+    )(address, slot, partial, partial_rests, positive, *parts)[0]
 
 
 def update_kernel(
-    pack, columns, asked_ref, packed_ref, sum_ref, table_ref,
-    new_table_hbm, new_sum_ref, shared_ref, rests_ref, rows_ref, halves_ref, out_ref, sems,
+    pack, columns, asked_ref, packed_hbm, sum_ref, table_ref, new_table_hbm, new_sum_ref,
+    packed_ref, shared_ref, rests_ref, rows_ref, halves_ref, out_ref, sems, packed_sems,
 ):
-    expand_rests(pack, packed_ref, shared_ref, rests_ref)
-
-    def body(owner):
-        rows = pl.ds(pl.multiple_of(owner * pack.capacity, SUBLANES), pack.capacity)
-        for c in range(pack.full):
-            rows_ref[rows, c * LANES : (c + 1) * LANES] = packed_ref[
-                pl.ds(owner * pack.stride + c, pack.capacity, stride=pack.full), :
-            ]
-        rows_ref[rows, pack.full * LANES :] = rests_ref[rows, :]
-
-    loop(pack.owners, body)
+    pieces = packed_sems.shape[0]
+    owners = pack.owners // pieces
+    loads = []
+    for index in range(pieces):
+        at = pl.ds(index * owners * pack.stride, owners * pack.stride)
+        loads.append(
+            pltpu.make_async_copy(packed_hbm.at[at, :], packed_ref.at[at, :], packed_sems.at[index])
+        )
+        loads[-1].start()
     width = pack.width
-    high, low = split(rows_ref[...].T)
-    halves_ref[:width] = high[:width]
-    halves_ref[width:] = low[:width]
+    for index, load in enumerate(loads):
+        load.wait()
+        expand_rests(pack, packed_ref, shared_ref, rests_ref, index * owners, owners)
+        for owner in range(index * owners, (index + 1) * owners):
+            rows = slice(owner * pack.capacity, (owner + 1) * pack.capacity)
+            for c in range(pack.full):
+                rows_ref[rows, c * LANES : (c + 1) * LANES] = packed_ref[
+                    pl.ds(owner * pack.stride + c, pack.capacity, stride=pack.full), :
+                ]
+            rows_ref[rows, pack.full * LANES :] = rests_ref[rows, :]
+        slots = slice(index * owners * pack.capacity, (index + 1) * owners * pack.capacity)
+        high, low = split(rows_ref[slots, :].T)
+        halves_ref[:width, slots] = high[:width]
+        halves_ref[width:, slots] = low[:width]
     asked = asked_ref[...]
     row = lax.broadcasted_iota(jnp.int32, (columns, pack.slots), 0)
     copies = []
@@ -538,18 +574,20 @@
     return pl.pallas_call(
         functools.partial(update_kernel, pack, columns),
         out_shape=(pltpu.HBM((width, rows), jnp.float32), shape((1, rows), jnp.float32)),
-        in_specs=[vmem()] * 4,
+        in_specs=[vmem(), hbm(), vmem(), vmem()],
         out_specs=(hbm(), vmem()),
-        scratch_shapes=rests_scratch(pack)
+        scratch_shapes=[pltpu.VMEM((pack.rows, LANES), jnp.float32)]
+        + rests_scratch(pack)
         + [
             pltpu.VMEM((pack.slots, pack.wide), jnp.float32),
             pltpu.VMEM((2 * width, pack.slots), jnp.bfloat16),
             pltpu.VMEM((width, rows), jnp.float32),
             pltpu.SemaphoreType.DMA((rows // columns,)),
+            pltpu.SemaphoreType.DMA((4,)),
         ],
         compiler_params=compiler_params(),
         name="update_table",
-    )(asked, packed, adagrad_sum, table_columns)
+    )(asked, in_hbm(packed), adagrad_sum, table_columns)
 
 
 def exchange(payload):
@@ -590,20 +628,19 @@
     weight = float(blk_count * neg_count)
     arriving = [to_chip(queries, blk_count, hops) for hops in range(1, chip_count)]
     nearby = [queries, to_sibling(queries, blk_count)]
-    positive, negatives = unpack_rest(pack, neg_count, address, slot_of, fetched, queries)
-    near, *near_parts = negative_terms(pack, weight, negatives, nearby)
+    positive, negatives, *negative_parts = unpack_rest(pack, neg_count, address, slot_of, fetched, queries)
+    near, *near_parts = negative_terms(pack, weight, negative_parts, nearby)
     arriving, near, near_parts = lax.optimization_barrier((arriving, near, near_parts))
     distant = []
     for same in arriving:
         distant += [same, to_sibling(same, blk_count)]
-    far, *far_parts = negative_terms(pack, weight, negatives, distant)
-    group = nearby + distant
+    far, *far_parts = negative_terms(pack, weight, negative_parts, distant)
     totals = [near_parts[0], to_sibling(near_parts[1], blk_count)]
     for hops in range(1, chip_count):
         total = far_parts[2 * hops - 2] + to_sibling(far_parts[2 * hops - 1], blk_count)
         totals.append(to_chip(total, blk_count, chip_count - hops))
     partial, partial_rests = block_gradients(
-        pack, address, slot_of, positive, negatives, group, (near, far)
+        pack, address, slot_of, positive, negatives, nearby + distant, (near, far)
     )
     outgoing = finish_gradients(
         pack, address, slot_of, partial, partial_rests, positive, totals

time: 185 us -> 182 us (0.984)
  Pallas kernels: 40.1 us -> 37.2 us
where the time goes in v4:
time: 182 us
  waiting for transfers between devices  99.2 us (55%)
  Pallas kernels  37.2 us (20%)
  local copies, waits for them, and re-layouts  23 us (13%)
  starting transfers between devices  20.5 us (11%)
    all_to_all x3, waiting for transfers between devices, exchange(): lax.all_to_all(payload, ('dp', 'blk'), split_axis=0, concat_axis=0, tiled...  93.3 us
    all_to_all x3, starting transfers between devices, exchange(): lax.all_to_all(payload, ('dp', 'blk'), split_axis=0, concat_axis=0, tiled...  17.2 us
    unnamed x9, local copies, waits for them, and re-layouts  16.1 us
    pallas_call x1, Pallas kernels, update(): pl.pallas_call(functools.partial(update_kernel, pack, columns), out_shape...  9.41 us
    pallas_call x1, Pallas kernels, serve(): pl.pallas_call(functools.partial(serve_kernel, pack), out_shape=pltpu.HBM...  6.48 us
    gather x2, local copies, waits for them, and re-layouts, on_device(): relations[rel_ids]  6.32 us
    pallas_call x1, Pallas kernels, to_rows(): pl.pallas_call(functools.partial(rows_kernel, pack), out_shape=pltpu.HBM(...  4.33 us
  transfers between devices with their start and end apart: 9, of which 7 were waited for; matrix products, arithmetic and copies ran while one was open for 12% of the time, Pallas kernels for 7%

profile of v4, /device:TPU:0, one launch (start us, length us, event | category | flops | bytes accessed | tf_op | source)
XLA Modules:
  0.0 181.6 jit_solution(16968510231456118911)
XLA Ops:
  0.6 2.7 %build_requests.1 = (s32[32,1,48]{2,1,0:T(1,128)}, s32[1,768]{1,0:T(1,128)S(1)}, s32[1,768]{1,0:T(1,128)S(1)}) custom-call(s32[512,128]{1,0:T(8,128)} %bitcast.21, s32[1,128]{1,0:T(1,128)} %bitcast.23, s32[1,128]{1,0:T(1,128)} %bitcast.24, s32[1,512]{1,0:T(1,128)} %bitcast.22), custom_call_target="tpu_custom_call" | custom-call | tf_op jit(solution)/shard_map/build_requests/pallas_call | solution.py:163
  3.4 7.3 %all-to-all-start = ((s32[32,1,48]{2,1,0:T(1,128)}), s32[32,1,48]{2,1,0:T(1,128)S(1)}, u32[]{:S(2)}, u32[]{:S(2)}) async-start(s32[32,1,48]{2,1,0:T(1,128)} %get-tuple-element.27), calls=%async_computation | async-start | bytes 32768 | tf_op jit(solution)/shard_map/all_to_all | solution.py:594
  10.7 1.9 %copy-done = f32[2048,400]{0,1:T(8,128)S(1)} copy-done((f32[2048,400]{0,1:T(8,128)S(1)}, f32[2048,400]{0,1:T(8,128)}, u32[]{:S(2)}) %copy-start) | copy-done | bytes 3276824
  12.6 4.3 %table_rows.1.table_hbm = f32[2056,4,128]{2,1,0:T(4,128)} custom-call(f32[400,2048]{1,0:T(8,128)S(1)} %bitcast.15), custom_call_target="tpu_custom_call" | custom-call | tf_op jit(solution)/shard_map/table_rows/pallas_call | solution.py:201
  17.7 6.5 %serve_rows.1 = f32[4864,128]{1,0:T(8,128)} custom-call(s32[32,1,48]{2,1,0:T(1,128)S(1)} %all-to-all-done.asked_ref, f32[2056,4,128]{2,1,0:T(4,128)} %table_rows.1.table_hbm), custom_call_target="tpu_custom_call" | custom-call | tf_op jit(solution)/shard_map/serve_rows/pallas_call | solution.py:278
  24.2 5.2 %all-to-all-start.1 = ((f32[32,152,128]{2,1,0:T(8,128)}), f32[32,152,128]{2,1,0:T(8,128)S(1)}, u32[]{:S(2)}, u32[]{:S(2)}) async-start(f32[32,152,128]{2,1,0:T(8,128)} %bitcast.19), calls=%async_computation.1 | async-start | bytes 4980736 | tf_op jit(solution)/shard_map/all_to_all | solution.py:594
  29.5 14.1 %copy.12 = f32[7424,400]{1,0:T(8,128)} copy(f32[7424,400]{0,1:T(8,128)} %param.10) | data formatting | bytes 23756800 | tf_op args[2]
  43.6 6.2 %gather_fusion = f32[128,400]{1,0:T(8,128)S(1)} fusion(f32[7424,400]{1,0:T(8,128)} %copy.12, s32[1024]{0:T(1024)S(1)} %pad_clamp_fusion), kind=kCustom, calls=%fused_computation | custom fusion | bytes 410112 | tf_op jit(solution)/shard_map/gather | solution.py:627
  49.9 36.7 %all-to-all-done.1 = f32[32,152,128]{2,1,0:T(8,128)S(1)} async-done(((f32[32,152,128]{2,1,0:T(8,128)}), f32[32,152,128]{2,1,0:T(8,128)S(1)}, u32[]{:S(2)}, u32[]{:S(2)}) %all-to-all-start.1) | async-done | bytes 2490400 | tf_op jit(solution)/shard_map/all_to_all | solution.py:594
  86.6 1.3 unpack_heads.1.query_ref.refs_5_.refs_2_
  88.0 1.4 collective-permute-start.1
  89.4 3.1 %unpack_rest.1 = (f32[400,128]{1,0:T(8,128)S(1)}, f32[512,512]{1,0:T(8,128)S(1)}, bf16[512,512]{1,0:T(8,128)(2,1)S(1)}, bf16[512,512]{1,0:T(8,128)(2,1)S(1)}, bf...) custom-call(s32[1,768]{1,0:T(1,128)S(1)} %get-tuple-element.28.address_ref, ...), custom_call_target="tpu_custom_call" | custom-call | flops 10000000 | bytes 9000000 | tf_op jit(solution)/shard_map/unpack_rest/pallas_call | solution.py:358
  92.5 1.8 negative_terms.2
  94.3 1.2 collective-permute-done.1.refs_5_.refs_4_
  95.5 1.5 collective-permute-done.2.refs_6_.refs_5_
  97.0 1.8 negative_terms.3
  99.4 0.9 collective-permute-done.4
  100.3 1.4 collective-permute-start.5
  101.7 3.5 %block_gradients.1 = (f32[4864,128]{1,0:T(8,128)S(1)}, f32[1536,128]{1,0:T(8,128)S(1)}) custom-call(s32[1,768]{1,0:T(1,128)S(1)} %get-tuple-element.28.address_ref, s32[1,768]{1,0:T(1,128)S(1)} %get-tuple-element.29.slot_ref, f32[400,128]{1,0:T(8,128)S(1)} %get-tuple-element.30.refs_0_.refs_2_, f32[512,512]{1,0:T(8,128)S(1)} %get-tuple-element.31.refs_1_, ...), custom_call_target="tpu_custom_call" | custom-call | flops 805306368 | bytes 10000000 | tf_op jit(solution)/shard_map/block_gradients/pallas_call | solution.py:465
  105.2 2.3 %collective-permute-done.5.refs_5_ = f32[400,128]{1,0:T(8,128)S(1)} collective-permute-done((f32[400,128]{1,0:T(8,128)S(1)}, f32[400,128]{1,0:T(8,128)S(1)}, u32[]{:S(2)}, u32[]{:S(2)}) %collective-permute-start.5) | collective-permute-done | bytes 204832 | tf_op jit(solution)/shard_map/ppermute | solution.py:602
  107.5 2.7 %finish_gradients.1 = (f32[4864,128]{1,0:T(8,128)}, f32[4864,128]{1,0:T(8,128)S(1)}, f32[1536,128]{1,0:T(8,128)S(1)}) custom-call(s32[1,768]{1,0:T(1,128)S(1)} %get-tuple-element.28.address_ref, s32[1,768]{1,0:T(1,128)S(1)} %get-tuple-element.29.slot_ref, f32[4864,128]{1,0:T(8,128)S(1)} %get-tuple-element.43.refs_0_, ...), custom_call_target="tpu_custom_call", output_to_operand_aliasing={{1}: (2, {}), {2}: (3, {})} | custom-call | tf_op jit(solution)/shard_map/finish_gradients/pallas_call | solution.py:502
  110.3 4.6 %all-to-all-start.2 = ((f32[32,152,128]{2,1,0:T(8,128)}), f32[32,152,128]{2,1,0:T(8,128)}, u32[]{:S(2)}, u32[]{:S(2)}) async-start(f32[32,152,128]{2,1,0:T(8,128)} %bitcast.20), calls=%async_computation.2 | async-start | bytes 4980736 | tf_op jit(solution)/shard_map/all_to_all | solution.py:594
  116.2 55.8 %all-to-all-done.2 = f32[32,152,128]{2,1,0:T(8,128)} async-done(((f32[32,152,128]{2,1,0:T(8,128)}), f32[32,152,128]{2,1,0:T(8,128)}, u32[]{:S(2)}, u32[]{:S(2)}) %all-to-all-start.2) | async-done | bytes 2490400 | tf_op jit(solution)/shard_map/all_to_all | solution.py:594
  172.0 9.4 %update_table.1 = (f32[400,2048]{1,0:T(8,128)}, f32[1,2048]{1,0:T(1,128)}) custom-call(s32[1,1536]{1,0:T(1,128)S(1)} %reshape.41.asked_ref, f32[4864,128]{1,0:T(8,128)} %bitcast.9.packed_hbm, f32[1,2048]{1,0:T(1,128)S(1)} %bitcast.18, f32[400,2048]{1,0:T(8,128)S(1)} %bitcast.16), custom_call_target="tpu_custom_call" | custom-call | tf_op jit(solution)/shard_map/update_table/pallas_call | solution.py:574
  (21 shorter events, 2.9 us)
Async XLA Ops:
  3.4 14.4 %all-to-all-start = ((s32[32,1,48]{2,1,0:T(1,128)}), s32[32,1,48]{2,1,0:T(1,128)S(1)}, u32[]{:S(2)}, u32[]{:S(2)}) async-start(s32[32,1,48]{2,1,0:T(1,128)} %get-tuple-element.27), calls=%async_computation | async-start | bytes 32768 | tf_op jit(solution)/shard_map/all_to_all | solution.py:594
  10.7 1.9 %copy-start = (f32[2048,400]{0,1:T(8,128)S(1)}, f32[2048,400]{0,1:T(8,128)}, u32[]{:S(2)}) copy-start(f32[2048,400]{0,1:T(8,128)} %param.8) | copy-start | bytes 9830404
  24.2 62.4 %all-to-all-start.1 = ((f32[32,152,128]{2,1,0:T(8,128)}), f32[32,152,128]{2,1,0:T(8,128)S(1)}, u32[]{:S(2)}, u32[]{:S(2)}) async-start(f32[32,152,128]{2,1,0:T(8,128)} %bitcast.19), calls=%async_computation.1 | async-start | bytes 4980736 | tf_op jit(solution)/shard_map/all_to_all | solution.py:594
  29.5 14.1 %copy-start.3 = (s32[128]{0:T(128)S(1)}, s32[128]{0:T(128)}, u32[]{:S(2)}) copy-start(s32[128]{0:T(128)} %param.13) | copy-start | bytes 1540
  87.9 4.5 %collective-permute-start = (f32[400,128]{1,0:T(8,128)S(1)}, f32[400,128]{1,0:T(8,128)S(1)}, u32[]{:S(2)}, u32[]{:S(2)}) collective-permute-start(f32[400,128]{1,0:T(8,128)S(1)} %unpack_heads.1.query_ref.refs_5_.refs_2_), channel_id=1, source_target_pairs={{0,1},{1,0},{2,3},{3,2},{4,5},{5,4},{6,7},{7,6},{8,9},{9,8},{10,11... | collective-permute-start | bytes 614408 | tf_op jit(solution)/shard_map/ppermute | solution.py:598
  88.0 7.5 %collective-permute-start.1 = (f32[400,128]{1,0:T(8,128)S(1)}, f32[400,128]{1,0:T(8,128)S(1)}, u32[]{:S(2)}, u32[]{:S(2)}) collective-permute-start(f32[400,128]{1,0:T(8,128)S(1)} %unpack_heads.1.query_ref.refs_5_.refs_2_), channel_id=1, source_target_pairs={{0,2},{1,3},{2,0},{3,1},{4,6},{5,7},{6,4},{7,5},{8,10},{9,11},{10,... | collective-permute-start | bytes 614408 | tf_op jit(solution)/shard_map/ppermute | solution.py:602
  95.5 1.5 collective-permute-start.2
  98.8 1.5 collective-permute-start.4
  99.0 6.2 %collective-permute-start.3 = (f32[400,128]{1,0:T(8,128)S(1)}, f32[400,128]{1,0:T(8,128)S(1)}, u32[]{:S(2)}, u32[]{:S(2)}) collective-permute-start(f32[400,128]{1,0:T(8,128)S(1)} %get-tuple-element.46), channel_id=1, source_target_pairs={{0,1},{1,0},{2,3},{3,2},{4,5},{5,4},{6,7},{7,6},{8,9},{9,8},{10,11... | collective-permute-start | bytes 614408 | tf_op jit(solution)/shard_map/ppermute | solution.py:598
  100.3 7.2 %collective-permute-start.5 = (f32[400,128]{1,0:T(8,128)S(1)}, f32[400,128]{1,0:T(8,128)S(1)}, u32[]{:S(2)}, u32[]{:S(2)}) collective-permute-start(f32[400,128]{1,0:T(8,128)S(1)} %add.11), channel_id=1, source_target_pairs={{0,2},{1,3},{2,0},{3,1},{4,6},{5,7},{6,4},{7,5},{8,10},{9,11},{10,... | collective-permute-start | bytes 614408 | tf_op jit(solution)/shard_map/ppermute | solution.py:602
  110.2 61.8 %copy-start.1 = (f32[2048,400]{0,1:T(8,128)S(1)}, f32[2048,400]{0,1:T(8,128)}, u32[]{:S(2)}) copy-start(f32[2048,400]{0,1:T(8,128)} %param.8) | copy-start | bytes 9830404
  110.2 61.8 %copy-start.2 = (f32[2048]{0:T(1024)S(1)}, f32[2048]{0:T(1024)}, u32[]{:S(2)}) copy-start(f32[2048]{0:T(1024)} %param.9) | copy-start | bytes 24580
  110.3 61.8 %all-to-all-start.2 = ((f32[32,152,128]{2,1,0:T(8,128)}), f32[32,152,128]{2,1,0:T(8,128)}, u32[]{:S(2)}, u32[]{:S(2)}) async-start(f32[32,152,128]{2,1,0:T(8,128)} %bitcast.20), calls=%async_computation.2 | async-start | bytes 4980736 | tf_op jit(solution)/shard_map/all_to_all | solution.py:594

commit v5 on v4

--- a/solution.py
+++ b/solution.py
@@ -27,7 +27,7 @@
         self.groups = self.full + 1
         self.wide = self.groups * LANES
         self.rests_at = self.full * capacity
-        self.stride = -(-(self.rests_at + self.shared) // SUBLANES) * SUBLANES
+        self.stride = self.rests_at + self.shared
         self.slots = owners * capacity
         self.rows = owners * self.stride
 
@@ -182,31 +182,38 @@
     )
 
 
-def rows_kernel(pack, columns_ref, rows_hbm, rows_ref, sem):
+def rows_kernel(pack, columns_ref, rows_ref, line_ref):
     count = columns_ref.shape[1]
     fill = jnp.zeros((pack.wide - pack.width, LANES), jnp.float32)
+    place = lax.broadcasted_iota(jnp.int32, (LANES // SUBLANES, LANES), 1) // pack.rest
     for block in range(count // LANES):
         at = slice(block * LANES, (block + 1) * LANES)
         tile = jnp.concatenate([columns_ref[:, at], fill], axis=0)
-        for c in range(pack.groups):
-            rows_ref[at, c, :] = tile[c * LANES : (c + 1) * LANES].T
-    rows_ref[count:] = jnp.zeros((SUBLANES, pack.groups, LANES), jnp.float32)
-    copy = pltpu.make_async_copy(rows_ref, rows_hbm, sem)
-    copy.start()
-    copy.wait()
+        for c in range(pack.full):
+            rows_ref[pl.ds(block * LANES * pack.full + c, LANES, stride=pack.full), :] = tile[
+                c * LANES : (c + 1) * LANES
+            ].T
+        line_ref[...] = tile[pack.full * LANES :].T
+        shared = line_ref[pl.ds(0, LANES // SUBLANES, stride=SUBLANES), :]
+        for j in range(1, SUBLANES):
+            rest = line_ref[pl.ds(j, LANES // SUBLANES, stride=SUBLANES), :]
+            shared = jnp.where(place == j, pltpu.roll(rest, j * pack.rest, axis=1), shared)
+        first = pack.full * (count + SUBLANES) + block * (LANES // SUBLANES)
+        rows_ref[first : first + LANES // SUBLANES, :] = shared
+    zeros = jnp.zeros((pack.full * SUBLANES, LANES), jnp.float32)
+    rows_ref[pack.full * count : pack.full * (count + SUBLANES), :] = zeros
+    rows_ref[pack.full * (count + SUBLANES) + count // SUBLANES :, :] = zeros[:SUBLANES]
 
 
 def to_rows(pack, columns):
     count = columns.shape[1]
+    lines = pack.full * (count + SUBLANES) + count // SUBLANES + SUBLANES
     return pl.pallas_call(
         functools.partial(rows_kernel, pack),
-        out_shape=pltpu.HBM((count + SUBLANES, pack.groups, LANES), jnp.float32),
+        out_shape=pltpu.VMEM((lines, LANES), jnp.float32),
         in_specs=[vmem()],
-        out_specs=hbm(),
-        scratch_shapes=[
-            pltpu.VMEM((count + SUBLANES, pack.groups, LANES), jnp.float32),
-            pltpu.SemaphoreType.DMA(()),
-        ],
+        out_specs=vmem(),
+        scratch_shapes=[pltpu.VMEM((LANES, LANES), jnp.float32)],
         compiler_params=compiler_params(),
         name="table_rows",
     )(columns)
@@ -238,33 +245,24 @@
 
 
 def serve_kernel(
-    pack, asked_ref, table_hbm, out_hbm, table_ref, out_ref, rests_ref, sems, table_sems
+    pack, rows_here, asked_ref, table_ref, out_hbm, out_ref, rests_ref, table_rests_ref, sems
 ):
-    pieces = table_sems.shape[0]
-    rows = table_ref.shape[0] // pieces
-    loads = []
-    for index in range(pieces):
-        at = pl.ds(index * rows, rows)
-        loads.append(
-            pltpu.make_async_copy(table_hbm.at[at], table_ref.at[at], table_sems.at[index])
-        )
-        loads[-1].start()
-    for load in loads:
-        load.wait()
     copies, each = sends(pack, out_ref, out_hbm, sems)
+    shared = table_ref[pack.full * (rows_here + SUBLANES) :, :]
+    for j in range(SUBLANES):
+        moved = shared if j == 0 else pltpu.roll(shared, LANES - j * pack.rest, axis=1)
+        table_rests_ref[pl.ds(j, shared.shape[0], stride=SUBLANES), :] = moved
 
     def body(owner):
-        base = pl.multiple_of(owner * pack.stride, SUBLANES)
+        base = owner * pack.stride
         slots = pl.multiple_of(owner * pack.capacity, SUBLANES)
         for first in range(0, pack.capacity, SUBLANES):
-            values = [table_ref[asked_ref[owner, 0, first + j]] for j in range(SUBLANES)]
-            rests_ref[pl.ds(slots + first, SUBLANES), :] = jnp.concatenate(
-                [value[pack.full :] for value in values], axis=0
-            )
+            rows = [asked_ref[owner, 0, first + j] for j in range(SUBLANES)]
+            values = [table_ref[pl.ds(row * pack.full, pack.full), :] for row in rows]
+            rests = [table_rests_ref[pl.ds(row, 1), :] for row in rows]
             for j in range(SUBLANES):
-                out_ref[pl.ds(base + (first + j) * pack.full, pack.full), :] = values[j][
-                    : pack.full
-                ]
+                out_ref[pl.ds(base + (first + j) * pack.full, pack.full), :] = values[j]
+            rests_ref[pl.ds(slots + first, SUBLANES), :] = jnp.concatenate(rests, axis=0)
 
     for index, copy in enumerate(copies):
         loop(each, lambda owner: body(index * each + owner))
@@ -274,22 +272,21 @@
         copy.wait()
 
 
-def serve(pack, asked, table_rows):
-    return pl.pallas_call(
-        functools.partial(serve_kernel, pack),
+def serve(pack, rows_here, asked, table_rows):
+    return pl.pallas_call(
+        functools.partial(serve_kernel, pack, rows_here),
         out_shape=pltpu.HBM((pack.rows, LANES), jnp.float32),
-        in_specs=[smem(), hbm()],
+        in_specs=[smem(), vmem()],
         out_specs=hbm(),
         scratch_shapes=[
-            pltpu.VMEM(table_rows.shape, jnp.float32),
             pltpu.VMEM((pack.rows, LANES), jnp.float32),
             pltpu.VMEM((pack.slots, LANES), jnp.float32),
-            pltpu.SemaphoreType.DMA((8,)),
-            pltpu.SemaphoreType.DMA((8,)),
+            pltpu.VMEM((rows_here + SUBLANES * SUBLANES, LANES), jnp.float32),
+            pltpu.SemaphoreType.DMA((4,)),
         ],
         compiler_params=compiler_params(),
         name="serve_rows",
-    )(asked, in_hbm(table_rows))
+    )(asked, pltpu.with_memory_space_constraint(table_rows, pltpu.VMEM))
 
 
 def copy_rows(pack, first_request, address_ref, slot_ref, packed_ref, rests_ref, rows_ref):
@@ -511,7 +508,7 @@
         input_output_aliases={2: 1, 3: 2},
         scratch_shapes=[
             pltpu.VMEM((edges, pack.groups, LANES), jnp.float32),
-            pltpu.SemaphoreType.DMA((8,)),
+            pltpu.SemaphoreType.DMA((4,)),
         ],
         compiler_params=compiler_params(),
         name="finish_gradients",
@@ -583,7 +580,7 @@
             pltpu.VMEM((2 * width, pack.slots), jnp.bfloat16),
             pltpu.VMEM((width, rows), jnp.float32),
             pltpu.SemaphoreType.DMA((rows // columns,)),
-            pltpu.SemaphoreType.DMA((4,)),
+            pltpu.SemaphoreType.DMA((2,)),
         ],
         compiler_params=compiler_params(),
         name="update_table",
@@ -621,8 +618,8 @@
         pack, rows_here, owner_map, head_ids, tail_ids, neg_ids
     )
     asked = exchange(requests)
-    served = serve(pack, asked, to_rows(pack, entity_table.T))
-    fetched = exchange(served.reshape(owner_count, pack.stride, LANES))
+    served = serve(pack, rows_here, asked, to_rows(pack, entity_table.T))
+    fetched = exchange(served.reshape(owner_count, 1, pack.stride * LANES))
     fetched = fetched.reshape(pack.rows, LANES)
     queries = unpack_heads(pack, edge_count, address, slot_of, fetched, relations[rel_ids].T)
     weight = float(blk_count * neg_count)
@@ -645,7 +642,7 @@
     outgoing = finish_gradients(
         pack, address, slot_of, partial, partial_rests, positive, totals
     )
-    incoming = exchange(outgoing.reshape(owner_count, pack.stride, LANES))
+    incoming = exchange(outgoing.reshape(owner_count, 1, pack.stride * LANES))
     new_columns, new_sum = update(
         pack, asked.reshape(1, -1), incoming.reshape(pack.rows, LANES),
         adagrad_sum.reshape(1, -1), entity_table.T,

time: 182 us -> 176 us (0.967)
  Pallas kernels: 37.2 us -> 32.1 us
  starting transfers between devices: 20.5 us -> 17.9 us
    pallas_call x2, Pallas kernels: 10.8 us -> 6.07 us  [the longest x1 4.65 us: serve(): pl.pallas_call(functools.partial(serve_kernel, pack, rows_here), out_shap...]
    all_to_all x3, starting transfers between devices: 17.2 us -> 14.6 us  [exchange(): lax.all_to_all(payload, ('dp', 'blk'), split_axis=0, concat_axis=0, tiled...]
  transfers between devices with their start and end apart: 9 -> 9, of which waited for: 7 -> 7; matrix products, arithmetic and copies ran while one was open for 12% -> 12% of each run, Pallas kernels for 7% -> 6%
where the time goes in v5:
time: 176 us
  waiting for transfers between devices  101 us (57%)
  Pallas kernels  32.1 us (18%)
  local copies, waits for them, and re-layouts  23 us (13%)
  starting transfers between devices  17.9 us (10%)
    all_to_all x3, waiting for transfers between devices, exchange(): lax.all_to_all(payload, ('dp', 'blk'), split_axis=0, concat_axis=0, tiled...  95 us
    unnamed x9, local copies, waits for them, and re-layouts  16.1 us
    all_to_all x3, starting transfers between devices, exchange(): lax.all_to_all(payload, ('dp', 'blk'), split_axis=0, concat_axis=0, tiled...  14.6 us
    pallas_call x1, Pallas kernels, update(): pl.pallas_call(functools.partial(update_kernel, pack, columns), out_shape...  9.16 us
    gather x2, local copies, waits for them, and re-layouts, on_device(): relations[rel_ids]  6.32 us
    pallas_call x1, Pallas kernels, serve(): pl.pallas_call(functools.partial(serve_kernel, pack, rows_here), out_shap...  4.65 us
    pallas_call x2, Pallas kernels, negative_terms(): pl.pallas_call(functools.partial(negatives_kernel, pack, len(queries), we...  3.61 us
    ppermute x2, waiting for transfers between devices, to_chip(): lax.ppermute(value, 'blk', [(i, (i + 2 * hops) % blk_count) for i in rang...  3.59 us
  transfers between devices with their start and end apart: 9, of which 7 were waited for; matrix products, arithmetic and copies ran while one was open for 12% of the time, Pallas kernels for 6%

profile of v5, /device:TPU:0, one launch (start us, length us, event | category | flops | bytes accessed | tf_op | source)
XLA Modules:
  0.0 175.7 jit_solution(8514648598069596653)
XLA Ops:
  0.6 2.7 %build_requests.1 = (s32[32,1,48]{2,1,0:T(1,128)}, s32[1,768]{1,0:T(1,128)S(1)}, s32[1,768]{1,0:T(1,128)S(1)}) custom-call(s32[512,128]{1,0:T(8,128)} %bitcast.21, s32[1,128]{1,0:T(1,128)} %bitcast.23, s32[1,128]{1,0:T(1,128)} %bitcast.24, s32[1,512]{1,0:T(1,128)} %bitcast.22), custom_call_target="tpu_custom_call" | custom-call | tf_op jit(solution)/shard_map/build_requests/pallas_call | solution.py:163
  3.4 7.3 %all-to-all-start = ((s32[32,1,48]{2,1,0:T(1,128)}), s32[32,1,48]{2,1,0:T(1,128)S(1)}, u32[]{:S(2)}, u32[]{:S(2)}) async-start(s32[32,1,48]{2,1,0:T(1,128)} %get-tuple-element.27), calls=%async_computation | async-start | bytes 32768 | tf_op jit(solution)/shard_map/all_to_all | solution.py:591
  10.7 1.9 %copy-done = f32[2048,400]{0,1:T(8,128)S(1)} copy-done((f32[2048,400]{0,1:T(8,128)S(1)}, f32[2048,400]{0,1:T(8,128)}, u32[]{:S(2)}) %copy-start) | copy-done | bytes 3276824
  12.6 1.4 table_rows.1.table_ref
  14.0 3.7 %all-to-all-done.asked_ref = s32[32,1,48]{2,1,0:T(1,128)S(1)} async-done(((s32[32,1,48]{2,1,0:T(1,128)}), s32[32,1,48]{2,1,0:T(1,128)S(1)}, u32[]{:S(2)}, u32[]{:S(2)}) %all-to-all-start) | async-done | bytes 6176 | tf_op jit(solution)/shard_map/all_to_all | solution.py:591
  17.7 4.7 %serve_rows.1 = f32[4800,128]{1,0:T(8,128)} custom-call(s32[32,1,48]{2,1,0:T(1,128)S(1)} %all-to-all-done.asked_ref, f32[6432,128]{1,0:T(8,128)S(1)} %table_rows.1.table_ref), custom_call_target="tpu_custom_call" | custom-call | tf_op jit(solution)/shard_map/serve_rows/pallas_call | solution.py:276
  22.4 2.8 %all-to-all-start.1 = ((f32[32,1,19200]{2,1,0:T(1,128)}), f32[32,1,19200]{2,1,0:T(1,128)S(1)}, u32[]{:S(2)}, u32[]{:S(2)}) async-start(f32[32,1,19200]{2,1,0:T(1,128)} %bitcast.19), calls=%async_computation.1 | async-start | bytes 4915200 | tf_op jit(solution)/shard_map/all_to_all | solution.py:591
  25.2 14.1 %copy.15 = f32[7424,400]{1,0:T(8,128)} copy(f32[7424,400]{0,1:T(8,128)} %param.10) | data formatting | bytes 23756800 | tf_op args[2]
  39.4 6.2 %gather_fusion = f32[128,400]{1,0:T(8,128)S(1)} fusion(f32[7424,400]{1,0:T(8,128)} %copy.15, s32[1024]{0:T(1024)S(1)} %pad_clamp_fusion), kind=kCustom, calls=%fused_computation | custom fusion | bytes 410112 | tf_op jit(solution)/shard_map/gather | solution.py:624
  45.7 36.1 %all-to-all-done.1 = f32[32,1,19200]{2,1,0:T(1,128)S(1)} async-done(((f32[32,1,19200]{2,1,0:T(1,128)}), f32[32,1,19200]{2,1,0:T(1,128)S(1)}, u32[]{:S(2)}, u32[]{:S(2)}) %all-to-all-start.1) | async-done | bytes 2457632 | tf_op jit(solution)/shard_map/all_to_all | solution.py:591
  81.8 1.3 unpack_heads.1.query_ref.refs_5_.refs_2_
  83.2 1.3 collective-permute-start.1
  84.6 3.0 %unpack_rest.1 = (f32[400,128]{1,0:T(8,128)S(1)}, f32[512,512]{1,0:T(8,128)S(1)}, bf16[512,512]{1,0:T(8,128)(2,1)S(1)}, bf16[512,512]{1,0:T(8,128)(2,1)S(1)}, bf...) custom-call(s32[1,768]{1,0:T(1,128)S(1)} %get-tuple-element.28.address_ref, ...), custom_call_target="tpu_custom_call" | custom-call | flops 10000000 | bytes 9000000 | tf_op jit(solution)/shard_map/unpack_rest/pallas_call | solution.py:355
  87.6 1.8 %negative_terms.2 = (f32[512,256]{1,0:T(8,128)S(1)}, f32[400,128]{1,0:T(8,128)S(1)}, f32[400,128]{1,0:T(8,128)S(1)}) custom-call(bf16[512,512]{1,0:T(8,128)(2,1)S(1)} %get-tuple-element.32.refs_0_, bf16[512,512]{1,0:T(8,128)(2,1)S(1)} %get-tuple-element.33.refs_1_, bf16[400,512]{1,0:T(8,128)(2,1)S(1)} %get-tuple-element.34.refs_2_, ...), custom_call_target="tpu_custom_call" | custom-call | flops 805306368 | bytes 4000000 | tf_op jit(solution)/shard_map/negative_terms/pallas_call | solution.py:407
  89.4 1.3 collective-permute-done.1.refs_5_.refs_4_
  90.7 1.5 collective-permute-done.2.refs_6_.refs_5_
  92.2 1.8 %negative_terms.3 = (f32[512,256]{1,0:T(8,128)S(1)}, f32[400,128]{1,0:T(8,128)S(1)}, f32[400,128]{1,0:T(8,128)S(1)}) custom-call(bf16[512,512]{1,0:T(8,128)(2,1)S(1)} %get-tuple-element.32.refs_0_, bf16[512,512]{1,0:T(8,128)(2,1)S(1)} %get-tuple-element.33.refs_1_, bf16[400,512]{1,0:T(8,128)(2,1)S(1)} %get-tuple-element.34.refs_2_, ...), custom_call_target="tpu_custom_call" | custom-call | flops 805306368 | bytes 4000000 | tf_op jit(solution)/shard_map/negative_terms/pallas_call | solution.py:407
  95.5 1.3 collective-permute-start.5
  96.9 3.5 %block_gradients.1 = (f32[4800,128]{1,0:T(8,128)S(1)}, f32[1536,128]{1,0:T(8,128)S(1)}) custom-call(s32[1,768]{1,0:T(1,128)S(1)} %get-tuple-element.28.address_ref, s32[1,768]{1,0:T(1,128)S(1)} %get-tuple-element.29.slot_ref, f32[400,128]{1,0:T(8,128)S(1)} %get-tuple-element.30.refs_0_.refs_2_, f32[512,512]{1,0:T(8,128)S(1)} %get-tuple-element.31.refs_1_, ...), custom_call_target="tpu_custom_call" | custom-call | flops 805306368 | bytes 10000000 | tf_op jit(solution)/shard_map/block_gradients/pallas_call | solution.py:462
  100.4 2.3 %collective-permute-done.5.refs_5_ = f32[400,128]{1,0:T(8,128)S(1)} collective-permute-done((f32[400,128]{1,0:T(8,128)S(1)}, f32[400,128]{1,0:T(8,128)S(1)}, u32[]{:S(2)}, u32[]{:S(2)}) %collective-permute-start.5) | collective-permute-done | bytes 204832 | tf_op jit(solution)/shard_map/ppermute | solution.py:599
  102.7 2.7 %finish_gradients.1 = (f32[4800,128]{1,0:T(8,128)}, f32[4800,128]{1,0:T(8,128)S(1)}, f32[1536,128]{1,0:T(8,128)S(1)}) custom-call(s32[1,768]{1,0:T(1,128)S(1)} %get-tuple-element.28.address_ref, s32[1,768]{1,0:T(1,128)S(1)} %get-tuple-element.29.slot_ref, f32[4800,128]{1,0:T(8,128)S(1)} %get-tuple-element.43.refs_0_, ...), custom_call_target="tpu_custom_call", output_to_operand_aliasing={{1}: (2, {}), {2}: (3, {})} | custom-call | tf_op jit(solution)/shard_map/finish_gradients/pallas_call | solution.py:499
  105.4 4.5 %all-to-all-start.2 = ((f32[32,1,19200]{2,1,0:T(1,128)}), f32[32,1,19200]{2,1,0:T(1,128)}, u32[]{:S(2)}, u32[]{:S(2)}) async-start(f32[32,1,19200]{2,1,0:T(1,128)} %bitcast.20), calls=%async_computation.2 | async-start | bytes 4915200 | tf_op jit(solution)/shard_map/all_to_all | solution.py:591
  111.2 55.1 %all-to-all-done.2 = f32[32,1,19200]{2,1,0:T(1,128)} async-done(((f32[32,1,19200]{2,1,0:T(1,128)}), f32[32,1,19200]{2,1,0:T(1,128)}, u32[]{:S(2)}, u32[]{:S(2)}) %all-to-all-start.2) | async-done | bytes 2457632 | tf_op jit(solution)/shard_map/all_to_all | solution.py:591
  166.3 9.2 %update_table.1 = (f32[400,2048]{1,0:T(8,128)}, f32[1,2048]{1,0:T(1,128)}) custom-call(s32[1,1536]{1,0:T(1,128)S(1)} %reshape.41.asked_ref, f32[4800,128]{1,0:T(8,128)} %bitcast.9.packed_hbm, f32[1,2048]{1,0:T(1,128)S(1)} %bitcast.18, f32[400,2048]{1,0:T(8,128)S(1)} %bitcast.16), custom_call_target="tpu_custom_call" | custom-call | tf_op jit(solution)/shard_map/update_table/pallas_call | solution.py:571
  (21 shorter events, 3.1 us)
Async XLA Ops:
  3.4 14.4 %all-to-all-start = ((s32[32,1,48]{2,1,0:T(1,128)}), s32[32,1,48]{2,1,0:T(1,128)S(1)}, u32[]{:S(2)}, u32[]{:S(2)}) async-start(s32[32,1,48]{2,1,0:T(1,128)} %get-tuple-element.27), calls=%async_computation | async-start | bytes 32768 | tf_op jit(solution)/shard_map/all_to_all | solution.py:591
  10.7 1.9 %copy-start = (f32[2048,400]{0,1:T(8,128)S(1)}, f32[2048,400]{0,1:T(8,128)}, u32[]{:S(2)}) copy-start(f32[2048,400]{0,1:T(8,128)} %param.8) | copy-start | bytes 9830404
  22.4 59.4 %all-to-all-start.1 = ((f32[32,1,19200]{2,1,0:T(1,128)}), f32[32,1,19200]{2,1,0:T(1,128)S(1)}, u32[]{:S(2)}, u32[]{:S(2)}) async-start(f32[32,1,19200]{2,1,0:T(1,128)} %bitcast.19), calls=%async_computation.1 | async-start | bytes 4915200 | tf_op jit(solution)/shard_map/all_to_all | solution.py:591
  25.2 14.1 %copy-start.3 = (s32[128]{0:T(128)S(1)}, s32[128]{0:T(128)}, u32[]{:S(2)}) copy-start(s32[128]{0:T(128)} %param.13) | copy-start | bytes 1540
  83.1 4.5 %collective-permute-start = (f32[400,128]{1,0:T(8,128)S(1)}, f32[400,128]{1,0:T(8,128)S(1)}, u32[]{:S(2)}, u32[]{:S(2)}) collective-permute-start(f32[400,128]{1,0:T(8,128)S(1)} %unpack_heads.1.query_ref.refs_5_.refs_2_), channel_id=1, source_target_pairs={{0,1},{1,0},{2,3},{3,2},{4,5},{5,4},{6,7},{7,6},{8,9},{9,8},{10,11... | collective-permute-start | bytes 614408 | tf_op jit(solution)/shard_map/ppermute | solution.py:595
  83.2 7.5 %collective-permute-start.1 = (f32[400,128]{1,0:T(8,128)S(1)}, f32[400,128]{1,0:T(8,128)S(1)}, u32[]{:S(2)}, u32[]{:S(2)}) collective-permute-start(f32[400,128]{1,0:T(8,128)S(1)} %unpack_heads.1.query_ref.refs_5_.refs_2_), channel_id=1, source_target_pairs={{0,2},{1,3},{2,0},{3,1},{4,6},{5,7},{6,4},{7,5},{8,10},{9,11},{10,... | collective-permute-start | bytes 614408 | tf_op jit(solution)/shard_map/ppermute | solution.py:599
  90.7 1.5 collective-permute-start.2
  94.0 1.5 collective-permute-start.4
  94.2 6.2 %collective-permute-start.3 = (f32[400,128]{1,0:T(8,128)S(1)}, f32[400,128]{1,0:T(8,128)S(1)}, u32[]{:S(2)}, u32[]{:S(2)}) collective-permute-start(f32[400,128]{1,0:T(8,128)S(1)} %get-tuple-element.46), channel_id=1, source_target_pairs={{0,1},{1,0},{2,3},{3,2},{4,5},{5,4},{6,7},{7,6},{8,9},{9,8},{10,11... | collective-permute-start | bytes 614408 | tf_op jit(solution)/shard_map/ppermute | solution.py:595
  95.5 7.2 %collective-permute-start.5 = (f32[400,128]{1,0:T(8,128)S(1)}, f32[400,128]{1,0:T(8,128)S(1)}, u32[]{:S(2)}, u32[]{:S(2)}) collective-permute-start(f32[400,128]{1,0:T(8,128)S(1)} %add.11), channel_id=1, source_target_pairs={{0,2},{1,3},{2,0},{3,1},{4,6},{5,7},{6,4},{7,5},{8,10},{9,11},{10,... | collective-permute-start | bytes 614408 | tf_op jit(solution)/shard_map/ppermute | solution.py:599
  105.4 60.9 %copy-start.1 = (f32[2048,400]{0,1:T(8,128)S(1)}, f32[2048,400]{0,1:T(8,128)}, u32[]{:S(2)}) copy-start(f32[2048,400]{0,1:T(8,128)} %param.8) | copy-start | bytes 9830404
  105.4 60.9 %copy-start.2 = (f32[2048]{0:T(1024)S(1)}, f32[2048]{0:T(1024)}, u32[]{:S(2)}) copy-start(f32[2048]{0:T(1024)} %param.9) | copy-start | bytes 24580
  105.4 60.9 %all-to-all-start.2 = ((f32[32,1,19200]{2,1,0:T(1,128)}), f32[32,1,19200]{2,1,0:T(1,128)}, u32[]{:S(2)}, u32[]{:S(2)}) async-start(f32[32,1,19200]{2,1,0:T(1,128)} %bitcast.20), calls=%async_computation.2 | async-start | bytes 4915200 | tf_op jit(solution)/shard_map/all_to_all | solution.py:591

commit v6 on v5

--- a/solution.py
+++ b/solution.py
@@ -12,6 +12,7 @@
 LEARNING_RATE = 0.1
 LANES = 128
 SUBLANES = 8
+SCORE_STEPS = 2
 VMEM_BYTES = 24 * 1024 * 1024
 
 
@@ -29,6 +30,7 @@
         self.rests_at = self.full * capacity
         self.stride = self.rests_at + self.shared
         self.slots = owners * capacity
+        self.rest_rows = self.slots + SUBLANES
         self.rows = owners * self.stride
 
 
@@ -93,7 +95,7 @@
 def rests_scratch(pack):
     return [
         pltpu.VMEM((pack.owners * pack.shared, LANES), jnp.float32),
-        pltpu.VMEM((pack.slots, LANES), jnp.float32),
+        pltpu.VMEM((pack.rest_rows, LANES), jnp.float32),
     ]
 
 
@@ -118,7 +120,7 @@
         first += source.shape[1]
     for copy in copies:
         copy.start()
-    for copy in copies:
+    for copy in copies[1:]:
         copy.wait()
     ids = ids_ref[...]
     count = ids.shape[1]
@@ -128,6 +130,8 @@
         return lax.broadcasted_iota(jnp.int32, (rows, count), axis)
 
     line_chosen = one_hot(iota(lines, 0) == ids // LANES)
+    earlier = one_hot(iota(count, 0) < iota(count, 1))
+    copies[0].wait()
     table = map_ref[...].T
     digits = [(table >> shift) & 255 for shift in range(0, 24, 8)]
     stacked = jnp.concatenate(digits, axis=0).astype(jnp.float32).astype(jnp.bfloat16)
@@ -138,7 +142,6 @@
     owner = position // rows_here
     row = position % rows_here
     to_owner = iota(pack.owners, 0) == owner
-    earlier = one_hot(iota(count, 0) < iota(count, 1))
     before = jnp.dot(one_hot(to_owner), earlier, preferred_element_type=jnp.float32)
     rank = jnp.sum(jnp.where(to_owner, before, 0.0), axis=0, keepdims=True).astype(jnp.int32)
     slot_ref[...] = owner * pack.capacity + rank
@@ -193,7 +196,7 @@
             rows_ref[pl.ds(block * LANES * pack.full + c, LANES, stride=pack.full), :] = tile[
                 c * LANES : (c + 1) * LANES
             ].T
-        line_ref[...] = tile[pack.full * LANES :].T
+        line_ref[:LANES, :] = tile[pack.full * LANES :].T
         shared = line_ref[pl.ds(0, LANES // SUBLANES, stride=SUBLANES), :]
         for j in range(1, SUBLANES):
             rest = line_ref[pl.ds(j, LANES // SUBLANES, stride=SUBLANES), :]
@@ -213,7 +216,7 @@
         out_shape=pltpu.VMEM((lines, LANES), jnp.float32),
         in_specs=[vmem()],
         out_specs=vmem(),
-        scratch_shapes=[pltpu.VMEM((LANES, LANES), jnp.float32)],
+        scratch_shapes=[pltpu.VMEM((LANES + SUBLANES, LANES), jnp.float32)],
         compiler_params=compiler_params(),
         name="table_rows",
     )(columns)
@@ -280,8 +283,8 @@
         out_specs=hbm(),
         scratch_shapes=[
             pltpu.VMEM((pack.rows, LANES), jnp.float32),
-            pltpu.VMEM((pack.slots, LANES), jnp.float32),
-            pltpu.VMEM((rows_here + SUBLANES * SUBLANES, LANES), jnp.float32),
+            pltpu.VMEM((pack.rest_rows, LANES), jnp.float32),
+            pltpu.VMEM((rows_here + SUBLANES * (SUBLANES + 1), LANES), jnp.float32),
             pltpu.SemaphoreType.DMA((4,)),
         ],
         compiler_params=compiler_params(),
@@ -387,14 +390,21 @@
     coefficient_ref, *part_refs = refs[5 + blocks :]
     queries = gather_queries(pack, query_refs)
     query_sq = jnp.sum(queries * queries, axis=0, keepdims=True)
-    inner = dot_halves([ref[...] for ref in half_refs], split(queries), ((1,), (0,)))
-    squared = jnp.maximum(query_sq + square_ref[...] - 2.0 * inner + EPSILON, EPSILON)
-    distance = jnp.sqrt(squared)
-    coefficient = -1.0 / ((1.0 + jnp.exp(distance - MARGIN)) * (weight * distance))
-    coefficient_ref[...] = coefficient
-    part = queries[: pack.width] * jnp.sum(coefficient, axis=0, keepdims=True) - dot_halves(
-        [ref[...] for ref in column_refs], split(coefficient), ((1,), (0,))
-    )
+    query_halves = split(queries)
+    count = square_ref.shape[0]
+    weights, parts = [], []
+    for first in range(0, count, count // SCORE_STEPS):
+        rows = slice(first, first + count // SCORE_STEPS)
+        inner = dot_halves([ref[rows, :] for ref in half_refs], query_halves, ((1,), (0,)))
+        squared = jnp.maximum(query_sq + square_ref[rows, :] - 2.0 * inner + EPSILON, EPSILON)
+        distance = jnp.sqrt(squared)
+        coefficient = -1.0 / ((1.0 + jnp.exp(distance - MARGIN)) * (weight * distance))
+        coefficient_ref[rows, :] = coefficient
+        weights.append(jnp.sum(coefficient, axis=0, keepdims=True))
+        parts.append(
+            dot_halves([ref[:, rows] for ref in column_refs], split(coefficient), ((1,), (0,)))
+        )
+    part = queries[: pack.width] * sum(weights) - sum(parts)
     width = query_refs[0].shape[1]
     for index, ref in enumerate(part_refs):
         ref[...] = part[:, index * width : (index + 1) * width]
@@ -463,7 +473,7 @@
         functools.partial(block_kernel, pack, len(queries), len(coefficients)),
         out_shape=(
             shape((pack.rows, LANES), jnp.float32),
-            shape((pack.slots, LANES), jnp.float32),
+            shape((pack.rest_rows, LANES), jnp.float32),
         ),
         in_specs=[smem()] * 2 + [vmem()] * (2 + len(queries) + len(coefficients)),
         out_specs=(vmem(), vmem()),

time: 176 us -> 176 us (level)
  transfers between devices with their start and end apart: 9 -> 9, of which waited for: 7 -> 7; matrix products, arithmetic and copies ran while one was open for 12% -> 12% of each run, Pallas kernels for 6% -> 5%
where the time goes in v6:
time: 176 us; the launch traced here: 175 us
  waiting for transfers between devices  101 us (57%)
  Pallas kernels  31.4 us (18%)
  local copies, waits for them, and re-layouts  23 us (13%)
  starting transfers between devices  17.9 us (10%)
    all_to_all x3, waiting for transfers between devices, exchange(): lax.all_to_all(payload, ('dp', 'blk'), split_axis=0, concat_axis=0, tiled...  95 us
    unnamed x9, local copies, waits for them, and re-layouts  16.1 us
    all_to_all x3, starting transfers between devices, exchange(): lax.all_to_all(payload, ('dp', 'blk'), split_axis=0, concat_axis=0, tiled...  14.6 us
    pallas_call x1, Pallas kernels, update(): pl.pallas_call(functools.partial(update_kernel, pack, columns), out_shape...  9.18 us
    gather x2, local copies, waits for them, and re-layouts, on_device(): relations[rel_ids]  6.32 us
    pallas_call x1, Pallas kernels, serve(): pl.pallas_call(functools.partial(serve_kernel, pack, rows_here), out_shap...  4.65 us
    ppermute x2, waiting for transfers between devices, to_chip(): lax.ppermute(value, 'blk', [(i, (i + 2 * hops) % blk_count) for i in rang...  4.02 us
  transfers between devices with their start and end apart: 9, of which 7 were waited for; matrix products, arithmetic and copies ran while one was open for 12% of the time, Pallas kernels for 5%

profile of v6, /device:TPU:0, one launch (start us, length us, event | category | flops | bytes accessed | tf_op | source)
XLA Modules:
  0.0 175.4 jit_solution(7969955944172289129)
XLA Ops:
  0.6 2.8 %build_requests.1 = (s32[32,1,48]{2,1,0:T(1,128)}, s32[1,768]{1,0:T(1,128)S(1)}, s32[1,768]{1,0:T(1,128)S(1)}) custom-call(s32[512,128]{1,0:T(8,128)} %bitcast.21, s32[1,128]{1,0:T(1,128)} %bitcast.23, s32[1,128]{1,0:T(1,128)} %bitcast.24, s32[1,512]{1,0:T(1,128)} %bitcast.22), custom_call_target="tpu_custom_call" | custom-call | tf_op jit(solution)/shard_map/build_requests/pallas_call | solution.py:166
  3.5 7.3 %all-to-all-start = ((s32[32,1,48]{2,1,0:T(1,128)}), s32[32,1,48]{2,1,0:T(1,128)S(1)}, u32[]{:S(2)}, u32[]{:S(2)}) async-start(s32[32,1,48]{2,1,0:T(1,128)} %get-tuple-element.27), calls=%async_computation | async-start | bytes 32768 | tf_op jit(solution)/shard_map/all_to_all | solution.py:601
  10.8 1.9 %copy-done = f32[2048,400]{0,1:T(8,128)S(1)} copy-done((f32[2048,400]{0,1:T(8,128)S(1)}, f32[2048,400]{0,1:T(8,128)}, u32[]{:S(2)}) %copy-start) | copy-done | bytes 3276824
  12.7 1.4 table_rows.1.table_ref
  14.1 3.7 %all-to-all-done.asked_ref = s32[32,1,48]{2,1,0:T(1,128)S(1)} async-done(((s32[32,1,48]{2,1,0:T(1,128)}), s32[32,1,48]{2,1,0:T(1,128)S(1)}, u32[]{:S(2)}, u32[]{:S(2)}) %all-to-all-start) | async-done | bytes 6176 | tf_op jit(solution)/shard_map/all_to_all | solution.py:601
  17.9 4.7 %serve_rows.1 = f32[4800,128]{1,0:T(8,128)} custom-call(s32[32,1,48]{2,1,0:T(1,128)S(1)} %all-to-all-done.asked_ref, f32[6432,128]{1,0:T(8,128)S(1)} %table_rows.1.table_ref), custom_call_target="tpu_custom_call" | custom-call | tf_op jit(solution)/shard_map/serve_rows/pallas_call | solution.py:279
  22.5 2.8 %all-to-all-start.1 = ((f32[32,1,19200]{2,1,0:T(1,128)}), f32[32,1,19200]{2,1,0:T(1,128)S(1)}, u32[]{:S(2)}, u32[]{:S(2)}) async-start(f32[32,1,19200]{2,1,0:T(1,128)} %bitcast.19), calls=%async_computation.1 | async-start | bytes 4915200 | tf_op jit(solution)/shard_map/all_to_all | solution.py:601
  25.3 14.1 %copy.15 = f32[7424,400]{1,0:T(8,128)} copy(f32[7424,400]{0,1:T(8,128)} %param.10) | data formatting | bytes 23756800 | tf_op args[2]
  39.5 6.2 %gather_fusion = f32[128,400]{1,0:T(8,128)S(1)} fusion(f32[7424,400]{1,0:T(8,128)} %copy.15, s32[1024]{0:T(1024)S(1)} %pad_clamp_fusion), kind=kCustom, calls=%fused_computation | custom fusion | bytes 410112 | tf_op jit(solution)/shard_map/gather | solution.py:634
  45.8 36.1 %all-to-all-done.1 = f32[32,1,19200]{2,1,0:T(1,128)S(1)} async-done(((f32[32,1,19200]{2,1,0:T(1,128)}), f32[32,1,19200]{2,1,0:T(1,128)S(1)}, u32[]{:S(2)}, u32[]{:S(2)}) %all-to-all-start.1) | async-done | bytes 2457632 | tf_op jit(solution)/shard_map/all_to_all | solution.py:601
  81.9 1.3 unpack_heads.1.query_ref.refs_5_.refs_2_
  83.3 1.3 collective-permute-start.1
  84.7 3.0 %unpack_rest.1 = (f32[400,128]{1,0:T(8,128)S(1)}, f32[512,512]{1,0:T(8,128)S(1)}, bf16[512,512]{1,0:T(8,128)(2,1)S(1)}, bf16[512,512]{1,0:T(8,128)(2,1)S(1)}, bf...) custom-call(s32[1,768]{1,0:T(1,128)S(1)} %get-tuple-element.28.address_ref, ...), custom_call_target="tpu_custom_call" | custom-call | flops 10000000 | bytes 9000000 | tf_op jit(solution)/shard_map/unpack_rest/pallas_call | solution.py:358
  87.7 1.4 negative_terms.2
  89.1 1.7 collective-permute-done.1.refs_5_.refs_4_
  90.8 1.5 collective-permute-done.2.refs_6_.refs_5_
  92.3 1.4 negative_terms.3
  95.2 1.3 collective-permute-start.5
  96.6 3.5 %block_gradients.1 = (f32[4800,128]{1,0:T(8,128)S(1)}, f32[1544,128]{1,0:T(8,128)S(1)}) custom-call(s32[1,768]{1,0:T(1,128)S(1)} %get-tuple-element.28.address_ref, s32[1,768]{1,0:T(1,128)S(1)} %get-tuple-element.29.slot_ref, f32[400,128]{1,0:T(8,128)S(1)} %get-tuple-element.30.refs_0_.refs_2_, f32[512,512]{1,0:T(8,128)S(1)} %get-tuple-element.31.refs_1_, ...), custom_call_target="tpu_custom_call" | custom-call | flops 805306368 | bytes 10000000 | tf_op jit(solution)/shard_map/block_gradients/pallas_call | solution.py:472
  100.1 2.3 %collective-permute-done.5.refs_5_ = f32[400,128]{1,0:T(8,128)S(1)} collective-permute-done((f32[400,128]{1,0:T(8,128)S(1)}, f32[400,128]{1,0:T(8,128)S(1)}, u32[]{:S(2)}, u32[]{:S(2)}) %collective-permute-start.5) | collective-permute-done | bytes 204832 | tf_op jit(solution)/shard_map/ppermute | solution.py:609
  102.4 2.7 %finish_gradients.1 = (f32[4800,128]{1,0:T(8,128)}, f32[4800,128]{1,0:T(8,128)S(1)}, f32[1544,128]{1,0:T(8,128)S(1)}) custom-call(s32[1,768]{1,0:T(1,128)S(1)} %get-tuple-element.28.address_ref, s32[1,768]{1,0:T(1,128)S(1)} %get-tuple-element.29.slot_ref, f32[4800,128]{1,0:T(8,128)S(1)} %get-tuple-element.43.refs_0_, ...), custom_call_target="tpu_custom_call", output_to_operand_aliasing={{1}: (2, {}), {2}: (3, {})} | custom-call | tf_op jit(solution)/shard_map/finish_gradients/pallas_call | solution.py:509
  105.1 4.5 %all-to-all-start.2 = ((f32[32,1,19200]{2,1,0:T(1,128)}), f32[32,1,19200]{2,1,0:T(1,128)}, u32[]{:S(2)}, u32[]{:S(2)}) async-start(f32[32,1,19200]{2,1,0:T(1,128)} %bitcast.20), calls=%async_computation.2 | async-start | bytes 4915200 | tf_op jit(solution)/shard_map/all_to_all | solution.py:601
  110.9 55.1 %all-to-all-done.2 = f32[32,1,19200]{2,1,0:T(1,128)} async-done(((f32[32,1,19200]{2,1,0:T(1,128)}), f32[32,1,19200]{2,1,0:T(1,128)}, u32[]{:S(2)}, u32[]{:S(2)}) %all-to-all-start.2) | async-done | bytes 2457632 | tf_op jit(solution)/shard_map/all_to_all | solution.py:601
  166.0 9.2 %update_table.1 = (f32[400,2048]{1,0:T(8,128)}, f32[1,2048]{1,0:T(1,128)}) custom-call(s32[1,1536]{1,0:T(1,128)S(1)} %reshape.41.asked_ref, f32[4800,128]{1,0:T(8,128)} %bitcast.9.packed_hbm, f32[1,2048]{1,0:T(1,128)S(1)} %bitcast.18, f32[400,2048]{1,0:T(8,128)S(1)} %bitcast.16), custom_call_target="tpu_custom_call" | custom-call | tf_op jit(solution)/shard_map/update_table/pallas_call | solution.py:581
  (21 shorter events, 3.1 us)
Async XLA Ops:
  3.5 14.4 %all-to-all-start = ((s32[32,1,48]{2,1,0:T(1,128)}), s32[32,1,48]{2,1,0:T(1,128)S(1)}, u32[]{:S(2)}, u32[]{:S(2)}) async-start(s32[32,1,48]{2,1,0:T(1,128)} %get-tuple-element.27), calls=%async_computation | async-start | bytes 32768 | tf_op jit(solution)/shard_map/all_to_all | solution.py:601
  10.8 1.9 %copy-start = (f32[2048,400]{0,1:T(8,128)S(1)}, f32[2048,400]{0,1:T(8,128)}, u32[]{:S(2)}) copy-start(f32[2048,400]{0,1:T(8,128)} %param.8) | copy-start | bytes 9830404
  22.5 59.4 %all-to-all-start.1 = ((f32[32,1,19200]{2,1,0:T(1,128)}), f32[32,1,19200]{2,1,0:T(1,128)S(1)}, u32[]{:S(2)}, u32[]{:S(2)}) async-start(f32[32,1,19200]{2,1,0:T(1,128)} %bitcast.19), calls=%async_computation.1 | async-start | bytes 4915200 | tf_op jit(solution)/shard_map/all_to_all | solution.py:601
  25.3 14.1 %copy-start.3 = (s32[128]{0:T(128)S(1)}, s32[128]{0:T(128)}, u32[]{:S(2)}) copy-start(s32[128]{0:T(128)} %param.13) | copy-start | bytes 1540
  83.2 4.5 %collective-permute-start = (f32[400,128]{1,0:T(8,128)S(1)}, f32[400,128]{1,0:T(8,128)S(1)}, u32[]{:S(2)}, u32[]{:S(2)}) collective-permute-start(f32[400,128]{1,0:T(8,128)S(1)} %unpack_heads.1.query_ref.refs_5_.refs_2_), channel_id=1, source_target_pairs={{0,1},{1,0},{2,3},{3,2},{4,5},{5,4},{6,7},{7,6},{8,9},{9,8},{10,11... | collective-permute-start | bytes 614408 | tf_op jit(solution)/shard_map/ppermute | solution.py:605
  83.3 7.5 %collective-permute-start.1 = (f32[400,128]{1,0:T(8,128)S(1)}, f32[400,128]{1,0:T(8,128)S(1)}, u32[]{:S(2)}, u32[]{:S(2)}) collective-permute-start(f32[400,128]{1,0:T(8,128)S(1)} %unpack_heads.1.query_ref.refs_5_.refs_2_), channel_id=1, source_target_pairs={{0,2},{1,3},{2,0},{3,1},{4,6},{5,7},{6,4},{7,5},{8,10},{9,11},{10,... | collective-permute-start | bytes 614408 | tf_op jit(solution)/shard_map/ppermute | solution.py:609
  90.8 1.5 collective-permute-start.2
  93.7 1.5 collective-permute-start.4
  93.9 6.2 %collective-permute-start.3 = (f32[400,128]{1,0:T(8,128)S(1)}, f32[400,128]{1,0:T(8,128)S(1)}, u32[]{:S(2)}, u32[]{:S(2)}) collective-permute-start(f32[400,128]{1,0:T(8,128)S(1)} %get-tuple-element.46), channel_id=1, source_target_pairs={{0,1},{1,0},{2,3},{3,2},{4,5},{5,4},{6,7},{7,6},{8,9},{9,8},{10,11... | collective-permute-start | bytes 614408 | tf_op jit(solution)/shard_map/ppermute | solution.py:605
  95.2 7.2 %collective-permute-start.5 = (f32[400,128]{1,0:T(8,128)S(1)}, f32[400,128]{1,0:T(8,128)S(1)}, u32[]{:S(2)}, u32[]{:S(2)}) collective-permute-start(f32[400,128]{1,0:T(8,128)S(1)} %add.11), channel_id=1, source_target_pairs={{0,2},{1,3},{2,0},{3,1},{4,6},{5,7},{6,4},{7,5},{8,10},{9,11},{10,... | collective-permute-start | bytes 614408 | tf_op jit(solution)/shard_map/ppermute | solution.py:609
  105.1 60.9 %copy-start.1 = (f32[2048,400]{0,1:T(8,128)S(1)}, f32[2048,400]{0,1:T(8,128)}, u32[]{:S(2)}) copy-start(f32[2048,400]{0,1:T(8,128)} %param.8) | copy-start | bytes 9830404
  105.1 60.9 %copy-start.2 = (f32[2048]{0:T(1024)S(1)}, f32[2048]{0:T(1024)}, u32[]{:S(2)}) copy-start(f32[2048]{0:T(1024)} %param.9) | copy-start | bytes 24580
  105.1 60.9 %all-to-all-start.2 = ((f32[32,1,19200]{2,1,0:T(1,128)}), f32[32,1,19200]{2,1,0:T(1,128)}, u32[]{:S(2)}, u32[]{:S(2)}) async-start(f32[32,1,19200]{2,1,0:T(1,128)} %bitcast.20), calls=%async_computation.2 | async-start | bytes 4915200 | tf_op jit(solution)/shard_map/all_to_all | solution.py:601

commit v7 on v6

--- a/solution.py
+++ b/solution.py
@@ -13,6 +13,7 @@
 LANES = 128
 SUBLANES = 8
 SCORE_STEPS = 2
+SERVE_OWNERS = 4
 VMEM_BYTES = 24 * 1024 * 1024
 
 
@@ -268,7 +269,11 @@
             rests_ref[pl.ds(slots + first, SUBLANES), :] = jnp.concatenate(rests, axis=0)
 
     for index, copy in enumerate(copies):
-        loop(each, lambda owner: body(index * each + owner))
+        def step(some):
+            for owner in range(SERVE_OWNERS):
+                body(index * each + some * SERVE_OWNERS + owner)
+
+        loop(each // SERVE_OWNERS, step)
         share_rests(pack, rests_ref, out_ref, index * each, each)
         copy.start()
     for copy in copies:
@@ -294,9 +299,9 @@
 
 def copy_rows(pack, first_request, address_ref, slot_ref, packed_ref, rests_ref, rows_ref):
     def body(group):
-        first = group * SUBLANES
+        first = group * 2 * SUBLANES
         values = []
-        for j in range(SUBLANES):
+        for j in range(2 * SUBLANES):
             request = first_request + first + j
             values.append(
                 (
@@ -308,7 +313,7 @@
             rows_ref[first + j, : pack.full, :] = groups
             rows_ref[first + j, pack.full :, :] = rest
 
-    loop(rows_ref.shape[0] // SUBLANES, body)
+    loop(rows_ref.shape[0] // (2 * SUBLANES), body)
 
 
 def heads_kernel(
@@ -430,14 +435,14 @@
 
 def store_rows(pack, first_request, address_ref, slot_ref, rows_ref, out_ref, rests_ref):
     def body(group):
-        first = group * SUBLANES
-        values = [rows_ref[first + j] for j in range(SUBLANES)]
+        first = group * 2 * SUBLANES
+        values = [rows_ref[first + j] for j in range(2 * SUBLANES)]
         for j, value in enumerate(values):
             request = first_request + first + j
             out_ref[pl.ds(address_ref[0, request], pack.full), :] = value[: pack.full]
             rests_ref[pl.ds(slot_ref[0, request], 1), :] = value[pack.full :]
 
-    loop(rows_ref.shape[0] // SUBLANES, body)
+    loop(rows_ref.shape[0] // (2 * SUBLANES), body)
 
 
 def store_columns(pack, columns, rows_ref):

time: 176 us -> 176 us (level)
  no operation moved by 1% of the time
where the time goes in v7:
time: 176 us; the launch traced here: 175 us
  waiting for transfers between devices  102 us (58%)
  Pallas kernels  30.8 us (18%)
  local copies, waits for them, and re-layouts  23 us (13%)
  starting transfers between devices  17.9 us (10%)
    all_to_all x3, waiting for transfers between devices, exchange(): lax.all_to_all(payload, ('dp', 'blk'), split_axis=0, concat_axis=0, tiled...  95.1 us
    unnamed x9, local copies, waits for them, and re-layouts  16.1 us
    all_to_all x3, starting transfers between devices, exchange(): lax.all_to_all(payload, ('dp', 'blk'), split_axis=0, concat_axis=0, tiled...  14.6 us
    pallas_call x1, Pallas kernels, update(): pl.pallas_call(functools.partial(update_kernel, pack, columns), out_shape...  9.18 us
    gather x2, local copies, waits for them, and re-layouts, on_device(): relations[rel_ids]  6.32 us
    pallas_call x1, Pallas kernels, serve(): pl.pallas_call(functools.partial(serve_kernel, pack, rows_here), out_shap...  4.5 us
    ppermute x2, waiting for transfers between devices, to_chip(): lax.ppermute(value, 'blk', [(i, (i + 2 * hops) % blk_count) for i in rang...  4.38 us
  transfers between devices with their start and end apart: 9, of which 7 were waited for; matrix products, arithmetic and copies ran while one was open for 12% of the time, Pallas kernels for 5%

profile of v7, /device:TPU:0, one launch (start us, length us, event | category | flops | bytes accessed | tf_op | source)
XLA Modules:
  0.0 175.3 jit_solution(16893488102640011490)
XLA Ops:
  0.6 2.8 %build_requests.1 = (s32[32,1,48]{2,1,0:T(1,128)}, s32[1,768]{1,0:T(1,128)S(1)}, s32[1,768]{1,0:T(1,128)S(1)}) custom-call(s32[512,128]{1,0:T(8,128)} %bitcast.21, s32[1,128]{1,0:T(1,128)} %bitcast.23, s32[1,128]{1,0:T(1,128)} %bitcast.24, s32[1,512]{1,0:T(1,128)} %bitcast.22), custom_call_target="tpu_custom_call" | custom-call | tf_op jit(solution)/shard_map/build_requests/pallas_call | solution.py:167
  3.5 7.3 %all-to-all-start = ((s32[32,1,48]{2,1,0:T(1,128)}), s32[32,1,48]{2,1,0:T(1,128)S(1)}, u32[]{:S(2)}, u32[]{:S(2)}) async-start(s32[32,1,48]{2,1,0:T(1,128)} %get-tuple-element.27), calls=%async_computation | async-start | bytes 32768 | tf_op jit(solution)/shard_map/all_to_all | solution.py:606
  10.8 1.9 %copy-done = f32[2048,400]{0,1:T(8,128)S(1)} copy-done((f32[2048,400]{0,1:T(8,128)S(1)}, f32[2048,400]{0,1:T(8,128)}, u32[]{:S(2)}) %copy-start) | copy-done | bytes 3276824
  12.7 1.4 table_rows.1.table_ref
  14.1 3.7 %all-to-all-done.asked_ref = s32[32,1,48]{2,1,0:T(1,128)S(1)} async-done(((s32[32,1,48]{2,1,0:T(1,128)}), s32[32,1,48]{2,1,0:T(1,128)S(1)}, u32[]{:S(2)}, u32[]{:S(2)}) %all-to-all-start) | async-done | bytes 6176 | tf_op jit(solution)/shard_map/all_to_all | solution.py:606
  17.9 4.5 %serve_rows.1 = f32[4800,128]{1,0:T(8,128)} custom-call(s32[32,1,48]{2,1,0:T(1,128)S(1)} %all-to-all-done.asked_ref, f32[6432,128]{1,0:T(8,128)S(1)} %table_rows.1.table_ref), custom_call_target="tpu_custom_call" | custom-call | tf_op jit(solution)/shard_map/serve_rows/pallas_call | solution.py:284
  22.4 2.8 %all-to-all-start.1 = ((f32[32,1,19200]{2,1,0:T(1,128)}), f32[32,1,19200]{2,1,0:T(1,128)S(1)}, u32[]{:S(2)}, u32[]{:S(2)}) async-start(f32[32,1,19200]{2,1,0:T(1,128)} %bitcast.19), calls=%async_computation.1 | async-start | bytes 4915200 | tf_op jit(solution)/shard_map/all_to_all | solution.py:606
  25.2 14.1 %copy.15 = f32[7424,400]{1,0:T(8,128)} copy(f32[7424,400]{0,1:T(8,128)} %param.10) | data formatting | bytes 23756800 | tf_op args[2]
  39.3 6.2 %gather_fusion = f32[128,400]{1,0:T(8,128)S(1)} fusion(f32[7424,400]{1,0:T(8,128)} %copy.15, s32[1024]{0:T(1024)S(1)} %pad_clamp_fusion), kind=kCustom, calls=%fused_computation | custom fusion | bytes 410112 | tf_op jit(solution)/shard_map/gather | solution.py:639
  45.6 36.1 %all-to-all-done.1 = f32[32,1,19200]{2,1,0:T(1,128)S(1)} async-done(((f32[32,1,19200]{2,1,0:T(1,128)}), f32[32,1,19200]{2,1,0:T(1,128)S(1)}, u32[]{:S(2)}, u32[]{:S(2)}) %all-to-all-start.1) | async-done | bytes 2457632 | tf_op jit(solution)/shard_map/all_to_all | solution.py:606
  81.8 1.3 unpack_heads.1.query_ref.refs_5_.refs_2_
  83.1 1.3 collective-permute-start.1
  84.5 2.9 %unpack_rest.1 = (f32[400,128]{1,0:T(8,128)S(1)}, f32[512,512]{1,0:T(8,128)S(1)}, bf16[512,512]{1,0:T(8,128)(2,1)S(1)}, bf16[512,512]{1,0:T(8,128)(2,1)S(1)}, bf...) custom-call(s32[1,768]{1,0:T(1,128)S(1)} %get-tuple-element.28.address_ref, ...), custom_call_target="tpu_custom_call" | custom-call | flops 10000000 | bytes 9000000 | tf_op jit(solution)/shard_map/unpack_rest/pallas_call | solution.py:363
  87.4 1.4 negative_terms.2
  88.7 1.9 %collective-permute-done.1.refs_5_.refs_4_ = f32[400,128]{1,0:T(8,128)S(1)} collective-permute-done((f32[400,128]{1,0:T(8,128)S(1)}, f32[400,128]{1,0:T(8,128)S(1)}, u32[]{:S(2)}, u32[]{:S(2)}) %collective-permute-start.1) | collective-permute-done | bytes 204832 | tf_op jit(solution)/shard_map/ppermute | solution.py:614
  90.6 1.5 collective-permute-done.2.refs_6_.refs_5_
  92.1 1.4 negative_terms.3
  95.0 1.3 collective-permute-start.5
  96.4 3.3 %block_gradients.1 = (f32[4800,128]{1,0:T(8,128)S(1)}, f32[1544,128]{1,0:T(8,128)S(1)}) custom-call(s32[1,768]{1,0:T(1,128)S(1)} %get-tuple-element.28.address_ref, s32[1,768]{1,0:T(1,128)S(1)} %get-tuple-element.29.slot_ref, f32[400,128]{1,0:T(8,128)S(1)} %get-tuple-element.30.refs_0_.refs_2_, f32[512,512]{1,0:T(8,128)S(1)} %get-tuple-element.31.refs_1_, ...), custom_call_target="tpu_custom_call" | custom-call | flops 805306368 | bytes 10000000 | tf_op jit(solution)/shard_map/block_gradients/pallas_call | solution.py:477
  99.7 2.5 %collective-permute-done.5.refs_5_ = f32[400,128]{1,0:T(8,128)S(1)} collective-permute-done((f32[400,128]{1,0:T(8,128)S(1)}, f32[400,128]{1,0:T(8,128)S(1)}, u32[]{:S(2)}, u32[]{:S(2)}) %collective-permute-start.5) | collective-permute-done | bytes 204832 | tf_op jit(solution)/shard_map/ppermute | solution.py:614
  102.2 2.6 %finish_gradients.1 = (f32[4800,128]{1,0:T(8,128)}, f32[4800,128]{1,0:T(8,128)S(1)}, f32[1544,128]{1,0:T(8,128)S(1)}) custom-call(s32[1,768]{1,0:T(1,128)S(1)} %get-tuple-element.28.address_ref, s32[1,768]{1,0:T(1,128)S(1)} %get-tuple-element.29.slot_ref, f32[4800,128]{1,0:T(8,128)S(1)} %get-tuple-element.43.refs_0_, ...), custom_call_target="tpu_custom_call", output_to_operand_aliasing={{1}: (2, {}), {2}: (3, {})} | custom-call | tf_op jit(solution)/shard_map/finish_gradients/pallas_call | solution.py:514
  104.9 4.5 %all-to-all-start.2 = ((f32[32,1,19200]{2,1,0:T(1,128)}), f32[32,1,19200]{2,1,0:T(1,128)}, u32[]{:S(2)}, u32[]{:S(2)}) async-start(f32[32,1,19200]{2,1,0:T(1,128)} %bitcast.20), calls=%async_computation.2 | async-start | bytes 4915200 | tf_op jit(solution)/shard_map/all_to_all | solution.py:606
  110.7 55.3 %all-to-all-done.2 = f32[32,1,19200]{2,1,0:T(1,128)} async-done(((f32[32,1,19200]{2,1,0:T(1,128)}), f32[32,1,19200]{2,1,0:T(1,128)}, u32[]{:S(2)}, u32[]{:S(2)}) %all-to-all-start.2) | async-done | bytes 2457632 | tf_op jit(solution)/shard_map/all_to_all | solution.py:606
  165.9 9.2 %update_table.1 = (f32[400,2048]{1,0:T(8,128)}, f32[1,2048]{1,0:T(1,128)}) custom-call(s32[1,1536]{1,0:T(1,128)S(1)} %reshape.41.asked_ref, f32[4800,128]{1,0:T(8,128)} %bitcast.9.packed_hbm, f32[1,2048]{1,0:T(1,128)S(1)} %bitcast.18, f32[400,2048]{1,0:T(8,128)S(1)} %bitcast.16), custom_call_target="tpu_custom_call" | custom-call | tf_op jit(solution)/shard_map/update_table/pallas_call | solution.py:586
  (21 shorter events, 3.1 us)
Async XLA Ops:
  3.5 14.4 %all-to-all-start = ((s32[32,1,48]{2,1,0:T(1,128)}), s32[32,1,48]{2,1,0:T(1,128)S(1)}, u32[]{:S(2)}, u32[]{:S(2)}) async-start(s32[32,1,48]{2,1,0:T(1,128)} %get-tuple-element.27), calls=%async_computation | async-start | bytes 32768 | tf_op jit(solution)/shard_map/all_to_all | solution.py:606
  10.8 1.9 %copy-start = (f32[2048,400]{0,1:T(8,128)S(1)}, f32[2048,400]{0,1:T(8,128)}, u32[]{:S(2)}) copy-start(f32[2048,400]{0,1:T(8,128)} %param.8) | copy-start | bytes 9830404
  22.4 59.4 %all-to-all-start.1 = ((f32[32,1,19200]{2,1,0:T(1,128)}), f32[32,1,19200]{2,1,0:T(1,128)S(1)}, u32[]{:S(2)}, u32[]{:S(2)}) async-start(f32[32,1,19200]{2,1,0:T(1,128)} %bitcast.19), calls=%async_computation.1 | async-start | bytes 4915200 | tf_op jit(solution)/shard_map/all_to_all | solution.py:606
  25.2 14.1 %copy-start.3 = (s32[128]{0:T(128)S(1)}, s32[128]{0:T(128)}, u32[]{:S(2)}) copy-start(s32[128]{0:T(128)} %param.13) | copy-start | bytes 1540
  83.1 4.3 %collective-permute-start = (f32[400,128]{1,0:T(8,128)S(1)}, f32[400,128]{1,0:T(8,128)S(1)}, u32[]{:S(2)}, u32[]{:S(2)}) collective-permute-start(f32[400,128]{1,0:T(8,128)S(1)} %unpack_heads.1.query_ref.refs_5_.refs_2_), channel_id=1, source_target_pairs={{0,1},{1,0},{2,3},{3,2},{4,5},{5,4},{6,7},{7,6},{8,9},{9,8},{10,11... | collective-permute-start | bytes 614408 | tf_op jit(solution)/shard_map/ppermute | solution.py:610
  83.1 7.5 %collective-permute-start.1 = (f32[400,128]{1,0:T(8,128)S(1)}, f32[400,128]{1,0:T(8,128)S(1)}, u32[]{:S(2)}, u32[]{:S(2)}) collective-permute-start(f32[400,128]{1,0:T(8,128)S(1)} %unpack_heads.1.query_ref.refs_5_.refs_2_), channel_id=1, source_target_pairs={{0,2},{1,3},{2,0},{3,1},{4,6},{5,7},{6,4},{7,5},{8,10},{9,11},{10,... | collective-permute-start | bytes 614408 | tf_op jit(solution)/shard_map/ppermute | solution.py:614
  90.6 1.5 collective-permute-start.2
  93.5 1.5 collective-permute-start.4
  93.7 6.0 %collective-permute-start.3 = (f32[400,128]{1,0:T(8,128)S(1)}, f32[400,128]{1,0:T(8,128)S(1)}, u32[]{:S(2)}, u32[]{:S(2)}) collective-permute-start(f32[400,128]{1,0:T(8,128)S(1)} %get-tuple-element.46), channel_id=1, source_target_pairs={{0,1},{1,0},{2,3},{3,2},{4,5},{5,4},{6,7},{7,6},{8,9},{9,8},{10,11... | collective-permute-start | bytes 614408 | tf_op jit(solution)/shard_map/ppermute | solution.py:610
  95.0 7.2 %collective-permute-start.5 = (f32[400,128]{1,0:T(8,128)S(1)}, f32[400,128]{1,0:T(8,128)S(1)}, u32[]{:S(2)}, u32[]{:S(2)}) collective-permute-start(f32[400,128]{1,0:T(8,128)S(1)} %add.11), channel_id=1, source_target_pairs={{0,2},{1,3},{2,0},{3,1},{4,6},{5,7},{6,4},{7,5},{8,10},{9,11},{10,... | collective-permute-start | bytes 614408 | tf_op jit(solution)/shard_map/ppermute | solution.py:614
  104.9 61.1 %copy-start.1 = (f32[2048,400]{0,1:T(8,128)S(1)}, f32[2048,400]{0,1:T(8,128)}, u32[]{:S(2)}) copy-start(f32[2048,400]{0,1:T(8,128)} %param.8) | copy-start | bytes 9830404
  104.9 61.0 %copy-start.2 = (f32[2048]{0:T(1024)S(1)}, f32[2048]{0:T(1024)}, u32[]{:S(2)}) copy-start(f32[2048]{0:T(1024)} %param.9) | copy-start | bytes 24580
  104.9 61.0 %all-to-all-start.2 = ((f32[32,1,19200]{2,1,0:T(1,128)}), f32[32,1,19200]{2,1,0:T(1,128)}, u32[]{:S(2)}, u32[]{:S(2)}) async-start(f32[32,1,19200]{2,1,0:T(1,128)} %bitcast.20), calls=%async_computation.2 | async-start | bytes 4915200 | tf_op jit(solution)/shard_map/all_to_all | solution.py:606

commit v8 on v7

--- a/solution.py
+++ b/solution.py
@@ -305,8 +305,8 @@
             request = first_request + first + j
             values.append(
                 (
-                    packed_ref[pl.ds(address_ref[0, request], pack.full), :],
-                    rests_ref[pl.ds(slot_ref[0, request], 1), :],
+                    packed_ref[pl.ds(address_ref[request], pack.full), :],
+                    rests_ref[pl.ds(slot_ref[request], 1), :],
                 )
             )
         for j, (groups, rest) in enumerate(values):
@@ -439,8 +439,8 @@
         values = [rows_ref[first + j] for j in range(2 * SUBLANES)]
         for j, value in enumerate(values):
             request = first_request + first + j
-            out_ref[pl.ds(address_ref[0, request], pack.full), :] = value[: pack.full]
-            rests_ref[pl.ds(slot_ref[0, request], 1), :] = value[pack.full :]
+            out_ref[pl.ds(address_ref[request], pack.full), :] = value[: pack.full]
+            rests_ref[pl.ds(slot_ref[request], 1), :] = value[pack.full :]
 
     loop(rows_ref.shape[0] // (2 * SUBLANES), body)
 
@@ -633,6 +633,7 @@
         pack, rows_here, owner_map, head_ids, tail_ids, neg_ids
     )
     asked = exchange(requests)
+    address, slot_of = address.reshape(-1), slot_of.reshape(-1)
     served = serve(pack, rows_here, asked, to_rows(pack, entity_table.T))
     fetched = exchange(served.reshape(owner_count, 1, pack.stride * LANES))
     fetched = fetched.reshape(pack.rows, LANES)

time: 176 us -> 176 us (level)
  no operation moved by 1% of the time
where the time goes in v8:
time: 176 us; the launch traced here: 175 us
  waiting for transfers between devices  102 us (58%)
  Pallas kernels  30.6 us (17%)
  local copies, waits for them, and re-layouts  23 us (13%)
  starting transfers between devices  18 us (10%)
    all_to_all x3, waiting for transfers between devices, exchange(): lax.all_to_all(payload, ('dp', 'blk'), split_axis=0, concat_axis=0, tiled...  94.8 us
    unnamed x9, local copies, waits for them, and re-layouts  16 us
    all_to_all x3, starting transfers between devices, exchange(): lax.all_to_all(payload, ('dp', 'blk'), split_axis=0, concat_axis=0, tiled...  14.8 us
    pallas_call x1, Pallas kernels, update(): pl.pallas_call(functools.partial(update_kernel, pack, columns), out_shape...  9.08 us
    gather x2, local copies, waits for them, and re-layouts, on_device(): relations[rel_ids]  6.32 us
    pallas_call x1, Pallas kernels, serve(): pl.pallas_call(functools.partial(serve_kernel, pack, rows_here), out_shap...  4.5 us
    ppermute x2, waiting for transfers between devices, to_chip(): lax.ppermute(value, 'blk', [(i, (i + 2 * hops) % blk_count) for i in rang...  4.45 us
  transfers between devices with their start and end apart: 9, of which 7 were waited for; matrix products, arithmetic and copies ran while one was open for 12% of the time, Pallas kernels for 5%

profile of v8, /device:TPU:0, one launch (start us, length us, event | category | flops | bytes accessed | tf_op | source)
XLA Modules:
  0.0 175.0 jit_solution(6394153743865114355)
XLA Ops:
  0.6 2.8 %build_requests.1 = (s32[32,1,48]{2,1,0:T(1,128)}, s32[1,768]{1,0:T(1,128)S(1)}, s32[1,768]{1,0:T(1,128)S(1)}) custom-call(s32[512,128]{1,0:T(8,128)} %bitcast.21, s32[1,128]{1,0:T(1,128)} %bitcast.23, s32[1,128]{1,0:T(1,128)} %bitcast.24, s32[1,512]{1,0:T(1,128)} %bitcast.22), custom_call_target="tpu_custom_call" | custom-call | tf_op jit(solution)/shard_map/build_requests/pallas_call | solution.py:167
  3.5 7.3 %all-to-all-start = ((s32[32,1,48]{2,1,0:T(1,128)}), s32[32,1,48]{2,1,0:T(1,128)S(1)}, u32[]{:S(2)}, u32[]{:S(2)}) async-start(s32[32,1,48]{2,1,0:T(1,128)} %get-tuple-element.27), calls=%async_computation | async-start | bytes 32768 | tf_op jit(solution)/shard_map/all_to_all | solution.py:606
  10.8 1.9 %copy-done = f32[2048,400]{0,1:T(8,128)S(1)} copy-done((f32[2048,400]{0,1:T(8,128)S(1)}, f32[2048,400]{0,1:T(8,128)}, u32[]{:S(2)}) %copy-start) | copy-done | bytes 3276824
  12.7 1.4 table_rows.1.table_ref
  14.1 3.7 %all-to-all-done.asked_ref = s32[32,1,48]{2,1,0:T(1,128)S(1)} async-done(((s32[32,1,48]{2,1,0:T(1,128)}), s32[32,1,48]{2,1,0:T(1,128)S(1)}, u32[]{:S(2)}, u32[]{:S(2)}) %all-to-all-start) | async-done | bytes 6176 | tf_op jit(solution)/shard_map/all_to_all | solution.py:606
  17.9 4.5 %serve_rows.1 = f32[4800,128]{1,0:T(8,128)} custom-call(s32[32,1,48]{2,1,0:T(1,128)S(1)} %all-to-all-done.asked_ref, f32[6432,128]{1,0:T(8,128)S(1)} %table_rows.1.table_ref), custom_call_target="tpu_custom_call" | custom-call | tf_op jit(solution)/shard_map/serve_rows/pallas_call | solution.py:284
  22.4 3.0 %all-to-all-start.1 = ((f32[32,1,19200]{2,1,0:T(1,128)}), f32[32,1,19200]{2,1,0:T(1,128)S(1)}, u32[]{:S(2)}, u32[]{:S(2)}) async-start(f32[32,1,19200]{2,1,0:T(1,128)} %bitcast.19), calls=%async_computation.1 | async-start | bytes 4915200 | tf_op jit(solution)/shard_map/all_to_all | solution.py:606
  25.4 14.1 %copy.15 = f32[7424,400]{1,0:T(8,128)} copy(f32[7424,400]{0,1:T(8,128)} %param.10) | data formatting | bytes 23756800 | tf_op args[2]
  39.5 6.2 %gather_fusion = f32[128,400]{1,0:T(8,128)S(1)} fusion(f32[7424,400]{1,0:T(8,128)} %copy.15, s32[1024]{0:T(1024)S(1)} %pad_clamp_fusion), kind=kCustom, calls=%fused_computation | custom fusion | bytes 410112 | tf_op jit(solution)/shard_map/gather | solution.py:640
  45.8 36.0 %all-to-all-done.1 = f32[32,1,19200]{2,1,0:T(1,128)S(1)} async-done(((f32[32,1,19200]{2,1,0:T(1,128)}), f32[32,1,19200]{2,1,0:T(1,128)S(1)}, u32[]{:S(2)}, u32[]{:S(2)}) %all-to-all-start.1) | async-done | bytes 2457632 | tf_op jit(solution)/shard_map/all_to_all | solution.py:606
  81.8 1.3 unpack_heads.1.query_ref.refs_5_.refs_2_
  83.2 1.3 collective-permute-start.1
  84.5 2.9 %unpack_rest.1 = (f32[400,128]{1,0:T(8,128)S(1)}, f32[512,512]{1,0:T(8,128)S(1)}, bf16[512,512]{1,0:T(8,128)(2,1)S(1)}, bf16[512,512]{1,0:T(8,128)(2,1)S(1)}, bf...) custom-call(s32[768]{0:T(1024)S(1)} %reduce.1.address_ref, ...), custom_call_target="tpu_custom_call" | custom-call | flops 10000000 | bytes 9000000 | tf_op jit(solution)/shard_map/unpack_rest/pallas_call | solution.py:363
  87.4 1.4 negative_terms.2
  88.7 1.9 %collective-permute-done.1.refs_5_.refs_4_ = f32[400,128]{1,0:T(8,128)S(1)} collective-permute-done((f32[400,128]{1,0:T(8,128)S(1)}, f32[400,128]{1,0:T(8,128)S(1)}, u32[]{:S(2)}, u32[]{:S(2)}) %collective-permute-start.1) | collective-permute-done | bytes 204832 | tf_op jit(solution)/shard_map/ppermute | solution.py:614
  90.7 1.5 collective-permute-done.2.refs_6_.refs_5_
  92.1 1.4 negative_terms.3
  95.0 1.3 collective-permute-start.5
  96.3 3.3 %block_gradients.1 = (f32[4800,128]{1,0:T(8,128)S(1)}, f32[1544,128]{1,0:T(8,128)S(1)}) custom-call(s32[768]{0:T(1024)S(1)} %reduce.1.address_ref, s32[768]{0:T(1024)S(1)} %reduce.2.slot_ref, f32[400,128]{1,0:T(8,128)S(1)} %get-tuple-element.30.refs_0_.refs_2_, f32[512,512]{1,0:T(8,128)S(1)} %get-tuple-element.31.refs_1_, ...), custom_call_target="tpu_custom_call" | custom-call | flops 805306368 | bytes 10000000 | tf_op jit(solution)/shard_map/block_gradients/pallas_call | solution.py:477
  99.7 2.5 %collective-permute-done.5.refs_5_ = f32[400,128]{1,0:T(8,128)S(1)} collective-permute-done((f32[400,128]{1,0:T(8,128)S(1)}, f32[400,128]{1,0:T(8,128)S(1)}, u32[]{:S(2)}, u32[]{:S(2)}) %collective-permute-start.5) | collective-permute-done | bytes 204832 | tf_op jit(solution)/shard_map/ppermute | solution.py:614
  102.2 2.6 %finish_gradients.1 = (f32[4800,128]{1,0:T(8,128)}, f32[4800,128]{1,0:T(8,128)S(1)}, f32[1544,128]{1,0:T(8,128)S(1)}) custom-call(s32[768]{0:T(1024)S(1)} %reduce.1.address_ref, s32[768]{0:T(1024)S(1)} %reduce.2.slot_ref, f32[4800,128]{1,0:T(8,128)S(1)} %get-tuple-element.43.refs_0_, ...), custom_call_target="tpu_custom_call", output_to_operand_aliasing={{1}: (2, {}), {2}: (3, {})} | custom-call | tf_op jit(solution)/shard_map/finish_gradients/pallas_call | solution.py:514
  104.9 4.5 %all-to-all-start.2 = ((f32[32,1,19200]{2,1,0:T(1,128)}), f32[32,1,19200]{2,1,0:T(1,128)}, u32[]{:S(2)}, u32[]{:S(2)}) async-start(f32[32,1,19200]{2,1,0:T(1,128)} %bitcast.20), calls=%async_computation.2 | async-start | bytes 4915200 | tf_op jit(solution)/shard_map/all_to_all | solution.py:606
  110.7 55.1 %all-to-all-done.2 = f32[32,1,19200]{2,1,0:T(1,128)} async-done(((f32[32,1,19200]{2,1,0:T(1,128)}), f32[32,1,19200]{2,1,0:T(1,128)}, u32[]{:S(2)}, u32[]{:S(2)}) %all-to-all-start.2) | async-done | bytes 2457632 | tf_op jit(solution)/shard_map/all_to_all | solution.py:606
  165.8 9.1 %update_table.1 = (f32[400,2048]{1,0:T(8,128)}, f32[1,2048]{1,0:T(1,128)}) custom-call(s32[1,1536]{1,0:T(1,128)S(1)} %reshape.47.asked_ref, f32[4800,128]{1,0:T(8,128)} %bitcast.9.packed_hbm, f32[1,2048]{1,0:T(1,128)S(1)} %bitcast.18, f32[400,2048]{1,0:T(8,128)S(1)} %bitcast.16), custom_call_target="tpu_custom_call" | custom-call | tf_op jit(solution)/shard_map/update_table/pallas_call | solution.py:586
  (23 shorter events, 3.1 us)
Async XLA Ops:
  3.5 14.4 %all-to-all-start = ((s32[32,1,48]{2,1,0:T(1,128)}), s32[32,1,48]{2,1,0:T(1,128)S(1)}, u32[]{:S(2)}, u32[]{:S(2)}) async-start(s32[32,1,48]{2,1,0:T(1,128)} %get-tuple-element.27), calls=%async_computation | async-start | bytes 32768 | tf_op jit(solution)/shard_map/all_to_all | solution.py:606
  10.8 1.9 %copy-start = (f32[2048,400]{0,1:T(8,128)S(1)}, f32[2048,400]{0,1:T(8,128)}, u32[]{:S(2)}) copy-start(f32[2048,400]{0,1:T(8,128)} %param.8) | copy-start | bytes 9830404
  22.4 59.5 %all-to-all-start.1 = ((f32[32,1,19200]{2,1,0:T(1,128)}), f32[32,1,19200]{2,1,0:T(1,128)S(1)}, u32[]{:S(2)}, u32[]{:S(2)}) async-start(f32[32,1,19200]{2,1,0:T(1,128)} %bitcast.19), calls=%async_computation.1 | async-start | bytes 4915200 | tf_op jit(solution)/shard_map/all_to_all | solution.py:606
  25.4 14.1 %copy-start.3 = (s32[128]{0:T(128)S(1)}, s32[128]{0:T(128)}, u32[]{:S(2)}) copy-start(s32[128]{0:T(128)} %param.13) | copy-start | bytes 1540
  83.1 4.3 %collective-permute-start = (f32[400,128]{1,0:T(8,128)S(1)}, f32[400,128]{1,0:T(8,128)S(1)}, u32[]{:S(2)}, u32[]{:S(2)}) collective-permute-start(f32[400,128]{1,0:T(8,128)S(1)} %unpack_heads.1.query_ref.refs_5_.refs_2_), channel_id=1, source_target_pairs={{0,1},{1,0},{2,3},{3,2},{4,5},{5,4},{6,7},{7,6},{8,9},{9,8},{10,11... | collective-permute-start | bytes 614408 | tf_op jit(solution)/shard_map/ppermute | solution.py:610
  83.2 7.5 %collective-permute-start.1 = (f32[400,128]{1,0:T(8,128)S(1)}, f32[400,128]{1,0:T(8,128)S(1)}, u32[]{:S(2)}, u32[]{:S(2)}) collective-permute-start(f32[400,128]{1,0:T(8,128)S(1)} %unpack_heads.1.query_ref.refs_5_.refs_2_), channel_id=1, source_target_pairs={{0,2},{1,3},{2,0},{3,1},{4,6},{5,7},{6,4},{7,5},{8,10},{9,11},{10,... | collective-permute-start | bytes 614408 | tf_op jit(solution)/shard_map/ppermute | solution.py:614
  90.7 1.5 collective-permute-start.2
  93.5 1.5 collective-permute-start.4
  93.7 6.0 %collective-permute-start.3 = (f32[400,128]{1,0:T(8,128)S(1)}, f32[400,128]{1,0:T(8,128)S(1)}, u32[]{:S(2)}, u32[]{:S(2)}) collective-permute-start(f32[400,128]{1,0:T(8,128)S(1)} %get-tuple-element.46), channel_id=1, source_target_pairs={{0,1},{1,0},{2,3},{3,2},{4,5},{5,4},{6,7},{7,6},{8,9},{9,8},{10,11... | collective-permute-start | bytes 614408 | tf_op jit(solution)/shard_map/ppermute | solution.py:610
  95.0 7.2 %collective-permute-start.5 = (f32[400,128]{1,0:T(8,128)S(1)}, f32[400,128]{1,0:T(8,128)S(1)}, u32[]{:S(2)}, u32[]{:S(2)}) collective-permute-start(f32[400,128]{1,0:T(8,128)S(1)} %add.11), channel_id=1, source_target_pairs={{0,2},{1,3},{2,0},{3,1},{4,6},{5,7},{6,4},{7,5},{8,10},{9,11},{10,... | collective-permute-start | bytes 614408 | tf_op jit(solution)/shard_map/ppermute | solution.py:614
  104.9 60.9 %copy-start.1 = (f32[2048,400]{0,1:T(8,128)S(1)}, f32[2048,400]{0,1:T(8,128)}, u32[]{:S(2)}) copy-start(f32[2048,400]{0,1:T(8,128)} %param.8) | copy-start | bytes 9830404
  104.9 60.9 %copy-start.2 = (f32[2048]{0:T(1024)S(1)}, f32[2048]{0:T(1024)}, u32[]{:S(2)}) copy-start(f32[2048]{0:T(1024)} %param.9) | copy-start | bytes 24580
  104.9 60.9 %all-to-all-start.2 = ((f32[32,1,19200]{2,1,0:T(1,128)}), f32[32,1,19200]{2,1,0:T(1,128)}, u32[]{:S(2)}, u32[]{:S(2)}) async-start(f32[32,1,19200]{2,1,0:T(1,128)} %bitcast.20), calls=%async_computation.2 | async-start | bytes 4915200 | tf_op jit(solution)/shard_map/all_to_all | solution.py:606

commit v9 on v8

--- a/solution.py
+++ b/solution.py
@@ -555,9 +555,9 @@
                 ]
             rows_ref[rows, pack.full * LANES :] = rests_ref[rows, :]
         slots = slice(index * owners * pack.capacity, (index + 1) * owners * pack.capacity)
-        high, low = split(rows_ref[slots, :].T)
-        halves_ref[:width, slots] = high[:width]
-        halves_ref[width:, slots] = low[:width]
+        high, low = split(rows_ref[slots, :])
+        halves_ref[:width, slots] = high.T[:width]
+        halves_ref[width:, slots] = low.T[:width]
     asked = asked_ref[...]
     row = lax.broadcasted_iota(jnp.int32, (columns, pack.slots), 0)
     copies = []

time: 176 us -> 176 us (level)
  no operation moved by 1% of the time
where the time goes in v9:
time: 176 us; the launch traced here: 175 us
  waiting for transfers between devices  102 us (58%)
  Pallas kernels  30.7 us (17%)
  local copies, waits for them, and re-layouts  23 us (13%)
  starting transfers between devices  18 us (10%)
    all_to_all x3, waiting for transfers between devices, exchange(): lax.all_to_all(payload, ('dp', 'blk'), split_axis=0, concat_axis=0, tiled...  94.8 us
    unnamed x9, local copies, waits for them, and re-layouts  16 us
    all_to_all x3, starting transfers between devices, exchange(): lax.all_to_all(payload, ('dp', 'blk'), split_axis=0, concat_axis=0, tiled...  14.8 us
    pallas_call x1, Pallas kernels, update(): pl.pallas_call(functools.partial(update_kernel, pack, columns), out_shape...  9.11 us
    gather x2, local copies, waits for them, and re-layouts, on_device(): relations[rel_ids]  6.32 us
    pallas_call x1, Pallas kernels, serve(): pl.pallas_call(functools.partial(serve_kernel, pack, rows_here), out_shap...  4.5 us
    ppermute x2, waiting for transfers between devices, to_chip(): lax.ppermute(value, 'blk', [(i, (i + 2 * hops) % blk_count) for i in rang...  4.45 us
  transfers between devices with their start and end apart: 9, of which 7 were waited for; matrix products, arithmetic and copies ran while one was open for 12% of the time, Pallas kernels for 5%

profile of v9, /device:TPU:0, one launch (start us, length us, event | category | flops | bytes accessed | tf_op | source)
XLA Modules:
  0.0 175.1 jit_solution(17100980277950578818)
XLA Ops:
  0.6 2.8 %build_requests.1 = (s32[32,1,48]{2,1,0:T(1,128)}, s32[1,768]{1,0:T(1,128)S(1)}, s32[1,768]{1,0:T(1,128)S(1)}) custom-call(s32[512,128]{1,0:T(8,128)} %bitcast.21, s32[1,128]{1,0:T(1,128)} %bitcast.23, s32[1,128]{1,0:T(1,128)} %bitcast.24, s32[1,512]{1,0:T(1,128)} %bitcast.22), custom_call_target="tpu_custom_call" | custom-call | tf_op jit(solution)/shard_map/build_requests/pallas_call | solution.py:167
  3.5 7.3 %all-to-all-start = ((s32[32,1,48]{2,1,0:T(1,128)}), s32[32,1,48]{2,1,0:T(1,128)S(1)}, u32[]{:S(2)}, u32[]{:S(2)}) async-start(s32[32,1,48]{2,1,0:T(1,128)} %get-tuple-element.27), calls=%async_computation | async-start | bytes 32768 | tf_op jit(solution)/shard_map/all_to_all | solution.py:606
  10.8 1.9 %copy-done = f32[2048,400]{0,1:T(8,128)S(1)} copy-done((f32[2048,400]{0,1:T(8,128)S(1)}, f32[2048,400]{0,1:T(8,128)}, u32[]{:S(2)}) %copy-start) | copy-done | bytes 3276824
  12.7 1.4 table_rows.1.table_ref
  14.1 3.7 %all-to-all-done.asked_ref = s32[32,1,48]{2,1,0:T(1,128)S(1)} async-done(((s32[32,1,48]{2,1,0:T(1,128)}), s32[32,1,48]{2,1,0:T(1,128)S(1)}, u32[]{:S(2)}, u32[]{:S(2)}) %all-to-all-start) | async-done | bytes 6176 | tf_op jit(solution)/shard_map/all_to_all | solution.py:606
  17.9 4.5 %serve_rows.1 = f32[4800,128]{1,0:T(8,128)} custom-call(s32[32,1,48]{2,1,0:T(1,128)S(1)} %all-to-all-done.asked_ref, f32[6432,128]{1,0:T(8,128)S(1)} %table_rows.1.table_ref), custom_call_target="tpu_custom_call" | custom-call | tf_op jit(solution)/shard_map/serve_rows/pallas_call | solution.py:284
  22.4 3.0 %all-to-all-start.1 = ((f32[32,1,19200]{2,1,0:T(1,128)}), f32[32,1,19200]{2,1,0:T(1,128)S(1)}, u32[]{:S(2)}, u32[]{:S(2)}) async-start(f32[32,1,19200]{2,1,0:T(1,128)} %bitcast.19), calls=%async_computation.1 | async-start | bytes 4915200 | tf_op jit(solution)/shard_map/all_to_all | solution.py:606
  25.4 14.1 %copy.15 = f32[7424,400]{1,0:T(8,128)} copy(f32[7424,400]{0,1:T(8,128)} %param.10) | data formatting | bytes 23756800 | tf_op args[2]
  39.5 6.2 %gather_fusion = f32[128,400]{1,0:T(8,128)S(1)} fusion(f32[7424,400]{1,0:T(8,128)} %copy.15, s32[1024]{0:T(1024)S(1)} %pad_clamp_fusion), kind=kCustom, calls=%fused_computation | custom fusion | bytes 410112 | tf_op jit(solution)/shard_map/gather | solution.py:640
  45.8 36.0 %all-to-all-done.1 = f32[32,1,19200]{2,1,0:T(1,128)S(1)} async-done(((f32[32,1,19200]{2,1,0:T(1,128)}), f32[32,1,19200]{2,1,0:T(1,128)S(1)}, u32[]{:S(2)}, u32[]{:S(2)}) %all-to-all-start.1) | async-done | bytes 2457632 | tf_op jit(solution)/shard_map/all_to_all | solution.py:606
  81.8 1.3 unpack_heads.1.query_ref.refs_5_.refs_2_
  83.2 1.3 collective-permute-start.1
  84.5 2.9 %unpack_rest.1 = (f32[400,128]{1,0:T(8,128)S(1)}, f32[512,512]{1,0:T(8,128)S(1)}, bf16[512,512]{1,0:T(8,128)(2,1)S(1)}, bf16[512,512]{1,0:T(8,128)(2,1)S(1)}, bf...) custom-call(s32[768]{0:T(1024)S(1)} %reduce.1.address_ref, ...), custom_call_target="tpu_custom_call" | custom-call | flops 10000000 | bytes 9000000 | tf_op jit(solution)/shard_map/unpack_rest/pallas_call | solution.py:363
  87.4 1.4 negative_terms.2
  88.7 1.9 %collective-permute-done.1.refs_5_.refs_4_ = f32[400,128]{1,0:T(8,128)S(1)} collective-permute-done((f32[400,128]{1,0:T(8,128)S(1)}, f32[400,128]{1,0:T(8,128)S(1)}, u32[]{:S(2)}, u32[]{:S(2)}) %collective-permute-start.1) | collective-permute-done | bytes 204832 | tf_op jit(solution)/shard_map/ppermute | solution.py:614
  90.7 1.5 collective-permute-done.2.refs_6_.refs_5_
  92.1 1.4 negative_terms.3
  95.0 1.3 collective-permute-start.5
  96.3 3.3 %block_gradients.1 = (f32[4800,128]{1,0:T(8,128)S(1)}, f32[1544,128]{1,0:T(8,128)S(1)}) custom-call(s32[768]{0:T(1024)S(1)} %reduce.1.address_ref, s32[768]{0:T(1024)S(1)} %reduce.2.slot_ref, f32[400,128]{1,0:T(8,128)S(1)} %get-tuple-element.30.refs_0_.refs_2_, f32[512,512]{1,0:T(8,128)S(1)} %get-tuple-element.31.refs_1_, ...), custom_call_target="tpu_custom_call" | custom-call | flops 805306368 | bytes 10000000 | tf_op jit(solution)/shard_map/block_gradients/pallas_call | solution.py:477
  99.7 2.5 %collective-permute-done.5.refs_5_ = f32[400,128]{1,0:T(8,128)S(1)} collective-permute-done((f32[400,128]{1,0:T(8,128)S(1)}, f32[400,128]{1,0:T(8,128)S(1)}, u32[]{:S(2)}, u32[]{:S(2)}) %collective-permute-start.5) | collective-permute-done | bytes 204832 | tf_op jit(solution)/shard_map/ppermute | solution.py:614
  102.2 2.6 %finish_gradients.1 = (f32[4800,128]{1,0:T(8,128)}, f32[4800,128]{1,0:T(8,128)S(1)}, f32[1544,128]{1,0:T(8,128)S(1)}) custom-call(s32[768]{0:T(1024)S(1)} %reduce.1.address_ref, s32[768]{0:T(1024)S(1)} %reduce.2.slot_ref, f32[4800,128]{1,0:T(8,128)S(1)} %get-tuple-element.43.refs_0_, ...), custom_call_target="tpu_custom_call", output_to_operand_aliasing={{1}: (2, {}), {2}: (3, {})} | custom-call | tf_op jit(solution)/shard_map/finish_gradients/pallas_call | solution.py:514
  104.9 4.5 %all-to-all-start.2 = ((f32[32,1,19200]{2,1,0:T(1,128)}), f32[32,1,19200]{2,1,0:T(1,128)}, u32[]{:S(2)}, u32[]{:S(2)}) async-start(f32[32,1,19200]{2,1,0:T(1,128)} %bitcast.20), calls=%async_computation.2 | async-start | bytes 4915200 | tf_op jit(solution)/shard_map/all_to_all | solution.py:606
  110.7 55.1 %all-to-all-done.2 = f32[32,1,19200]{2,1,0:T(1,128)} async-done(((f32[32,1,19200]{2,1,0:T(1,128)}), f32[32,1,19200]{2,1,0:T(1,128)}, u32[]{:S(2)}, u32[]{:S(2)}) %all-to-all-start.2) | async-done | bytes 2457632 | tf_op jit(solution)/shard_map/all_to_all | solution.py:606
  165.8 9.1 %update_table.1 = (f32[400,2048]{1,0:T(8,128)}, f32[1,2048]{1,0:T(1,128)}) custom-call(s32[1,1536]{1,0:T(1,128)S(1)} %reshape.47.asked_ref, f32[4800,128]{1,0:T(8,128)} %bitcast.9.packed_hbm, f32[1,2048]{1,0:T(1,128)S(1)} %bitcast.18, f32[400,2048]{1,0:T(8,128)S(1)} %bitcast.16), custom_call_target="tpu_custom_call" | custom-call | tf_op jit(solution)/shard_map/update_table/pallas_call | solution.py:586
  (23 shorter events, 3.1 us)
Async XLA Ops:
  3.5 14.4 %all-to-all-start = ((s32[32,1,48]{2,1,0:T(1,128)}), s32[32,1,48]{2,1,0:T(1,128)S(1)}, u32[]{:S(2)}, u32[]{:S(2)}) async-start(s32[32,1,48]{2,1,0:T(1,128)} %get-tuple-element.27), calls=%async_computation | async-start | bytes 32768 | tf_op jit(solution)/shard_map/all_to_all | solution.py:606
  10.8 1.9 %copy-start = (f32[2048,400]{0,1:T(8,128)S(1)}, f32[2048,400]{0,1:T(8,128)}, u32[]{:S(2)}) copy-start(f32[2048,400]{0,1:T(8,128)} %param.8) | copy-start | bytes 9830404
  22.4 59.5 %all-to-all-start.1 = ((f32[32,1,19200]{2,1,0:T(1,128)}), f32[32,1,19200]{2,1,0:T(1,128)S(1)}, u32[]{:S(2)}, u32[]{:S(2)}) async-start(f32[32,1,19200]{2,1,0:T(1,128)} %bitcast.19), calls=%async_computation.1 | async-start | bytes 4915200 | tf_op jit(solution)/shard_map/all_to_all | solution.py:606
  25.4 14.1 %copy-start.3 = (s32[128]{0:T(128)S(1)}, s32[128]{0:T(128)}, u32[]{:S(2)}) copy-start(s32[128]{0:T(128)} %param.13) | copy-start | bytes 1540
  83.1 4.3 %collective-permute-start = (f32[400,128]{1,0:T(8,128)S(1)}, f32[400,128]{1,0:T(8,128)S(1)}, u32[]{:S(2)}, u32[]{:S(2)}) collective-permute-start(f32[400,128]{1,0:T(8,128)S(1)} %unpack_heads.1.query_ref.refs_5_.refs_2_), channel_id=1, source_target_pairs={{0,1},{1,0},{2,3},{3,2},{4,5},{5,4},{6,7},{7,6},{8,9},{9,8},{10,11... | collective-permute-start | bytes 614408 | tf_op jit(solution)/shard_map/ppermute | solution.py:610
  83.2 7.5 %collective-permute-start.1 = (f32[400,128]{1,0:T(8,128)S(1)}, f32[400,128]{1,0:T(8,128)S(1)}, u32[]{:S(2)}, u32[]{:S(2)}) collective-permute-start(f32[400,128]{1,0:T(8,128)S(1)} %unpack_heads.1.query_ref.refs_5_.refs_2_), channel_id=1, source_target_pairs={{0,2},{1,3},{2,0},{3,1},{4,6},{5,7},{6,4},{7,5},{8,10},{9,11},{10,... | collective-permute-start | bytes 614408 | tf_op jit(solution)/shard_map/ppermute | solution.py:614
  90.7 1.5 collective-permute-start.2
  93.5 1.5 collective-permute-start.4
  93.7 6.0 %collective-permute-start.3 = (f32[400,128]{1,0:T(8,128)S(1)}, f32[400,128]{1,0:T(8,128)S(1)}, u32[]{:S(2)}, u32[]{:S(2)}) collective-permute-start(f32[400,128]{1,0:T(8,128)S(1)} %get-tuple-element.46), channel_id=1, source_target_pairs={{0,1},{1,0},{2,3},{3,2},{4,5},{5,4},{6,7},{7,6},{8,9},{9,8},{10,11... | collective-permute-start | bytes 614408 | tf_op jit(solution)/shard_map/ppermute | solution.py:610
  95.0 7.2 %collective-permute-start.5 = (f32[400,128]{1,0:T(8,128)S(1)}, f32[400,128]{1,0:T(8,128)S(1)}, u32[]{:S(2)}, u32[]{:S(2)}) collective-permute-start(f32[400,128]{1,0:T(8,128)S(1)} %add.11), channel_id=1, source_target_pairs={{0,2},{1,3},{2,0},{3,1},{4,6},{5,7},{6,4},{7,5},{8,10},{9,11},{10,... | collective-permute-start | bytes 614408 | tf_op jit(solution)/shard_map/ppermute | solution.py:614
  104.9 60.9 %copy-start.1 = (f32[2048,400]{0,1:T(8,128)S(1)}, f32[2048,400]{0,1:T(8,128)}, u32[]{:S(2)}) copy-start(f32[2048,400]{0,1:T(8,128)} %param.8) | copy-start | bytes 9830404
  104.9 60.9 %copy-start.2 = (f32[2048]{0:T(1024)S(1)}, f32[2048]{0:T(1024)}, u32[]{:S(2)}) copy-start(f32[2048]{0:T(1024)} %param.9) | copy-start | bytes 24580
  104.9 60.9 %all-to-all-start.2 = ((f32[32,1,19200]{2,1,0:T(1,128)}), f32[32,1,19200]{2,1,0:T(1,128)}, u32[]{:S(2)}, u32[]{:S(2)}) async-start(f32[32,1,19200]{2,1,0:T(1,128)} %bitcast.20), calls=%async_computation.2 | async-start | bytes 4915200 | tf_op jit(solution)/shard_map/all_to_all | solution.py:606
